TPU v7x, 128 devices: a whole 4x4x4 slice. The times are simulated.
128 devices in a mesh: gx: 4 (over z), gy: 8 (over y, core), gz: 4 (over x).
Axes of the slice: x: 4, y: 4, z: 4, core: 2. Of those that a mesh axis runs over, the one named last changes fastest.
Arguments:
- atom_charge: float32 [4, 8, 4, 2048], P('gx', 'gy', 'gz'), may hold values from -6 to 6
- atom_fraction: float32 [3, 4, 8, 4, 2048], P(None, 'gx', 'gy', 'gz'), may hold values from 0 to 1
- atom_corner: int32 [3, 4, 8, 4, 2048], P(None, 'gx', 'gy', 'gz'), may hold values from 0 to 254, as said below
- block_count: int32 [4, 8, 4, 4], P('gx', 'gy', 'gz'), may hold values from 128 to 512, as said below
- permittivity: float32 [256, 512, 1024], P('gx', 'gy', 'gz'), may hold values from 0.1 to 2
- base_potential: float32 [256, 512, 1024], P('gx', 'gy', 'gz'), may hold values from -4 to 4
- ion_access: float32 [256, 512, 1024], P('gx', 'gy', 'gz'), may hold values from 0.05 to 0.5
Outputs:
- solution_field: float32 [256, 512, 1024], P('gx', 'gy', 'gz')
- atom_sensitivity: float32 [4, 8, 4, 2048], P('gx', 'gy', 'gz')
Inputs may be any that keep to these rules, and one draw needn't show every extreme that they name: `atom_corner`: coordinate k of every corner is at most the slab's cell count along k minus 2, so that all eight B-spline cells lie in the destination slab. `block_count`: every block holds 128 or more live atoms; the devices with first and second index 0 send full blocks of 512 to the slab of third index 0 from every owner along the third axis.
All inputs are finite; a program needn't handle non-finite values.
Results may differ from a plain program's by a relative error of at most 0.00016.
Values sent between devices are 32-bit elements; how exact they have to be, the bound alone decides.
A program may use at most 192 MiB of HBM per device.

v0:
```python
import jax
import jax.numpy as jnp
from jax import lax
from jax.sharding import PartitionSpec as P

ITERS = 3


def padded_2(block, sides, width):
    for axis, dim in sides:
        count = lax.axis_size(axis)
        forward = [(i, i + 1) for i in range(count - 1)]
        backward = [(target, source) for source, target in forward]
        low = lax.ppermute(
            lax.slice_in_dim(block, block.shape[dim] - width, None, axis=dim), axis, forward
        )
        high = lax.ppermute(lax.slice_in_dim(block, 0, width, axis=dim), axis, backward)
        block = jnp.concatenate([low, block, high], axis=dim)
    return block


def harmonic(former, latter):
    return 2.0 * former * latter / (former + latter)


def neighbour_views(padded):
    return [
        padded[2:, 1:-1, 1:-1],
        padded[:-2, 1:-1, 1:-1],
        padded[1:-1, 2:, 1:-1],
        padded[1:-1, :-2, 1:-1],
        padded[1:-1, 1:-1, 2:],
        padded[1:-1, 1:-1, :-2],
    ]


def ordered_total(items):
    result = items[0]
    for item in items[1:]:
        result = result + item
    return result


def spline_rows(coord, fraction, extent):
    positions = jnp.arange(extent, dtype=jnp.int32)[None, :]
    lower = jnp.where(positions == coord[:, None], (1.0 - fraction)[:, None], 0.0)
    upper = jnp.where(positions == coord[:, None] + 1, fraction[:, None], 0.0)
    return lower + upper


def plane_weights(coords, fraction, span_x, span_y, span_z):
    rows_x = spline_rows(coords[0], fraction[0], span_x)
    rows_y = spline_rows(coords[1], fraction[1], span_y)
    rows_z = spline_rows(coords[2], fraction[2], span_z)
    plane = (rows_x[:, :, None] * rows_y[:, None, :]).reshape(rows_x.shape[0], span_x * span_y)
    return (plane, rows_z)


def residual_norm(residual, precond):
    return lax.psum(jnp.sum(residual * precond), ("gx", "gy", "gz"))


def per_device(
    atom_charge, atom_fraction, atom_corner, block_count, permittivity, base_potential, ion_access
):
    groups = lax.axis_size("gz")
    capacity = atom_charge.shape[3] // groups
    span_x, span_y, span_z = permittivity.shape
    live = jnp.arange(capacity, dtype=jnp.int32)[None, :] < block_count.reshape(groups, 1)
    charge = jnp.where(live, atom_charge.reshape(groups, capacity), 0.0)
    fraction = atom_fraction.reshape(3, groups, capacity)
    corner = atom_corner.reshape(3, groups, capacity)
    record = jnp.concatenate([charge[None], fraction, corner.astype(jnp.float32)], axis=0)
    arrived = lax.all_to_all(record, "gz", split_axis=1, concat_axis=1, tiled=True)
    coords = arrived[4:7].astype(jnp.int32)
    block_coords = coords.transpose(1, 0, 2)
    block_fraction = arrived[1:4].transpose(1, 0, 2)
    block_charge = arrived[0]

    def spread(total, items):
        coord_block, fraction_block, charge_block = items
        plane, rows_z = plane_weights(coord_block, fraction_block, span_x, span_y, span_z)
        loaded = rows_z * charge_block[:, None]
        term = lax.dot_general(
            plane,
            loaded,
            (((0,), (0,)), ((), ())),
            precision=lax.Precision.HIGHEST,
            preferred_element_type=jnp.float32,
        )
        return (total + term, None)

    empty = jnp.zeros((span_x * span_y, span_z), jnp.float32)
    sources, _ = lax.scan(spread, empty, (block_coords, block_fraction, block_charge))
    sources = sources.reshape(span_x, span_y, span_z)
    padded_eps = padded_2(permittivity, (("gx", 0), ("gy", 1), ("gz", 2)), 1)
    center = padded_eps[1:-1, 1:-1, 1:-1]
    faces = [harmonic(center, other) for other in neighbour_views(padded_eps)]
    diagonal = ordered_total(faces) + ion_access * jnp.cosh(base_potential)
    solution_field = jnp.zeros_like(sources)
    residual = sources
    precond = residual / diagonal
    direction = precond
    product_now = residual_norm(residual, precond)
    for iteration in range(ITERS):
        padded = padded_2(direction, (("gx", 0), ("gy", 1), ("gz", 2)), 1)
        views = neighbour_views(padded)
        image = diagonal * direction - ordered_total(
            [face * view for face, view in zip(faces, views)]
        )
        alpha = product_now / lax.psum(jnp.sum(direction * image), ("gx", "gy", "gz"))
        solution_field = solution_field + alpha * direction
        residual = residual - alpha * image
        if iteration + 1 < ITERS:
            precond = residual / diagonal
            product_next = residual_norm(residual, precond)
            direction = precond + product_next / product_now * direction
            product_now = product_next
    field_plane = solution_field.reshape(span_x * span_y, span_z)

    def sample(carry, items):
        coord_block, fraction_block = items
        plane, rows_z = plane_weights(coord_block, fraction_block, span_x, span_y, span_z)
        along_z = lax.dot_general(
            rows_z,
            field_plane,
            (((1,), (1,)), ((), ())),
            precision=lax.Precision.HIGHEST,
            preferred_element_type=jnp.float32,
        )
        return (carry, jnp.sum(plane * along_z, axis=1))

    _, sampled = lax.scan(sample, 0.0, (block_coords, block_fraction))
    returned = lax.all_to_all(sampled, "gz", split_axis=0, concat_axis=0, tiled=True)
    atom_sensitivity = jnp.where(live, returned, 0.0).reshape(1, 1, 1, groups * capacity)
    return (solution_field, atom_sensitivity)


def solution(mesh):
    in_specs = (
        P("gx", "gy", "gz", None),
        P(None, "gx", "gy", "gz", None),
        P(None, "gx", "gy", "gz", None),
        P("gx", "gy", "gz", None),
        P("gx", "gy", "gz"),
        P("gx", "gy", "gz"),
        P("gx", "gy", "gz"),
    )
    out_specs = (P("gx", "gy", "gz"), P("gx", "gy", "gz", None))
    return jax.shard_map(
        per_device, mesh=mesh, in_specs=in_specs, out_specs=out_specs, check_vma=False
    )
```

profile of v0, /device:TPU:0, one launch (start us, length us, event | category | flops | bytes accessed | tf_op | source)
XLA Modules:
  0.0 821.4 jit_solution(12665819489419770546)
XLA Ops:
  1.5 3.9 collective-permute-start.1
  11.7 4.3 all-to-all-start
  36.3 4.7 collective-permute-start.5
  41.0 63.6 %while.22 = (s32[]{:T(128)}, f32[4096,256]{1,0:T(8,128)}, s32[4,3,512]{2,1,0:T(4,128)S(1)}, f32[4,3,512]{2,1,0:T(4,128)S(1)}, f32[4,512]{1,0:T(4,128)S(1)}, /*index=5*/s32[]{:T(128)}, s32[]{:T(128)}, s32[]{}, s32[]{}) while((s32[]{:T(128)}, f32[4096,256]{1,0:T(8,128)}, s32[4,3,512]{2,1,0:T(4,128)S(1)}, f32[4,3,512]{2,1,0:T(4,128)S(1)}, ...), condition=%wide.region_1.2_spmd.clone, body=%wide.region_0.1_spmd.clone.sunk | while | flops 6447762432 | bytes 25770136 | solution.py:94
  41.2 4.4 broadcast_multiply_fusion.5
  45.6 10.8 %convolution_add_fusion.2 = f32[4096,256]{1,0:T(8,128)} fusion(f32[512,4096]{0,1:T(8,128)} %bitcast.71, f32[4096,256]{1,0:T(8,128)} %get-tuple-element.279, pred[]{:T(512)S(6)} %compare.3, f32[512]{0:T(512)S(1)} %bitcast.100, f32[512]{0:T(512)S(1)} %bitcast.83, s32[512]{0:T(512)S(1)} %broadcast_add_fusion.17, f32[512]{0:T(512)S(1)} %broadcast_subtract_fusion.17, ...), kind=kOutput, calls=%fused_computation.31.clone.1 | convolution fusion | flops 6445334528 | bytes 16787456 | tf_op jit(solution)/shard_map/while/body/eval_jaxpr/dot_general | solution.py:84
  56.6 4.4 broadcast_multiply_fusion.5
  61.0 11.5 %convolution_add_fusion.2 = f32[4096,256]{1,0:T(8,128)} fusion(f32[512,4096]{0,1:T(8,128)} %bitcast.71, f32[4096,256]{1,0:T(8,128)} %get-tuple-element.279, pred[]{:T(512)S(6)} %compare.3, f32[512]{0:T(512)S(1)} %bitcast.100, f32[512]{0:T(512)S(1)} %bitcast.83, s32[512]{0:T(512)S(1)} %broadcast_add_fusion.17, f32[512]{0:T(512)S(1)} %broadcast_subtract_fusion.17, ...), kind=kOutput, calls=%fused_computation.31.clone.1 | convolution fusion | flops 6445334528 | bytes 16787456 | tf_op jit(solution)/shard_map/while/body/eval_jaxpr/dot_general | solution.py:84
  72.6 4.4 broadcast_multiply_fusion.5
  77.0 11.5 %convolution_add_fusion.2 = f32[4096,256]{1,0:T(8,128)} fusion(f32[512,4096]{0,1:T(8,128)} %bitcast.71, f32[4096,256]{1,0:T(8,128)} %get-tuple-element.279, pred[]{:T(512)S(6)} %compare.3, f32[512]{0:T(512)S(1)} %bitcast.100, f32[512]{0:T(512)S(1)} %bitcast.83, s32[512]{0:T(512)S(1)} %broadcast_add_fusion.17, f32[512]{0:T(512)S(1)} %broadcast_subtract_fusion.17, ...), kind=kOutput, calls=%fused_computation.31.clone.1 | convolution fusion | flops 6445334528 | bytes 16787456 | tf_op jit(solution)/shard_map/while/body/eval_jaxpr/dot_general | solution.py:84
  88.7 4.4 broadcast_multiply_fusion.5
  93.1 11.5 %convolution_add_fusion.2 = f32[4096,256]{1,0:T(8,128)} fusion(f32[512,4096]{0,1:T(8,128)} %bitcast.71, f32[4096,256]{1,0:T(8,128)} %get-tuple-element.279, pred[]{:T(512)S(6)} %compare.3, f32[512]{0:T(512)S(1)} %bitcast.100, f32[512]{0:T(512)S(1)} %bitcast.83, s32[512]{0:T(512)S(1)} %broadcast_add_fusion.17, f32[512]{0:T(512)S(1)} %broadcast_subtract_fusion.17, ...), kind=kOutput, calls=%fused_computation.31.clone.1 | convolution fusion | flops 6445334528 | bytes 16787456 | tf_op jit(solution)/shard_map/while/body/eval_jaxpr/dot_general | solution.py:84
  107.9 29.1 %bitcast_divide_fusion = (f32[64,64,256]{2,1,0:T(8,128)S(1)}, f32[64,64,256]{2,1,0:T(8,128)}, f32[64,64,256]{2,1,0:T(8,128)}, f32[64,64,256]{2,1,0:T(8,128)}, f32[64,64,256]{2,1,0:T(8,128)}, /*index=5*/f32[64,64,256]{2,1,0:T(8,128)}) fusion(f32[4096,256]{1,0:T(8,128)} %get-tuple-element.56, f32[64,64,256]{2,1,0:T(8,128)} %param.17, ...), kind=kLoop, calls=%fused_computation.215 | loop fusion | flops 41943040 | bytes 46569504 | tf_op jit(solution)/shard_map/div | solution.py:102
  138.3 5.2 collective-permute-start.7
  159.0 5.0 collective-permute-start.11
  167.6 33.6 %multiply_reduce_fusion.4 = (f32[]{:T(128)}, f32[]{:T(128)}, f32[64,64,256]{2,1,0:T(8,128)}) fusion(f32[64,64,256]{2,1,0:T(8,128)} %copy-done.1, f32[64,64,256]{2,1,0:T(8,128)} %bitcast.73, f32[64,64,256]{2,1,0:T(8,128)} %get-tuple-element.132, f32[66,1,256]{2,1,0:T(1,128)S(1)} %copy.64, f32[1,64,256]{2,1,0:T(8,128)S(1)} %collective-permute-done.6, ...), kind=kLoop, calls=%fused_computation.185 | loop fusion | flops 46137344 | bytes 38180904 | tf_op jit(solution)/shard_map/reduce_sum | solution.py:111
  201.3 73.1 %all-reduce = (f32[]{:T(128)}, f32[]{:T(128)}) all-reduce(f32[]{:T(128)} %get-tuple-element.99, f32[]{:T(128)} %get-tuple-element.98), channel_id=1, replica_groups=mesh['gx'=4,'gy'=8,'gz'=4] {'gx','gy','gz'}, use_global_device_ids=true, to_apply=%region_3.4 | all-reduce | flops 2 | bytes 16 | tf_op jit(solution)/shard_map/psum | solution.py:60
  275.7 4.5 multiply_subtract_fusion.1
  280.3 3.8 multiply_reduce_fusion.3
  284.1 63.9 %psum.44 = f32[]{:T(128)} all-reduce(f32[]{:T(128)} %get-tuple-element.124), channel_id=1, replica_groups=mesh['gx'=4,'gy'=8,'gz'=4] {'gx','gy','gz'}, use_global_device_ids=true, to_apply=%region_7.8 | all-reduce | flops 1 | bytes 8 | tf_op jit(solution)/shard_map/psum | solution.py:60
  349.4 4.3 multiply_add_fusion.2
  355.1 4.5 collective-permute-start.13
  362.9 3.4 collective-permute-start.15
  374.8 4.6 collective-permute-start.17
  383.3 32.5 %multiply_reduce_fusion.2 = (f32[]{:T(128)}, f32[64,64,256]{2,1,0:T(8,128)}) fusion(f32[64,64,256]{2,1,0:T(8,128)} %copy-done.2, f32[64,64,256]{2,1,0:T(8,128)} %get-tuple-element.132, f32[66,1,256]{2,1,0:T(1,128)S(1)} %copy.74, f32[1,64,256]{2,1,0:T(8,128)S(1)} %collective-permute-done.12, f32[1,64,256]{2,1,0:T(8,128)S(1)} %collective-permute-done.13, ...), kind=kLoop, calls=%fused_computation.181 | loop fusion | flops 44040192 | bytes 33986596 | tf_op jit(solution)/shard_map/reduce_sum | solution.py:111
  415.8 65.9 %psum.45 = f32[]{:T(128)} all-reduce(f32[]{:T(128)} %get-tuple-element.122), channel_id=1, replica_groups=mesh['gx'=4,'gy'=8,'gz'=4] {'gx','gy','gz'}, use_global_device_ids=true, to_apply=%region_9.10 | all-reduce | flops 1 | bytes 8 | tf_op jit(solution)/shard_map/psum | solution.py:111
  483.1 6.7 multiply_reduce_fusion.1
  489.7 63.1 %psum.46 = f32[]{:T(128)} all-reduce(f32[]{:T(128)} %multiply_reduce_fusion.1), channel_id=1, replica_groups=mesh['gx'=4,'gy'=8,'gz'=4] {'gx','gy','gz'}, use_global_device_ids=true, to_apply=%region_11.12 | all-reduce | flops 1 | bytes 8 | tf_op jit(solution)/shard_map/psum | solution.py:60
  554.1 9.5 %multiply_add_fusion.1 = f32[64,64,256]{2,1,0:T(8,128)S(1)} fusion(f32[64,64,256]{2,1,0:T(8,128)} %copy-done.2, f32[]{:T(128)S(6)} %div.54, f32[64,64,256]{2,1,0:T(8,128)} %get-tuple-element.128, f32[64,64,256]{2,1,0:T(8,128)} %get-tuple-element.123, f32[]{:T(128)S(6)} %div.52, f32[64,64,256]{2,1,0:T(8,128)} %get-tuple-element.126, f32[]{:T(128)S(6)} %div.49, ...), kind=kLoop, calls=%fused_computation.178 | loop fusion | flops 7340032 | bytes 25165836 | tf_op jit(solution)/shard_map/add | solution.py:117
  564.9 4.5 collective-permute-start.19
  585.9 4.5 collective-permute-start.23
  594.7 32.5 %fusion.24 = f32[]{:T(128)} fusion(f32[64,64,256]{2,1,0:T(8,128)} %copy-done.3, f32[64,64,256]{2,1,0:T(8,128)} %get-tuple-element.132, f32[66,66,1]{2,1,0:T(8,128)} %copy.92, f32[66,1,256]{2,1,0:T(1,128)} %copy-done.7, f32[66,1,256]{2,1,0:T(1,128)} %copy-done.8, f32[1,64,256]{2,1,0:T(8,128)} %copy-done.9, f32[1,64,256]{2,1,0:T(8,128)} %copy-done.10, ...), kind=kLoop, calls=%fused_computation.74 | loop fusion | flops 44040192 | bytes 29792292 | tf_op jit(solution)/shard_map/reduce_sum | solution.py:111
  627.2 66.7 %psum.47 = f32[]{:T(128)} all-reduce(f32[]{:T(128)} %fusion.24), channel_id=1, replica_groups=mesh['gx'=4,'gy'=8,'gz'=4] {'gx','gy','gz'}, use_global_device_ids=true, to_apply=%region_13.14 | all-reduce | flops 1 | bytes 8 | tf_op jit(solution)/shard_map/psum | solution.py:111
  695.1 12.0 %multiply_add_fusion = f32[64,64,256]{2,1,0:T(8,128)} fusion(f32[64,64,256]{2,1,0:T(8,128)} %copy-done.2, f32[64,64,256]{2,1,0:T(8,128)} %copy-done.1, f32[]{:T(128)S(6)} %div.55, f32[]{:T(128)S(6)} %div.52, f32[]{:T(128)S(6)} %div.49, f32[]{:T(128)S(6)} %div.54, f32[64,64,256]{2,1,0:T(8,128)} %get-tuple-element.128, f32[64,64,256]{2,1,0:T(8,128)} %get-tuple-element.123, ...), kind=kLoop, calls=%fused_computation.177 | loop fusion | flops 12582912 | bytes 29360144 | tf_op jit(solution)/shard_map/add | solution.py:112
  707.1 104.3 %while.21 = (s32[]{:T(128)}, f32[4,512]{1,0:T(4,128)S(1)}, s32[4,3,512]{2,1,0:T(4,128)}, f32[4,3,512]{2,1,0:T(4,128)S(1)}, f32[4096,256]{1,0:T(8,128)}, /*index=5*/s32[]{:T(128)}, s32[]{:T(128)}, s32[]{}, s32[]{}) while((s32[]{:T(128)}, f32[4,512]{1,0:T(4,128)S(1)}, s32[4,3,512]{2,1,0:T(4,128)}, f32[4,3,512]{2,1,0:T(4,128)S(1)}, ...), condition=%wide.region_16.17_spmd, body=%wide.region_14.16_spmd.sunk | while | flops 6449728000 | bytes 38353040 | solution.py:133
  708.0 4.4 broadcast_multiply_fusion.4
  712.4 9.0 %copy.97 = f32[512,4096]{1,0:T(8,128)} copy(f32[512,4096]{0,1:T(8,128)} %bitcast.72) | data formatting | bytes 16777216 | tf_op jit(solution)/shard_map/while/body/eval_jaxpr/mul | solution.py:55
  721.3 11.7 %multiply_reduce_fusion.7 = f32[512]{0:T(512)S(1)} fusion(f32[512,4096]{1,0:T(8,128)} %copy.97, f32[4096,256]{1,0:T(8,128)} %get-tuple-element.318, f32[512]{0:T(512)S(1)} %bitcast.79, s32[512]{0:T(512)S(1)} %broadcast_add_fusion.14, f32[512]{0:T(512)S(1)} %broadcast_subtract_fusion.14, s32[512]{0:T(512)S(1)} %bitcast.77), kind=kOutput, calls=%fused_computation.clone.1 | convolution fusion | flops 6447300096 | bytes 12593152 | tf_op jit(solution)/shard_map/while/body/eval_jaxpr/dot_general | solution.py:124
  734.1 4.4 broadcast_multiply_fusion.4
  738.4 9.0 %copy.97 = f32[512,4096]{1,0:T(8,128)} copy(f32[512,4096]{0,1:T(8,128)} %bitcast.72) | data formatting | bytes 16777216 | tf_op jit(solution)/shard_map/while/body/eval_jaxpr/mul | solution.py:55
  747.4 11.7 %multiply_reduce_fusion.7 = f32[512]{0:T(512)S(1)} fusion(f32[512,4096]{1,0:T(8,128)} %copy.97, f32[4096,256]{1,0:T(8,128)} %get-tuple-element.318, f32[512]{0:T(512)S(1)} %bitcast.79, s32[512]{0:T(512)S(1)} %broadcast_add_fusion.14, f32[512]{0:T(512)S(1)} %broadcast_subtract_fusion.14, s32[512]{0:T(512)S(1)} %bitcast.77), kind=kOutput, calls=%fused_computation.clone.1 | convolution fusion | flops 6447300096 | bytes 12593152 | tf_op jit(solution)/shard_map/while/body/eval_jaxpr/dot_general | solution.py:124
  760.1 4.4 broadcast_multiply_fusion.4
  764.5 9.0 %copy.97 = f32[512,4096]{1,0:T(8,128)} copy(f32[512,4096]{0,1:T(8,128)} %bitcast.72) | data formatting | bytes 16777216 | tf_op jit(solution)/shard_map/while/body/eval_jaxpr/mul | solution.py:55
  773.5 11.7 %multiply_reduce_fusion.7 = f32[512]{0:T(512)S(1)} fusion(f32[512,4096]{1,0:T(8,128)} %copy.97, f32[4096,256]{1,0:T(8,128)} %get-tuple-element.318, f32[512]{0:T(512)S(1)} %bitcast.79, s32[512]{0:T(512)S(1)} %broadcast_add_fusion.14, f32[512]{0:T(512)S(1)} %broadcast_subtract_fusion.14, s32[512]{0:T(512)S(1)} %bitcast.77), kind=kOutput, calls=%fused_computation.clone.1 | convolution fusion | flops 6447300096 | bytes 12593152 | tf_op jit(solution)/shard_map/while/body/eval_jaxpr/dot_general | solution.py:124
  786.2 4.4 broadcast_multiply_fusion.4
  790.6 9.0 %copy.97 = f32[512,4096]{1,0:T(8,128)} copy(f32[512,4096]{0,1:T(8,128)} %bitcast.72) | data formatting | bytes 16777216 | tf_op jit(solution)/shard_map/while/body/eval_jaxpr/mul | solution.py:55
  799.6 11.7 %multiply_reduce_fusion.7 = f32[512]{0:T(512)S(1)} fusion(f32[512,4096]{1,0:T(8,128)} %copy.97, f32[4096,256]{1,0:T(8,128)} %get-tuple-element.318, f32[512]{0:T(512)S(1)} %bitcast.79, s32[512]{0:T(512)S(1)} %broadcast_add_fusion.14, f32[512]{0:T(512)S(1)} %broadcast_subtract_fusion.14, s32[512]{0:T(512)S(1)} %bitcast.77), kind=kOutput, calls=%fused_computation.clone.1 | convolution fusion | flops 6447300096 | bytes 12593152 | tf_op jit(solution)/shard_map/while/body/eval_jaxpr/dot_general | solution.py:124
  815.4 5.2 all-to-all-done.1
  (217 shorter events, 98.7 us)
Async XLA Ops:
  1.5 14.5 %collective-permute-start.1 = (f32[1,64,256]{2,1,0:T(8,128)S(1)}, f32[1,64,256]{2,1,0:T(8,128)S(1)}, u32[]{:S(2)}, u32[]{:S(2)}) collective-permute-start(f32[1,64,256]{2,1,0:T(8,128)S(1)} %get-tuple-element.172), channel_id=1, source_target_pairs={{0,32},{32,64},{64,96},{1,33},{33,65},{65,97},{2,34},{34,66},{66,9... | collective-permute-start | bytes 196616 | tf_op jit(solution)/shard_map/ppermute | solution.py:14
  5.4 13.6 %collective-permute-start = (f32[1,64,256]{2,1,0:T(8,128)S(1)}, f32[1,64,256]{2,1,0:T(8,128)S(1)}, u32[]{:S(2)}, u32[]{:S(2)}) collective-permute-start(f32[1,64,256]{2,1,0:T(8,128)S(1)} %get-tuple-element.171), channel_id=1, source_target_pairs={{32,0},{64,32},{96,64},{33,1},{65,33},{97,65},{34,2},{66,34},{98,6... | collective-permute-start | bytes 196616 | tf_op jit(solution)/shard_map/ppermute | solution.py:17
  11.7 13.8 %all-to-all-start = ((f32[7,4,512]{2,0,1:T(8,128)}), f32[7,4,512]{2,0,1:T(8,128)S(1)}, u32[]{:S(2)}, u32[]{:S(2)}) async-start(f32[7,4,512]{2,0,1:T(8,128)} %copy.52), calls=%async_computation | async-start | bytes 131072 | tf_op jit(solution)/shard_map/all_to_all | solution.py:74
  19.0 364.3 %copy-start.6 = (f32[1,64,256]{2,1,0:T(8,128)}, f32[1,64,256]{2,1,0:T(8,128)S(1)}, u32[]{:S(2)}) copy-start(f32[1,64,256]{2,1,0:T(8,128)S(1)} %collective-permute-done) | copy-start | bytes 196612
  19.0 2.1 copy-start.5
  21.2 4.4 collective-permute-start.2
  22.5 3.9 collective-permute-start.3
  34.1 70.5 %collective-permute-start.4 = (f32[66,66,1]{1,0,2:T(8,128)S(1)}, f32[66,66,1]{1,0,2:T(8,128)S(1)}, u32[]{:S(2)}, u32[]{:S(2)}) collective-permute-start(f32[66,66,1]{1,0,2:T(8,128)S(1)} %copy.59), channel_id=1, source_target_pairs={{1,0},{2,1},{3,2},{5,4},{6,5},{7,6},{9,8},{10,9},{11,10},{13,12},{... | collective-permute-start | bytes 52280 | tf_op jit(solution)/shard_map/ppermute | solution.py:17
  36.3 69.3 %collective-permute-start.5 = (f32[66,66,1]{1,0,2:T(8,128)S(1)}, f32[66,66,1]{1,0,2:T(8,128)S(1)}, u32[]{:S(2)}, u32[]{:S(2)}) collective-permute-start(f32[66,66,1]{1,0,2:T(8,128)S(1)} %copy.61), channel_id=1, source_target_pairs={{0,1},{1,2},{2,3},{4,5},{5,6},{6,7},{8,9},{9,10},{10,11},{12,13},{... | collective-permute-start | bytes 52280 | tf_op jit(solution)/shard_map/ppermute | solution.py:14
  104.6 32.4 %copy-start.11 = (s32[4,3,512]{2,1,0:T(4,128)}, s32[4,3,512]{2,1,0:T(4,128)S(1)}, u32[]{:S(2)}) copy-start(s32[4,3,512]{2,1,0:T(4,128)S(1)} %get-tuple-element.334) | copy-start | bytes 73732
  137.0 14.9 %copy-start.1 = (f32[64,64,256]{2,1,0:T(8,128)}, f32[64,64,256]{2,1,0:T(8,128)S(1)}, u32[]{:S(2)}) copy-start(f32[64,64,256]{2,1,0:T(8,128)S(1)} %get-tuple-element.127) | copy-start | bytes 12582916
  137.0 6.8 collective-permute-start.6
  138.3 7.3 collective-permute-start.7
  145.7 4.4 collective-permute-start.8
  147.0 3.9 collective-permute-start.9
  156.8 7.2 collective-permute-start.10
  159.0 6.4 collective-permute-start.11
  275.7 4.6 copy-start
  280.3 3.8 copy-start.4
  353.7 14.1 %copy-start.2 = (f32[64,64,256]{2,1,0:T(8,128)}, f32[64,64,256]{2,1,0:T(8,128)S(1)}, u32[]{:S(2)}) copy-start(f32[64,64,256]{2,1,0:T(8,128)S(1)} %multiply_add_fusion.2) | copy-start | bytes 12582916
  353.8 6.2 collective-permute-start.12
  355.1 6.4 collective-permute-start.13
  361.6 4.8 collective-permute-start.14
  362.9 3.9 collective-permute-start.15
  372.6 6.8 collective-permute-start.16
  374.8 6.2 collective-permute-start.17
  563.6 14.7 %copy-start.3 = (f32[64,64,256]{2,1,0:T(8,128)}, f32[64,64,256]{2,1,0:T(8,128)S(1)}, u32[]{:S(2)}) copy-start(f32[64,64,256]{2,1,0:T(8,128)S(1)} %multiply_add_fusion.1) | copy-start | bytes 12582916
  563.6 6.2 collective-permute-start.18
  564.9 6.4 collective-permute-start.19
  569.8 7.0 copy-start.9
  571.4 5.4 copy-start.10
  571.5 4.4 collective-permute-start.20
  572.8 3.9 collective-permute-start.21
  575.9 0.9 copy-start.7
  576.8 0.6 copy-start.8
  583.1 7.4 collective-permute-start.22
  585.9 6.5 collective-permute-start.23
  707.1 108.2 %copy-start.12 = (s32[1,1,1,4]{3,2,1,0:T(1,128)S(1)}, s32[1,1,1,4]{3,2,1,0:T(1,128)}, u32[]{:S(2)}) copy-start(s32[1,1,1,4]{3,2,1,0:T(1,128)} %param.14) | copy-start | bytes 52
  812.0 8.6 %all-to-all-start.1 = ((f32[4,1,512]{2,1,0:T(1,128)}), f32[4,1,512]{2,1,0:T(1,128)S(1)}, u32[]{:S(2)}, u32[]{:S(2)}) async-start(f32[4,1,512]{2,1,0:T(1,128)} %all_to_all.12), calls=%async_computation.1 | async-start | bytes 16384 | tf_op jit(solution)/shard_map/all_to_all | solution.py:134
where the time goes:
time: 827 us; the launch traced here: 821 us
  blocking collectives  333 us (40%)
  other arithmetic  214 us (26%)
  matrix products  92.3 us (11%)
  local copies, waits for them, and re-layouts  86.1 us (10%)
  starting transfers between devices  72.7 us (9%)
  waiting for transfers between devices  15.1 us (2%)
    psum x3, blocking collectives, residual_norm(): return lax.psum(jnp.sum(residual * precond), ('gx', 'gy', 'gz'))  200 us
    psum x2, blocking collectives, per_device(): lax.psum(jnp.sum(direction * image), ('gx', 'gy', 'gz'))  133 us
    reduce_sum x3, other arithmetic, per_device(): jnp.sum(direction * image)  98.6 us
    ppermute x12, starting transfers between devices, padded_2(): lax.ppermute(lax.slice_in_dim(block, block.shape[dim] - width, None, axis...  49.5 us
    dot_general x4, matrix products, sample(): lax.dot_general(rows_z, field_plane, (((1,), (1,)), ((), ())), precision=...  46.9 us
    dot_general x4, matrix products, spread(): lax.dot_general(plane, loaded, (((0,), (0,)), ((), ())), precision=lax.Pr...  45.4 us
    mul x4, local copies, waits for them, and re-layouts, plane_weights(): rows_x[:, :, None] * rows_y[:, None, :]  35.9 us
    mul x8, other arithmetic, plane_weights(): rows_x[:, :, None] * rows_y[:, None, :]  35 us
  transfers between devices with their start and end apart: 26, of which 14 were waited for; matrix products, arithmetic and copies ran while one was open for 10% of the time, Pallas kernels for 0%

commit v1 on v0

v1 whole, which is shorter than its diff:
```python
import functools

import jax
import jax.numpy as jnp
from jax import lax
from jax.experimental import pallas as pl
from jax.experimental.pallas import tpu as pltpu
from jax.sharding import PartitionSpec as P

F = jnp.float32
AXES = ("gx", "gy", "gz")
MESH = pl.DeviceIdType.MESH
LANES = 128
PAD = 8
CHUNK = 16
SLOTS_PER_STEP = 16
TABLES = 2


def patterns():
    row = lax.broadcasted_iota(jnp.int32, (8, LANES), 0)
    lane = lax.broadcasted_iota(jnp.int32, (8, LANES), 1)
    return row, ((row % 2) * LANES + lane).astype(F)


def z_hat(pos, cz, fz):
    return jnp.maximum(1.0 - jnp.abs((pos - cz) - fz), 0.0)


def spread_kernel(slots, span_y, q_ref, f_ref, c_ref, out_ref, *scratch):
    tables, sem = scratch[:TABLES], scratch[TABLES]
    rows = out_ref.shape[0]
    block = 64

    def clear(i, _):
        for table in tables:
            table[pl.ds(pl.multiple_of(i * block, block), block), :] = jnp.zeros((block, LANES), F)
        return 0

    lax.fori_loop(0, rows // block, clear, 0)
    for table in tables:
        table[pl.ds(rows, 8), :] = jnp.zeros((8, LANES), F)
    row, pos = patterns()
    ya = jnp.where(row < 2, 1.0, 0.0).astype(F)
    yb = jnp.where(row < 2, -1.0, jnp.where(row < 4, 1.0, 0.0)).astype(F)
    plane = 2 * span_y

    def body(i, _):
        for first in range(0, SLOTS_PER_STEP, TABLES):
            items = []
            for which, table in enumerate(tables):
                s = i * SLOTS_PER_STEP + first + which
                r = pl.multiple_of((c_ref[s] * span_y + c_ref[slots + s]) * 2, 2)
                cz = c_ref[2 * slots + s].astype(F)
                fx, fy, fz = f_ref[s], f_ref[slots + s], f_ref[2 * slots + s]
                q = q_ref[s]
                w = (ya + yb * fy) * z_hat(pos, cz, fz)
                near = table[pl.ds(r, 8), :] + w * (q * (1.0 - fx))
                far = table[pl.ds(r + plane, 8), :] + w * (q * fx)
                items.append((table, r, near, far))
            for table, r, near, far in items:
                table[pl.ds(r, 8), :] = near
                table[pl.ds(r + plane, 8), :] = far
        return 0

    lax.fori_loop(0, slots // SLOTS_PER_STEP, body, 0)

    def combine(i, _):
        part = pl.ds(pl.multiple_of(i * block, block), block)
        total = tables[0][part, :]
        for table in tables[1:]:
            total = total + table[part, :]
        tables[0][part, :] = total
        return 0

    lax.fori_loop(0, rows // block, combine, 0)
    copy = pltpu.make_async_copy(tables[0].at[pl.ds(0, rows), :], out_ref, sem)
    copy.start()
    copy.wait()


def spread(charge, fraction, corner, span):
    slots = charge.shape[0]
    rows = span[0] * span[1] * 2
    return pl.pallas_call(
        functools.partial(spread_kernel, slots, span[1]),
        out_shape=jax.ShapeDtypeStruct((rows, LANES), F),
        in_specs=[pl.BlockSpec(memory_space=pltpu.SMEM)] * 3,
        out_specs=pl.BlockSpec(memory_space=pl.ANY),
        scratch_shapes=[pltpu.VMEM((rows + 8, LANES), F)] * TABLES + [pltpu.SemaphoreType.DMA(())],
        compiler_params=pltpu.CompilerParams(vmem_limit_bytes=56 << 20),
        name="spread",
    )(charge, fraction, corner)


def sample_kernel(
    slots, span_y, f_ref, c_ref, rows_ref, grid_ref, field_ref, out_ref, table, grid, parts, sums, sems
):
    rows = rows_ref.shape[0]
    load = pltpu.make_async_copy(rows_ref, table.at[pl.ds(8, rows), :], sems.at[1])
    load.start()
    hold = pltpu.make_async_copy(grid_ref, grid, sems.at[0])
    hold.start()
    table[pl.ds(0, 8), :] = jnp.zeros((8, LANES), F)
    table[pl.ds(rows + 8, 8), :] = jnp.zeros((8, LANES), F)
    load.wait()
    hold.wait()
    keep = pltpu.make_async_copy(grid, field_ref, sems.at[2])
    keep.start()
    row, pos = patterns()
    first_row, second_row = row % 4 < 2, row < 4
    yb = jnp.where(first_row, -1.0, 1.0).astype(F)
    ya = jnp.where(first_row, 1.0, 0.0).astype(F)
    masks = [jnp.where(second_row, 1.0, 0.0).astype(F), jnp.where(second_row, 0.0, 1.0).astype(F)]
    plane = 2 * span_y

    def body(i, _):
        for pair in range(SLOTS_PER_STEP // 2):
            total = None
            for which in (0, 1):
                s = i * SLOTS_PER_STEP + 2 * pair + which
                r = pl.multiple_of((c_ref[s] * span_y + c_ref[slots + s]) * 2, 2)
                r = r + (8 - 4 * which)
                cz = c_ref[2 * slots + s].astype(F)
                fx, fy, fz = f_ref[s], f_ref[slots + s], f_ref[2 * slots + s]
                w = (ya * masks[which] + (yb * masks[which]) * fy) * z_hat(pos, cz, fz)
                near, far = table[pl.ds(r, 8), :], table[pl.ds(r + plane, 8), :]
                term = w * (near * (1.0 - fx) + far * fx)
                total = term if total is None else total + term
            start = pl.multiple_of((i * (SLOTS_PER_STEP // 2) + pair) * 8, 8)
            parts[pl.ds(start, 8), :] = total
        return 0

    lax.fori_loop(0, slots // SLOTS_PER_STEP, body, 0)

    def fold(i, _):
        start = pl.multiple_of(i * 256, 256)
        total = parts[pl.ds(start, 64, stride=4), :]
        for j in range(1, 4):
            total = total + parts[pl.ds(start + j, 64, stride=4), :]
        sums[pl.ds(pl.multiple_of(i * 64, 64), 64), :] = total
        return 0

    lax.fori_loop(0, slots // 64, fold, 0)
    out_ref[...] = lax.dot_general(
        jnp.ones((8, LANES), F),
        sums[...],
        (((1,), (1,)), ((), ())),
        precision=lax.Precision.HIGHEST,
        preferred_element_type=F,
    )
    keep.wait()


def sample(fraction, corner, rows_field, grid_field):
    slots = fraction.shape[0] // 3
    span_x, span_y, span_z = grid_field.shape
    rows = rows_field.shape[0]
    smem, anywhere = pl.BlockSpec(memory_space=pltpu.SMEM), pl.BlockSpec(memory_space=pl.ANY)
    return pl.pallas_call(
        functools.partial(sample_kernel, slots, span_y),
        out_shape=(
            jax.ShapeDtypeStruct(grid_field.shape, F),
            jax.ShapeDtypeStruct((8, slots), F),
        ),
        in_specs=[smem, smem, anywhere, anywhere],
        out_specs=(anywhere, pl.BlockSpec(memory_space=pltpu.VMEM)),
        scratch_shapes=[
            pltpu.VMEM((rows + 16, LANES), F),
            pltpu.VMEM(grid_field.shape, F),
            pltpu.VMEM((slots * 4, LANES), F),
            pltpu.VMEM((slots, LANES), F),
            pltpu.SemaphoreType.DMA((3,)),
        ],
        compiler_params=pltpu.CompilerParams(vmem_limit_bytes=56 << 20),
        name="sample",
    )(fraction, corner, rows_field, grid_field)


def harmonic(former, latter):
    return 2.0 * former * latter / (former + latter)


def krylov_kernel(
    sizes,
    b_ref, eps_ref, pot_ref, ion_ref,
    out_ref, rows_ref,
    e, fx, fy, fz, rd, v0, v1, v2, b, pot, ion,
    y_send, y_recv, z_send, z_recv, zf, red, sem_in, send_sem, recv_sem, red_send, red_recv, sem_out,
):
    span_x, span_y, _ = eps_ref.shape
    places = [lax.axis_index(axis) for axis in AXES]
    lane = lax.broadcasted_iota(jnp.int32, (CHUNK, LANES), 1)
    edge = (lane == 0) | (lane == LANES - 1)
    chunks = range(0, span_y, CHUNK)
    body_rows = pl.ds(PAD, span_y)
    vs = (v0, v1, v2)

    loads = []
    for half in (0, 1):
        lanes = pl.ds(half * LANES, LANES)
        for n, (src, dst) in enumerate(
            (
                (eps_ref.at[:, :, lanes], e.at[pl.ds(1, span_x), half, body_rows, :]),
                (pot_ref.at[:, :, lanes], pot.at[:, half]),
                (ion_ref.at[:, :, lanes], ion.at[:, half]),
            )
        ):
            loads.append(pltpu.make_async_copy(src, dst, sem_in.at[2 * n + half]))
    loads.append(pltpu.make_async_copy(b_ref, b, sem_in.at[6]))
    for load in loads:
        load.start()

    zero = jnp.zeros((span_y, LANES), F)
    for field in (e, v0, v1, v2):
        for half in (0, 1):
            for x in (0, span_x + 1):
                field[x, half, body_rows, :] = zero
    for k in range(4):
        for side in (0, 1):
            z_recv[k, side] = zero
            for half in (0, 1):
                y_recv[k, side, half] = jnp.zeros((span_x, LANES), F)

    barrier = pltpu.get_barrier_semaphore()
    for axis, place, size in zip(AXES, places, sizes):
        for step in range(1, size):
            pl.semaphore_signal(
                barrier, inc=1, device_id={axis: lax.rem(place + step, size)}, device_id_type=MESH
            )
    pl.semaphore_wait(barrier, sum(size - 1 for size in sizes))

    def halo_copies(k, field):
        pairs = []
        for n, (axis, place, size) in enumerate(zip(AXES, places, sizes)):
            if size == 1:
                continue
            for side in (0, 1):
                slot = 2 * n + side
                if n == 0:
                    src = field.at[span_x if side == 0 else 1, :, body_rows, :]
                    dst = field.at[0 if side == 0 else span_x + 1, :, body_rows, :]
                elif n == 1:
                    src, dst = y_send.at[k, side], y_recv.at[k, side]
                else:
                    src, dst = z_send.at[k], z_recv.at[k, side]
                copy = pltpu.make_async_remote_copy(
                    src_ref=src,
                    dst_ref=dst,
                    send_sem=send_sem.at[k, slot],
                    recv_sem=recv_sem.at[k, slot],
                    device_id={axis: place + 1 if side == 0 else place - 1},
                    device_id_type=MESH,
                )
                above, below = place < size - 1, place > 0
                pairs.append((above if side == 0 else below, below if side == 0 else above, copy))
        return pairs

    def send(k, field):
        for has_target, _, copy in halo_copies(k, field):
            pl.when(has_target)(copy.start)

    def receive(k, field):
        for _, has_source, copy in halo_copies(k, field):
            pl.when(has_source)(copy.wait_recv)

    def sent(k, field):
        for has_target, _, copy in halo_copies(k, field):
            pl.when(has_target)(copy.wait_send)

    def pack_y(k, field, x):
        for half in (0, 1):
            y_send[k, 1, half, pl.ds(x, 1), :] = field[x + 1, half, pl.ds(PAD, 1), :]
            y_send[k, 0, half, pl.ds(x, 1), :] = field[x + 1, half, pl.ds(PAD + span_y - 1, 1), :]

    def unpack_y(k, field, x):
        for half in (0, 1):
            field[x + 1, half, pl.ds(PAD - 1, 1), :] = y_recv[k, 0, half, pl.ds(x, 1), :]
            field[x + 1, half, pl.ds(PAD + span_y, 1), :] = y_recv[k, 1, half, pl.ds(x, 1), :]

    def pack_z(acc, low, high, x):
        both = pltpu.roll(jnp.where(lane == 0, low, high), 2 * x, 1)
        return jnp.where((lane == 2 * x) | (lane == lax.rem(2 * x + LANES - 1, LANES)), both, acc)

    def open_z(packed, x):
        return pltpu.roll(packed, LANES - 1 - 2 * x, 1)

    empty = tuple(jnp.zeros((CHUNK, LANES), F) for _ in chunks)

    loads[0].wait()
    loads[3].wait()

    def pack_e(x, accs):
        pack_y(0, e, x)
        out = []
        for t, acc in zip(chunks, accs):
            rows = pl.ds(PAD + t, CHUNK)
            out.append(pack_z(acc, e[x + 1, 0, rows, :], e[x + 1, 1, rows, :], x))
        return tuple(out)

    accs = lax.fori_loop(0, span_x, pack_e, empty)
    for t, acc in zip(chunks, accs):
        z_send[0, pl.ds(t, CHUNK), :] = acc
    send(0, e)

    for n in (1, 4, 2, 5):
        loads[n].wait()

    def screen(x, _):
        for half in (0, 1):
            for t in chunks:
                rows = pl.ds(t, CHUNK)
                up = jnp.exp(pot[x, half, rows, :])
                rd[x, half, rows, :] = ion[x, half, rows, :] * (0.5 * (up + 1.0 / up))
        return 0

    lax.fori_loop(0, span_x, screen, 0)
    receive(0, e)

    odd = lane % 2 == 1
    for t in chunks:
        rows = pl.ds(t, CHUNK)
        own = z_send[0, rows, :]
        low = harmonic(z_recv[0, 0, rows, :], pltpu.roll(own, LANES - 1, 1))
        high = harmonic(z_recv[0, 1, rows, :], pltpu.roll(own, 1, 1))
        zf[0, rows, :] = jnp.where(odd, low, 0.0)
        zf[1, rows, :] = jnp.where(odd, 0.0, high)
        zf[2, rows, :] = pltpu.roll(zf[0, rows, :], 2, 1) + zf[1, rows, :]

    for half in (0, 1):
        for t in chunks:
            rows = pl.ds(PAD + t, CHUNK)
            fx[0, half, pl.ds(t, CHUNK), :] = harmonic(e[0, half, rows, :], e[1, half, rows, :])

    loads[6].wait()

    def faces(x, carry):
        accs, total = carry
        unpack_y(0, e, x)
        for half in (0, 1):
            fy[x, half, pl.ds(PAD - 1, 1), :] = harmonic(
                e[x + 1, half, pl.ds(PAD - 1, 1), :], e[x + 1, half, pl.ds(PAD, 1), :]
            )
        out = []
        for t, acc in zip(chunks, accs):
            rows, wide = pl.ds(t, CHUNK), pl.ds(PAD + t, CHUNK)
            center = [e[x + 1, half, wide, :] for half in (0, 1)]
            turned = [pltpu.roll(c, LANES - 1, 1) for c in center]
            z_next = [jnp.where(lane == LANES - 1, turned[1], turned[0]), turned[1]]
            z_face = [harmonic(c, n) for c, n in zip(center, z_next)]
            z_face[1] = jnp.where(lane == LANES - 1, 0.0, z_face[1])
            back = [pltpu.roll(f, 1, 1) for f in z_face]
            outer = open_z(zf[2, rows, :], x)
            z_both = [
                z_face[0] + jnp.where(lane == 0, outer, back[0]),
                z_face[1] + jnp.where(lane == 0, back[0], back[1])
                + jnp.where(lane == LANES - 1, outer, 0.0),
            ]
            fields = []
            for half in (0, 1):
                c = center[half]
                x_face = harmonic(c, e[x + 2, half, wide, :])
                fx[x + 1, half, rows, :] = x_face
                y_face = harmonic(c, e[x + 1, half, pl.ds(PAD + t + 1, CHUNK), :])
                fy[x, half, wide, :] = y_face
                fz[x, half, rows, :] = z_face[half]
                diagonal = (
                    x_face + fx[x, half, rows, :]
                    + y_face + fy[x, half, pl.ds(PAD + t - 1, CHUNK), :]
                    + z_both[half] + rd[x, half, rows, :]
                )
                inverse = 1.0 / diagonal
                rd[x, half, rows, :] = inverse
                source = b[pl.ds(x * (2 * span_y) + 2 * t + half, CHUNK, stride=2), :]
                value = source * inverse
                v0[x + 1, half, wide, :] = value
                total = total + source * value
                fields.append(value)
            out.append(pack_z(acc, fields[0], fields[1], x))
        pack_y(1, v0, x)
        return tuple(out), total

    nothing = jnp.zeros((CHUNK, LANES), F)
    accs, total = lax.fori_loop(0, span_x, faces, (empty, nothing))
    moments = [total]

    for k in range(3):
        v = vs[k]
        last = k == 2
        for t, acc in zip(chunks, accs):
            z_send[k + 1, pl.ds(t, CHUNK), :] = acc
        send(k + 1, v)
        receive(k + 1, v)
        for t in chunks:
            rows = pl.ds(t, CHUNK)
            zf[2, rows, :] = (
                pltpu.roll(zf[0, rows, :] * z_recv[k + 1, 0, rows, :], 2, 1)
                + zf[1, rows, :] * z_recv[k + 1, 1, rows, :]
            )

        def apply(x, carry, v=v, k=k, last=last):
            accs, first, second = carry
            unpack_y(k + 1, v, x)
            out = []
            for t, acc in zip(chunks, accs):
                rows, wide = pl.ds(t, CHUNK), pl.ds(PAD + t, CHUNK)
                up, down = pl.ds(PAD + t + 1, CHUNK), pl.ds(PAD + t - 1, CHUNK)
                center = [v[x + 1, half, wide, :] for half in (0, 1)]
                turned = [pltpu.roll(c, LANES - 1, 1) for c in center]
                z_next = [jnp.where(lane == LANES - 1, turned[1], turned[0]), turned[1]]
                z_face = [fz[x, half, rows, :] for half in (0, 1)]
                back = [pltpu.roll(f * c, 1, 1) for f, c in zip(z_face, center)]
                outer = open_z(zf[2, rows, :], x)
                z_both = [
                    z_face[0] * z_next[0] + jnp.where(lane == 0, outer, back[0]),
                    z_face[1] * z_next[1] + jnp.where(lane == 0, back[0], back[1])
                    + jnp.where(lane == LANES - 1, outer, 0.0),
                ]
                fields = []
                for half in (0, 1):
                    image = (
                        fx[x + 1, half, rows, :] * v[x + 2, half, wide, :]
                        + fx[x, half, rows, :] * v[x, half, wide, :]
                        + fy[x, half, wide, :] * v[x + 1, half, up, :]
                        + fy[x, half, down, :] * v[x + 1, half, down, :]
                        + z_both[half]
                    )
                    first = first + center[half] * image
                    if not last:
                        value = image * rd[x, half, rows, :]
                        vs[k + 1][x + 1, half, wide, :] = value
                        second = second + image * value
                        fields.append(value)
                out.append(acc if last else pack_z(acc, fields[0], fields[1], x))
            if not last:
                pack_y(k + 2, vs[k + 1], x)
            return tuple(out), first, second

        accs, first, second = lax.fori_loop(0, span_x, apply, (empty, nothing, nothing))
        moments.append(first)
        if not last:
            moments.append(second)

    row = lax.broadcasted_iota(jnp.int32, (8, LANES), 0)
    mine = jnp.zeros((8, LANES), F)
    for n, moment in enumerate(moments):
        folded = jnp.sum(moment, axis=0, keepdims=True)
        mine = mine + jnp.where(row == n, folded, 0.0)
    for n, (axis, place, size) in enumerate(zip(AXES, places, sizes)):
        red[n, place] = mine
        copies = []
        for step in range(1, size):
            target = lax.rem(place + step, size)
            copy = pltpu.make_async_remote_copy(
                src_ref=red.at[n, place],
                dst_ref=red.at[n, place],
                send_sem=red_send.at[n, step],
                recv_sem=red_recv.at[n, step],
                device_id={axis: target},
                device_id_type=MESH,
            )
            copy.start()
            copies.append(copy)
        for step in range(1, size):
            source = lax.rem(place + size - step, size)
            pltpu.make_async_remote_copy(
                src_ref=red.at[n, place],
                dst_ref=red.at[n, source],
                send_sem=red_send.at[n, step],
                recv_sem=red_recv.at[n, step],
                device_id={axis: source},
                device_id_type=MESH,
            ).wait_recv()
        for copy in copies:
            copy.wait_send()
        mine = red[n, 0]
        for other in range(1, size):
            mine = mine + red[n, other]
    totals = jnp.sum(mine, axis=1, keepdims=True)
    m = [totals[n:n + 1] for n in range(6)]
    m = [value / m[0] for value in m]

    h = [m[n] - m[n + 1] for n in range(5)]
    l1, l2 = h[1] / h[0], h[2] / h[0]
    d1 = h[2] - l1 * h[1]
    o1 = h[3] - l1 * h[2]
    l3 = o1 / d1
    d2 = h[4] - l2 * h[2] - l3 * o1
    r1 = m[1] - l1 * m[0]
    r2 = m[2] - l2 * m[0] - l3 * r1
    c2 = r2 / d2
    c1 = r1 / d1 - l3 * c2
    c0 = m[0] / h[0] - l1 * c1 - l2 * c2

    weights = [jnp.broadcast_to(c, (CHUNK, LANES)) for c in (c0, c1, c2)]

    def finish(x, _):
        for half in (0, 1):
            for t in chunks:
                wide = pl.ds(PAD + t, CHUNK)
                value = weights[0] * v0[x + 1, half, wide, :]
                value = value + weights[1] * v1[x + 1, half, wide, :]
                value = value + weights[2] * v2[x + 1, half, wide, :]
                pot[x, half, pl.ds(t, CHUNK), :] = value
                b[pl.ds(x * (2 * span_y) + 2 * t + half, CHUNK, stride=2), :] = value
        return 0

    lax.fori_loop(0, span_x, finish, 0)
    stores = [
        pltpu.make_async_copy(
            pot.at[:, half], out_ref.at[:, :, pl.ds(half * LANES, LANES)], sem_out.at[half]
        )
        for half in (0, 1)
    ]
    stores.append(pltpu.make_async_copy(b, rows_ref, sem_out.at[2]))
    for store in stores:
        store.start()
    for k, field in enumerate((e, v0, v1, v2)):
        sent(k, field)
    for store in stores:
        store.wait()


def krylov(sizes, b, eps, pot, ion):
    span_x, span_y, span_z = eps.shape
    tall = span_y + 2 * PAD
    padded = pltpu.VMEM((span_x + 2, 2, tall, LANES), F)
    plain = pltpu.VMEM((span_x, 2, span_y, LANES), F)
    dma = pltpu.SemaphoreType.DMA
    anywhere = pl.BlockSpec(memory_space=pl.ANY)
    most = max(sizes)
    return pl.pallas_call(
        functools.partial(krylov_kernel, sizes),
        out_shape=(
            jax.ShapeDtypeStruct(eps.shape, F),
            jax.ShapeDtypeStruct(b.shape, F),
        ),
        in_specs=[anywhere] * 4,
        out_specs=(anywhere, anywhere),
        scratch_shapes=[
            padded,
            pltpu.VMEM((span_x + 1, 2, span_y, LANES), F),
            pltpu.VMEM((span_x, 2, tall, LANES), F),
            plain,
            plain,
            padded, padded, padded,
            pltpu.VMEM(b.shape, F),
            plain,
            plain,
            pltpu.VMEM((4, 2, 2, span_x, LANES), F),
            pltpu.VMEM((4, 2, 2, span_x, LANES), F),
            pltpu.VMEM((4, span_y, LANES), F),
            pltpu.VMEM((4, 2, span_y, LANES), F),
            pltpu.VMEM((3, span_y, LANES), F),
            pltpu.VMEM((3, most, 8, LANES), F),
            dma((7,)),
            dma((4, 6)),
            dma((4, 6)),
            dma((3, most)),
            dma((3, most)),
            dma((3,)),
        ],
        compiler_params=pltpu.CompilerParams(
            vmem_limit_bytes=60 << 20, collective_id=0, has_side_effects=True
        ),
        name="krylov",
    )(b, eps, pot, ion)


def per_device(
    atom_charge, atom_fraction, atom_corner, block_count, permittivity, base_potential, ion_access
):
    sizes = tuple(lax.axis_size(axis) for axis in AXES)
    groups = sizes[2]
    capacity = atom_charge.shape[3] // groups
    live = jnp.arange(capacity, dtype=jnp.int32)[None, :] < block_count.reshape(groups, 1)
    charge = jnp.where(live, atom_charge.reshape(groups, capacity), 0.0)
    fraction = atom_fraction.reshape(3, groups, capacity)
    corner = atom_corner.reshape(3, groups, capacity)
    record = jnp.concatenate([charge[None], fraction, corner.astype(F)], axis=0)
    arrived = lax.all_to_all(record, "gz", split_axis=1, concat_axis=1, tiled=True)
    there_charge = arrived[0].reshape(-1)
    there_fraction = arrived[1:4].reshape(-1)
    there_corner = arrived[4:7].astype(jnp.int32).reshape(-1)
    sources = spread(there_charge, there_fraction, there_corner, permittivity.shape)
    grid_field, rows_field = krylov(sizes, sources, permittivity, base_potential, ion_access)
    solution_field, sampled = sample(there_fraction, there_corner, rows_field, grid_field)
    returned = lax.all_to_all(
        sampled[0].reshape(groups, capacity), "gz", split_axis=0, concat_axis=0, tiled=True
    )
    atom_sensitivity = jnp.where(live, returned, 0.0).reshape(1, 1, 1, groups * capacity)
    return (solution_field, atom_sensitivity)


def solution(mesh):
    in_specs = (
        P("gx", "gy", "gz", None),
        P(None, "gx", "gy", "gz", None),
        P(None, "gx", "gy", "gz", None),
        P("gx", "gy", "gz", None),
        P("gx", "gy", "gz"),
        P("gx", "gy", "gz"),
        P("gx", "gy", "gz"),
    )
    out_specs = (P("gx", "gy", "gz"), P("gx", "gy", "gz", None))
    return jax.shard_map(
        per_device, mesh=mesh, in_specs=in_specs, out_specs=out_specs, check_vma=False
    )
```

time: 827 us -> 151 us (0.18)
  blocking collectives: 333 us -> 9.8 us
  other arithmetic: 214 us -> 4.43 us
  Pallas kernels: 0 us -> 123 us
  matrix products: 92.3 us -> 0 us
  local copies, waits for them, and re-layouts: 86.1 us -> 3.91 us
  starting transfers between devices: 72.7 us -> 3.59 us
  waiting for transfers between devices: 15.1 us -> 5.23 us
    psum x5 -> x0, blocking collectives: 333 us -> none  [the longest x3 200 us: residual_norm(): return lax.psum(jnp.sum(residual * precond), ('gx', 'gy', 'gz'))]
    pallas_call x0 -> x3, Pallas kernels: none -> 123 us  [the longest x1 90.3 us: krylov(): pl.pallas_call(functools.partial(krylov_kernel, sizes), out_shape=(jax.Sh...]
    reduce_sum x5 -> x0, other arithmetic: 109 us -> none  [the longest x3 98.6 us: per_device(): jnp.sum(direction * image)]
    dot_general x8 -> x0, matrix products: 92.3 us -> none  [the longest x4 46.9 us: sample(): lax.dot_general(rows_z, field_plane, (((1,), (1,)), ((), ())), precision=...]
    ppermute x24 -> x0, starting transfers between devices: 65.1 us -> none  [the longest x12 49.5 us: padded_2(): lax.ppermute(lax.slice_in_dim(block, block.shape[dim] - width, None, axis...]
    mul x4 -> x0, local copies, waits for them, and re-layouts: 35.9 us -> none  [plane_weights(): rows_x[:, :, None] * rows_y[:, None, :]]
    mul x8 -> x0, other arithmetic: 35 us -> none  [plane_weights(): rows_x[:, :, None] * rows_y[:, None, :]]
    div x1 -> x0, other arithmetic: 29.1 us -> none  [per_device(): precond = residual / diagonal]
  transfers between devices with their start and end apart: 26 -> 1, of which waited for: 14 -> 1; matrix products, arithmetic and copies ran while one was open for 10% -> 0% of each run, Pallas kernels for 0% -> 0%
where the time goes in v1:
time: 151 us; the launch traced here: 150 us
  Pallas kernels  123 us (81%)
  blocking collectives  9.8 us (6%)
  waiting for transfers between devices  5.23 us (3%)
  other arithmetic  4.43 us (3%)
  local copies, waits for them, and re-layouts  3.91 us (3%)
  starting transfers between devices  3.59 us (2%)
    pallas_call x1, Pallas kernels, krylov(): pl.pallas_call(functools.partial(krylov_kernel, sizes), out_shape=(jax.Sh...  90.3 us
    pallas_call x1, Pallas kernels, sample(): pl.pallas_call(functools.partial(sample_kernel, slots, span_y), out_shape...  16.4 us
    pallas_call x1, Pallas kernels, spread(): pl.pallas_call(functools.partial(spread_kernel, slots, span[1]), out_shap...  16.1 us
    all_to_all x1, blocking collectives, per_device(): lax.all_to_all(record, 'gz', split_axis=1, concat_axis=1, tiled=True)  9.8 us
    all_to_all x1, waiting for transfers between devices, per_device(): lax.all_to_all(sampled[0].reshape(groups, capacity), 'gz', split_axis=0,...  5.23 us
    all_to_all x1, starting transfers between devices, per_device(): lax.all_to_all(sampled[0].reshape(groups, capacity), 'gz', split_axis=0,...  3.59 us
  transfers between devices with their start and end apart: 1, of which 1 were waited for; matrix products, arithmetic and copies ran while one was open for 0% of the time, Pallas kernels for 0%

profile of v1, /device:TPU:0, one launch (start us, length us, event | category | flops | bytes accessed | tf_op | source)
XLA Modules:
  0.0 150.5 jit_solution(13515980297427072047)
XLA Ops:
  0.6 0.5 broadcast.41
  1.1 1.4 reduce.6
  2.5 0.8 convert_reduce_fusion
  3.4 0.8 reduce.1
  4.2 0.7 fusion.1
  5.0 9.8 %all_to_all.17 = f32[7,4,512]{2,0,1:T(8,128)S(1)} all-to-all(f32[7,4,512]{2,0,1:T(8,128)S(1)} %copy.14), channel_id=1, replica_groups=mesh['gx'=4,'gy'=8,'gz'=4] {'gz'}, dimensions={1} | all-to-all | bytes 114688 | tf_op jit(solution)/shard_map/all_to_all | solution.py:581
  14.8 0.6 copy.19
  15.5 0.6 copy.20
  16.1 0.6 slice.18
  16.7 16.1 %spread.1.b_ref = f32[8192,128]{1,0:T(8,128)} custom-call(f32[2048]{0:T(1024)} %bitcast.14, f32[6144]{0:T(1024)} %bitcast.10, s32[6144]{0:T(1024)} %bitcast.12), custom_call_target="tpu_custom_call" | custom-call | tf_op jit(solution)/shard_map/spread/pallas_call | solution.py:85
  32.8 90.3 %krylov.1 = (f32[64,64,256]{2,1,0:T(8,128)}, f32[8192,128]{1,0:T(8,128)}) custom-call(f32[8192,128]{1,0:T(8,128)} %spread.1.b_ref, f32[64,64,256]{2,1,0:T(8,128)} %eps_ref.1, f32[64,64,256]{2,1,0:T(8,128)} %pot_ref.1, f32[64,64,256]{2,1,0:T(8,128)} %ion_ref.1), custom_call_target="tpu_custom_call" | custom-call | tf_op jit(solution)/shard_map/krylov/pallas_call | solution.py:532
  123.1 0.0 copy-start
  123.1 16.4 %sample.1 = (f32[64,64,256]{2,1,0:T(8,128)}, f32[8,2048]{1,0:T(8,128)}) custom-call(f32[6144]{0:T(1024)} %bitcast.11, s32[6144]{0:T(1024)} %bitcast.13, f32[8192,128]{1,0:T(8,128)} %get-tuple-element.6.rows_ref, f32[64,64,256]{2,1,0:T(8,128)} %get-tuple-element.7.grid_ref), custom_call_target="tpu_custom_call" | custom-call | tf_op jit(solution)/shard_map/sample/pallas_call | solution.py:160
  139.5 1.4 slice.15
  140.9 3.6 %all-to-all-start.1 = ((f32[4,1,512]{2,1,0:T(1,128)}), f32[4,1,512]{2,1,0:T(1,128)S(1)}, u32[]{:S(2)}, u32[]{:S(2)}) async-start(f32[4,1,512]{2,1,0:T(1,128)} %bitcast.2), calls=%async_computation.1 | async-start | bytes 16384 | tf_op jit(solution)/shard_map/all_to_all | solution.py:588
  144.5 0.0 copy-done
  144.5 0.1 iota_compare_fusion
  144.6 5.2 %all-to-all-done.1 = f32[4,1,512]{2,1,0:T(1,128)S(1)} async-done(((f32[4,1,512]{2,1,0:T(1,128)}), f32[4,1,512]{2,1,0:T(1,128)S(1)}, u32[]{:S(2)}, u32[]{:S(2)}) %all-to-all-start.1) | async-done | bytes 8224 | tf_op jit(solution)/shard_map/all_to_all | solution.py:588
  149.9 0.6 broadcast_select_fusion
  (8 shorter events, 0.2 us)
Async XLA Ops:
  123.1 21.5 %copy-start = (s32[1,1,1,4]{3,2,1,0:T(1,128)S(1)}, s32[1,1,1,4]{3,2,1,0:T(1,128)}, u32[]{:S(2)}) copy-start(s32[1,1,1,4]{3,2,1,0:T(1,128)} %param.10) | copy-start | bytes 52
  140.9 8.9 %all-to-all-start.1 = ((f32[4,1,512]{2,1,0:T(1,128)}), f32[4,1,512]{2,1,0:T(1,128)S(1)}, u32[]{:S(2)}, u32[]{:S(2)}) async-start(f32[4,1,512]{2,1,0:T(1,128)} %bitcast.2), calls=%async_computation.1 | async-start | bytes 16384 | tf_op jit(solution)/shard_map/all_to_all | solution.py:588

commit v2 on v1

--- a/solution.py
+++ b/solution.py
@@ -15,6 +15,9 @@
 CHUNK = 16
 SLOTS_PER_STEP = 16
 TABLES = 2
+START = 8
+UNROLL_FACES = 4
+UNROLL_APPLY = 8
 
 
 def patterns():
@@ -177,8 +180,13 @@
     )(fraction, corner, rows_field, grid_field)
 
 
+def inverse_of(value):
+    guess = pl.reciprocal(value, approx=True)
+    return guess * (2.0 - value * guess)
+
+
 def harmonic(former, latter):
-    return 2.0 * former * latter / (former + latter)
+    return (2.0 * former * latter) * inverse_of(former + latter)
 
 
 def krylov_kernel(
@@ -186,30 +194,34 @@
     b_ref, eps_ref, pot_ref, ion_ref,
     out_ref, rows_ref,
     e, fx, fy, fz, rd, v0, v1, v2, b, pot, ion,
-    y_send, y_recv, z_send, z_recv, zf, red, sem_in, send_sem, recv_sem, red_send, red_recv, sem_out,
+    y_send, y_recv, z_send, z_recv, z_in, red,
+    sem_in, send_sem, recv_sem, red_send, red_recv, sem_out,
 ):
     span_x, span_y, _ = eps_ref.shape
     places = [lax.axis_index(axis) for axis in AXES]
     lane = lax.broadcasted_iota(jnp.int32, (CHUNK, LANES), 1)
-    edge = (lane == 0) | (lane == LANES - 1)
+    at_first, at_last, odd = lane == 0, lane == LANES - 1, lane % 2 == 1
     chunks = range(0, span_y, CHUNK)
     body_rows = pl.ds(PAD, span_y)
     vs = (v0, v1, v2)
+    part = span_x // 2
+    fzm = ion
+
+    def plane_of(i):
+        return lax.rem(i + START, span_x)
 
     loads = []
-    for half in (0, 1):
-        lanes = pl.ds(half * LANES, LANES)
-        for n, (src, dst) in enumerate(
-            (
-                (eps_ref.at[:, :, lanes], e.at[pl.ds(1, span_x), half, body_rows, :]),
-                (pot_ref.at[:, :, lanes], pot.at[:, half]),
-                (ion_ref.at[:, :, lanes], ion.at[:, half]),
+    for n, (src, dst) in enumerate(((eps_ref, e), (pot_ref, pot), (ion_ref, ion))):
+        for half in (0, 1):
+            place = dst.at[pl.ds(1, span_x), half, body_rows, :] if n == 0 else dst.at[:, half]
+            loads.append(
+                pltpu.make_async_copy(
+                    src.at[:, :, pl.ds(half * LANES, LANES)], place, sem_in.at[2 * n + half]
+                )
             )
-        ):
-            loads.append(pltpu.make_async_copy(src, dst, sem_in.at[2 * n + half]))
     loads.append(pltpu.make_async_copy(b_ref, b, sem_in.at[6]))
-    for load in loads:
-        load.start()
+    loads[0].start()
+    loads[1].start()
 
     zero = jnp.zeros((span_y, LANES), F)
     for field in (e, v0, v1, v2):
@@ -218,9 +230,9 @@
                 field[x, half, body_rows, :] = zero
     for k in range(4):
         for side in (0, 1):
-            z_recv[k, side] = zero
-            for half in (0, 1):
-                y_recv[k, side, half] = jnp.zeros((span_x, LANES), F)
+            for which in (0, 1):
+                z_recv[k, side, which] = zero
+                y_recv[k, side, which] = jnp.zeros((span_x, LANES), F)
 
     barrier = pltpu.get_barrier_semaphore()
     for axis, place, size in zip(AXES, places, sizes):
@@ -230,216 +242,254 @@
             )
     pl.semaphore_wait(barrier, sum(size - 1 for size in sizes))
 
-    def halo_copies(k, field):
+    def halo_copies(k, field, x_faces, parts):
         pairs = []
         for n, (axis, place, size) in enumerate(zip(AXES, places, sizes)):
             if size == 1:
                 continue
-            for side in (0, 1):
-                slot = 2 * n + side
-                if n == 0:
+            for side in ((1,) if k == 3 else (0, 1)):
+                ends = []
+                if n == 0 and x_faces:
                     src = field.at[span_x if side == 0 else 1, :, body_rows, :]
-                    dst = field.at[0 if side == 0 else span_x + 1, :, body_rows, :]
-                elif n == 1:
-                    src, dst = y_send.at[k, side], y_recv.at[k, side]
-                else:
-                    src, dst = z_send.at[k], z_recv.at[k, side]
-                copy = pltpu.make_async_remote_copy(
-                    src_ref=src,
-                    dst_ref=dst,
-                    send_sem=send_sem.at[k, slot],
-                    recv_sem=recv_sem.at[k, slot],
-                    device_id={axis: place + 1 if side == 0 else place - 1},
-                    device_id_type=MESH,
+                    ends.append((0, src, field.at[0 if side == 0 else span_x + 1, :, body_rows, :]))
+                if n == 1:
+                    for which in parts:
+                        rows = pl.ds(which * part, part)
+                        src = y_send.at[k, side, :, rows, :]
+                        ends.append((1 + which, src, y_recv.at[k, side, :, rows, :]))
+                if n == 2:
+                    for which in parts:
+                        ends.append((3 + which, z_send.at[k, which], z_recv.at[k, side, which]))
+                for kind, src, dst in ends:
+                    copy = pltpu.make_async_remote_copy(
+                        src_ref=src,
+                        dst_ref=dst,
+                        send_sem=send_sem.at[k, 2 * kind + side],
+                        recv_sem=recv_sem.at[k, 2 * kind + side],
+                        device_id={axis: place + 1 if side == 0 else place - 1},
+                        device_id_type=MESH,
+                    )
+                    above, below = place < size - 1, place > 0
+                    pairs.append((above if side == 0 else below, below if side == 0 else above, copy))
+        return pairs
+
+    def send(*exchange):
+        for has_target, _, copy in halo_copies(*exchange):
+            pl.when(has_target)(copy.start)
+
+    def receive(*exchange):
+        for _, has_source, copy in halo_copies(*exchange):
+            pl.when(has_source)(copy.wait_recv)
+
+    def sent(*exchange):
+        for has_target, _, copy in halo_copies(*exchange):
+            pl.when(has_target)(copy.wait_send)
+
+    def pack(k, field, which):
+        def rows_of(i, _):
+            x = plane_of(i)
+            for half in (0, 1):
+                y_send[k, 1, half, pl.ds(i, 1), :] = field[x + 1, half, pl.ds(PAD, 1), :]
+                if k < 3:
+                    y_send[k, 0, half, pl.ds(i, 1), :] = field[
+                        x + 1, half, pl.ds(PAD + span_y - 1, 1), :
+                    ]
+            return 0
+
+        def columns_of(i, accs):
+            x = plane_of(i)
+            out = []
+            for t, acc in zip(chunks, accs):
+                rows = pl.ds(PAD + t, CHUNK)
+                ends = jnp.where(
+                    at_first,
+                    field[x + 1, 0, rows, :],
+                    jnp.where(at_last, field[x + 1, 1, rows, :], 0.0),
                 )
-                above, below = place < size - 1, place > 0
-                pairs.append((above if side == 0 else below, below if side == 0 else above, copy))
-        return pairs
-
-    def send(k, field):
-        for has_target, _, copy in halo_copies(k, field):
-            pl.when(has_target)(copy.start)
-
-    def receive(k, field):
-        for _, has_source, copy in halo_copies(k, field):
-            pl.when(has_source)(copy.wait_recv)
-
-    def sent(k, field):
-        for has_target, _, copy in halo_copies(k, field):
-            pl.when(has_target)(copy.wait_send)
-
-    def pack_y(k, field, x):
-        for half in (0, 1):
-            y_send[k, 1, half, pl.ds(x, 1), :] = field[x + 1, half, pl.ds(PAD, 1), :]
-            y_send[k, 0, half, pl.ds(x, 1), :] = field[x + 1, half, pl.ds(PAD + span_y - 1, 1), :]
-
-    def unpack_y(k, field, x):
-        for half in (0, 1):
-            field[x + 1, half, pl.ds(PAD - 1, 1), :] = y_recv[k, 0, half, pl.ds(x, 1), :]
-            field[x + 1, half, pl.ds(PAD + span_y, 1), :] = y_recv[k, 1, half, pl.ds(x, 1), :]
-
-    def pack_z(acc, low, high, x):
-        both = pltpu.roll(jnp.where(lane == 0, low, high), 2 * x, 1)
-        return jnp.where((lane == 2 * x) | (lane == lax.rem(2 * x + LANES - 1, LANES)), both, acc)
-
-    def open_z(packed, x):
-        return pltpu.roll(packed, LANES - 1 - 2 * x, 1)
-
-    empty = tuple(jnp.zeros((CHUNK, LANES), F) for _ in chunks)
+                out.append(acc + pltpu.roll(ends, 2 * x, 1))
+            return tuple(out)
+
+        first = which * part
+        lax.fori_loop(first, first + part, rows_of, 0, unroll=8)
+        empty = tuple(jnp.zeros((CHUNK, LANES), F) for _ in chunks)
+        accs = lax.fori_loop(first, first + part, columns_of, empty, unroll=8)
+        for t, acc in zip(chunks, accs):
+            z_send[k, which, pl.ds(t, CHUNK), :] = acc
+
+    def unpack(k, field, which):
+        def rows_of(i, _):
+            x = plane_of(i)
+            for half in (0, 1):
+                if k < 3:
+                    field[x + 1, half, pl.ds(PAD - 1, 1), :] = y_recv[k, 0, half, pl.ds(i, 1), :]
+                field[x + 1, half, pl.ds(PAD + span_y, 1), :] = y_recv[k, 1, half, pl.ds(i, 1), :]
+            return 0
+
+        first = which * part
+        lax.fori_loop(first, first + part, rows_of, 0, unroll=8)
+        for t in chunks:
+            rows = pl.ds(t, CHUNK)
+            low = pltpu.roll(z_recv[k, 0, which, rows, :], 2, 1)
+            z_in[which, rows, :] = jnp.where(odd, low, z_recv[k, 1, which, rows, :])
+
+    def z_neighbours(center, outer):
+        after = [pltpu.roll(c, LANES - 1, 1) for c in center]
+        before = [pltpu.roll(c, 1, 1) for c in center]
+        after = [jnp.where(at_last, after[1], after[0]), jnp.where(at_last, outer, after[1])]
+        before = [jnp.where(at_first, outer, before[0]), jnp.where(at_first, before[0], before[1])]
+        return after, before
+
+    def outer_z(which, t, x):
+        return pltpu.roll(z_in[which, pl.ds(t, CHUNK), :], LANES - 1 - 2 * x, 1)
+
+    def both_parts(body, carry, before, after, unroll):
+        for which in (0, 1):
+            before(which)
+            carry = lax.fori_loop(
+                which * part,
+                (which + 1) * part,
+                functools.partial(body, which),
+                carry,
+                unroll=unroll,
+            )
+            after(which)
+        return carry
 
     loads[0].wait()
-    loads[3].wait()
-
-    def pack_e(x, accs):
-        pack_y(0, e, x)
-        out = []
-        for t, acc in zip(chunks, accs):
-            rows = pl.ds(PAD + t, CHUNK)
-            out.append(pack_z(acc, e[x + 1, 0, rows, :], e[x + 1, 1, rows, :], x))
-        return tuple(out)
-
-    accs = lax.fori_loop(0, span_x, pack_e, empty)
-    for t, acc in zip(chunks, accs):
-        z_send[0, pl.ds(t, CHUNK), :] = acc
-    send(0, e)
-
-    for n in (1, 4, 2, 5):
-        loads[n].wait()
+    loads[1].wait()
+    for load in loads[2:]:
+        load.start()
+    send(0, e, True, ())
+    for which in (0, 1):
+        pack(0, e, which)
+        send(0, e, False, (which,))
+
+    for load in loads[2:6]:
+        load.wait()
 
     def screen(x, _):
         for half in (0, 1):
             for t in chunks:
                 rows = pl.ds(t, CHUNK)
                 up = jnp.exp(pot[x, half, rows, :])
-                rd[x, half, rows, :] = ion[x, half, rows, :] * (0.5 * (up + 1.0 / up))
+                rd[x, half, rows, :] = ion[x, half, rows, :] * (0.5 * (up + inverse_of(up)))
         return 0
 
-    lax.fori_loop(0, span_x, screen, 0)
-    receive(0, e)
-
-    odd = lane % 2 == 1
-    for t in chunks:
-        rows = pl.ds(t, CHUNK)
-        own = z_send[0, rows, :]
-        low = harmonic(z_recv[0, 0, rows, :], pltpu.roll(own, LANES - 1, 1))
-        high = harmonic(z_recv[0, 1, rows, :], pltpu.roll(own, 1, 1))
-        zf[0, rows, :] = jnp.where(odd, low, 0.0)
-        zf[1, rows, :] = jnp.where(odd, 0.0, high)
-        zf[2, rows, :] = pltpu.roll(zf[0, rows, :], 2, 1) + zf[1, rows, :]
-
-    for half in (0, 1):
-        for t in chunks:
-            rows = pl.ds(PAD + t, CHUNK)
-            fx[0, half, pl.ds(t, CHUNK), :] = harmonic(e[0, half, rows, :], e[1, half, rows, :])
-
+    lax.fori_loop(0, span_x, screen, 0, unroll=2)
     loads[6].wait()
 
-    def faces(x, carry):
-        accs, total = carry
-        unpack_y(0, e, x)
+    def x_face(x):
+        for half in (0, 1):
+            for t in chunks:
+                rows = pl.ds(PAD + t, CHUNK)
+                fx[x, half, pl.ds(t, CHUNK), :] = harmonic(e[x, half, rows, :], e[x + 1, half, rows, :])
+
+    def faces(which, i, total):
+        x = plane_of(i)
         for half in (0, 1):
             fy[x, half, pl.ds(PAD - 1, 1), :] = harmonic(
                 e[x + 1, half, pl.ds(PAD - 1, 1), :], e[x + 1, half, pl.ds(PAD, 1), :]
             )
-        out = []
-        for t, acc in zip(chunks, accs):
+        for t in chunks:
             rows, wide = pl.ds(t, CHUNK), pl.ds(PAD + t, CHUNK)
             center = [e[x + 1, half, wide, :] for half in (0, 1)]
-            turned = [pltpu.roll(c, LANES - 1, 1) for c in center]
-            z_next = [jnp.where(lane == LANES - 1, turned[1], turned[0]), turned[1]]
-            z_face = [harmonic(c, n) for c, n in zip(center, z_next)]
-            z_face[1] = jnp.where(lane == LANES - 1, 0.0, z_face[1])
-            back = [pltpu.roll(f, 1, 1) for f in z_face]
-            outer = open_z(zf[2, rows, :], x)
-            z_both = [
-                z_face[0] + jnp.where(lane == 0, outer, back[0]),
-                z_face[1] + jnp.where(lane == 0, back[0], back[1])
-                + jnp.where(lane == LANES - 1, outer, 0.0),
-            ]
-            fields = []
+            after, before = z_neighbours(center, outer_z(which, t, x))
             for half in (0, 1):
                 c = center[half]
-                x_face = harmonic(c, e[x + 2, half, wide, :])
-                fx[x + 1, half, rows, :] = x_face
-                y_face = harmonic(c, e[x + 1, half, pl.ds(PAD + t + 1, CHUNK), :])
-                fy[x, half, wide, :] = y_face
-                fz[x, half, rows, :] = z_face[half]
+                x_next = harmonic(c, e[x + 2, half, wide, :])
+                fx[x + 1, half, rows, :] = x_next
+                y_next = harmonic(c, e[x + 1, half, pl.ds(PAD + t + 1, CHUNK), :])
+                fy[x, half, wide, :] = y_next
+                z_next, z_last = harmonic(c, after[half]), harmonic(c, before[half])
+                fz[x, half, rows, :] = z_next
+                fzm[x, half, rows, :] = z_last
                 diagonal = (
-                    x_face + fx[x, half, rows, :]
-                    + y_face + fy[x, half, pl.ds(PAD + t - 1, CHUNK), :]
-                    + z_both[half] + rd[x, half, rows, :]
+                    x_next + fx[x, half, rows, :]
+                    + y_next + fy[x, half, pl.ds(PAD + t - 1, CHUNK), :]
+                    + z_next + z_last + rd[x, half, rows, :]
                 )
-                inverse = 1.0 / diagonal
+                inverse = inverse_of(diagonal)
                 rd[x, half, rows, :] = inverse
                 source = b[pl.ds(x * (2 * span_y) + 2 * t + half, CHUNK, stride=2), :]
                 value = source * inverse
                 v0[x + 1, half, wide, :] = value
                 total = total + source * value
-                fields.append(value)
-            out.append(pack_z(acc, fields[0], fields[1], x))
-        pack_y(1, v0, x)
-        return tuple(out), total
+        return total
+
+    def ready(k, field):
+        def before(which):
+            receive(k, field, which == 1, (which,))
+            unpack(k, field, which)
+            if k == 0:
+                x_face(START if which == 0 else 0)
+
+        return before
+
+    def done(k, field):
+        def after(which):
+            if which == 1:
+                send(k, field, True, ())
+            pack(k, field, which)
+            send(k, field, False, (which,))
+
+        return after
 
     nothing = jnp.zeros((CHUNK, LANES), F)
-    accs, total = lax.fori_loop(0, span_x, faces, (empty, nothing))
-    moments = [total]
-
-    for k in range(3):
-        v = vs[k]
-        last = k == 2
-        for t, acc in zip(chunks, accs):
-            z_send[k + 1, pl.ds(t, CHUNK), :] = acc
-        send(k + 1, v)
-        receive(k + 1, v)
-        for t in chunks:
-            rows = pl.ds(t, CHUNK)
-            zf[2, rows, :] = (
-                pltpu.roll(zf[0, rows, :] * z_recv[k + 1, 0, rows, :], 2, 1)
-                + zf[1, rows, :] * z_recv[k + 1, 1, rows, :]
-            )
-
-        def apply(x, carry, v=v, k=k, last=last):
-            accs, first, second = carry
-            unpack_y(k + 1, v, x)
-            out = []
-            for t, acc in zip(chunks, accs):
+    moments = [both_parts(faces, nothing, ready(0, e), done(1, v0), UNROLL_FACES)]
+
+    for k in (0, 1):
+        v, result = vs[k], vs[k + 1]
+
+        def apply(which, i, carry, v=v, result=result):
+            first, second = carry
+            x = plane_of(i)
+            for t in chunks:
                 rows, wide = pl.ds(t, CHUNK), pl.ds(PAD + t, CHUNK)
                 up, down = pl.ds(PAD + t + 1, CHUNK), pl.ds(PAD + t - 1, CHUNK)
                 center = [v[x + 1, half, wide, :] for half in (0, 1)]
-                turned = [pltpu.roll(c, LANES - 1, 1) for c in center]
-                z_next = [jnp.where(lane == LANES - 1, turned[1], turned[0]), turned[1]]
-                z_face = [fz[x, half, rows, :] for half in (0, 1)]
-                back = [pltpu.roll(f * c, 1, 1) for f, c in zip(z_face, center)]
-                outer = open_z(zf[2, rows, :], x)
-                z_both = [
-                    z_face[0] * z_next[0] + jnp.where(lane == 0, outer, back[0]),
-                    z_face[1] * z_next[1] + jnp.where(lane == 0, back[0], back[1])
-                    + jnp.where(lane == LANES - 1, outer, 0.0),
-                ]
-                fields = []
+                after, before = z_neighbours(center, outer_z(which, t, x))
                 for half in (0, 1):
                     image = (
                         fx[x + 1, half, rows, :] * v[x + 2, half, wide, :]
                         + fx[x, half, rows, :] * v[x, half, wide, :]
                         + fy[x, half, wide, :] * v[x + 1, half, up, :]
                         + fy[x, half, down, :] * v[x + 1, half, down, :]
-                        + z_both[half]
+                        + fz[x, half, rows, :] * after[half]
+                        + fzm[x, half, rows, :] * before[half]
                     )
+                    value = image * rd[x, half, rows, :]
+                    result[x + 1, half, wide, :] = value
                     first = first + center[half] * image
-                    if not last:
-                        value = image * rd[x, half, rows, :]
-                        vs[k + 1][x + 1, half, wide, :] = value
-                        second = second + image * value
-                        fields.append(value)
-                out.append(acc if last else pack_z(acc, fields[0], fields[1], x))
-            if not last:
-                pack_y(k + 2, vs[k + 1], x)
-            return tuple(out), first, second
-
-        accs, first, second = lax.fori_loop(0, span_x, apply, (empty, nothing, nothing))
-        moments.append(first)
-        if not last:
-            moments.append(second)
+                    second = second + image * value
+            return first, second
+
+        moments.extend(
+            both_parts(
+                apply, (nothing, nothing), ready(k + 1, v), done(k + 2, result), UNROLL_APPLY
+            )
+        )
+
+    def product(which, i, total):
+        x = plane_of(i)
+        for t in chunks:
+            rows, wide = pl.ds(t, CHUNK), pl.ds(PAD + t, CHUNK)
+            center = [v2[x + 1, half, wide, :] for half in (0, 1)]
+            after = [pltpu.roll(c, LANES - 1, 1) for c in center]
+            after = [
+                jnp.where(at_last, after[1], after[0]),
+                jnp.where(at_last, outer_z(which, t, x), after[1]),
+            ]
+            for half in (0, 1):
+                image = (
+                    fx[x + 1, half, rows, :] * v2[x + 2, half, wide, :]
+                    + fy[x, half, wide, :] * v2[x + 1, half, pl.ds(PAD + t + 1, CHUNK), :]
+                    + fz[x, half, rows, :] * after[half]
+                )
+                total = total + center[half] * image
+        return total
+
+    total = both_parts(product, nothing, ready(3, v2), lambda which: None, UNROLL_APPLY)
+    moments.append(2.0 * total)
 
     row = lax.broadcasted_iota(jnp.int32, (8, LANES), 0)
     mine = jnp.zeros((8, LANES), F)
@@ -505,7 +555,7 @@
                 b[pl.ds(x * (2 * span_y) + 2 * t + half, CHUNK, stride=2), :] = value
         return 0
 
-    lax.fori_loop(0, span_x, finish, 0)
+    lax.fori_loop(0, span_x, finish, 0, unroll=2)
     stores = [
         pltpu.make_async_copy(
             pot.at[:, half], out_ref.at[:, :, pl.ds(half * LANES, LANES)], sem_out.at[half]
@@ -516,7 +566,7 @@
     for store in stores:
         store.start()
     for k, field in enumerate((e, v0, v1, v2)):
-        sent(k, field)
+        sent(k, field, True, (0, 1))
     for store in stores:
         store.wait()
 
@@ -549,13 +599,13 @@
             plain,
             pltpu.VMEM((4, 2, 2, span_x, LANES), F),
             pltpu.VMEM((4, 2, 2, span_x, LANES), F),
-            pltpu.VMEM((4, span_y, LANES), F),
             pltpu.VMEM((4, 2, span_y, LANES), F),
-            pltpu.VMEM((3, span_y, LANES), F),
+            pltpu.VMEM((4, 2, 2, span_y, LANES), F),
+            pltpu.VMEM((2, span_y, LANES), F),
             pltpu.VMEM((3, most, 8, LANES), F),
             dma((7,)),
-            dma((4, 6)),
-            dma((4, 6)),
+            dma((4, 10)),
+            dma((4, 10)),
             dma((3, most)),
             dma((3, most)),
             dma((3,)),

time: 151 us -> 113 us (0.75)
  Pallas kernels: 123 us -> 84.6 us
    pallas_call x1, Pallas kernels: 90.3 us -> 52.1 us  [krylov(): pl.pallas_call(functools.partial(krylov_kernel, sizes), out_shape=(jax.Sh...]
where the time goes in v2:
time: 113 us; the launch traced here: 112 us
  Pallas kernels  84.6 us (75%)
  blocking collectives  9.8 us (9%)
  waiting for transfers between devices  5.18 us (5%)
  other arithmetic  4.43 us (4%)
  local copies, waits for them, and re-layouts  3.91 us (3%)
  starting transfers between devices  3.25 us (3%)
    pallas_call x1, Pallas kernels, krylov(): pl.pallas_call(functools.partial(krylov_kernel, sizes), out_shape=(jax.Sh...  52.1 us
    pallas_call x1, Pallas kernels, sample(): pl.pallas_call(functools.partial(sample_kernel, slots, span_y), out_shape...  16.4 us
    pallas_call x1, Pallas kernels, spread(): pl.pallas_call(functools.partial(spread_kernel, slots, span[1]), out_shap...  16.1 us
    all_to_all x1, blocking collectives, per_device(): lax.all_to_all(record, 'gz', split_axis=1, concat_axis=1, tiled=True)  9.8 us
    all_to_all x1, waiting for transfers between devices, per_device(): lax.all_to_all(sampled[0].reshape(groups, capacity), 'gz', split_axis=0,...  5.18 us
    all_to_all x1, starting transfers between devices, per_device(): lax.all_to_all(sampled[0].reshape(groups, capacity), 'gz', split_axis=0,...  3.25 us
  transfers between devices with their start and end apart: 1, of which 1 were waited for; matrix products, arithmetic and copies ran while one was open for 0% of the time, Pallas kernels for 0%

profile of v2, /device:TPU:0, one launch (start us, length us, event | category | flops | bytes accessed | tf_op | source)
XLA Modules:
  0.0 111.8 jit_solution(6649758386464947355)
XLA Ops:
  0.6 0.5 broadcast.41
  1.1 1.4 %reduce.6 = f32[2048]{0:T(1024)S(1)} reduce(f32[1,1,1,2048]{3,2,1,0:T(1,128)} %param.7, f32[]{:T(128)} %broadcast.41), dimensions={0,1,2}, to_apply=%param.7.reduce_sub_computation.3 | reduce | bytes 16388 | tf_op args[0]
  2.5 0.8 convert_reduce_fusion
  3.4 0.8 reduce.1
  4.2 0.7 fusion.1
  5.0 9.8 %all_to_all.17 = f32[7,4,512]{2,0,1:T(8,128)S(1)} all-to-all(f32[7,4,512]{2,0,1:T(8,128)S(1)} %copy.14), channel_id=1, replica_groups=mesh['gx'=4,'gy'=8,'gz'=4] {'gz'}, dimensions={1} | all-to-all | bytes 114688 | tf_op jit(solution)/shard_map/all_to_all | solution.py:631
  14.8 0.6 copy.19
  15.5 0.6 copy.20
  16.1 0.6 slice.18
  16.7 16.1 %spread.1.b_ref = f32[8192,128]{1,0:T(8,128)} custom-call(f32[2048]{0:T(1024)} %bitcast.14, f32[6144]{0:T(1024)} %bitcast.10, s32[6144]{0:T(1024)} %bitcast.12), custom_call_target="tpu_custom_call" | custom-call | tf_op jit(solution)/shard_map/spread/pallas_call | solution.py:88
  32.8 52.1 %krylov.1 = (f32[64,64,256]{2,1,0:T(8,128)}, f32[8192,128]{1,0:T(8,128)}) custom-call(f32[8192,128]{1,0:T(8,128)} %spread.1.b_ref, f32[64,64,256]{2,1,0:T(8,128)} %eps_ref.1, f32[64,64,256]{2,1,0:T(8,128)} %pot_ref.1, f32[64,64,256]{2,1,0:T(8,128)} %ion_ref.1), custom_call_target="tpu_custom_call" | custom-call | tf_op jit(solution)/shard_map/krylov/pallas_call | solution.py:582
  84.8 0.0 copy-start
  84.8 16.4 %sample.1 = (f32[64,64,256]{2,1,0:T(8,128)}, f32[8,2048]{1,0:T(8,128)}) custom-call(f32[6144]{0:T(1024)} %bitcast.11, s32[6144]{0:T(1024)} %bitcast.13, f32[8192,128]{1,0:T(8,128)} %get-tuple-element.6.rows_ref, f32[64,64,256]{2,1,0:T(8,128)} %get-tuple-element.7.grid_ref), custom_call_target="tpu_custom_call" | custom-call | tf_op jit(solution)/shard_map/sample/pallas_call | solution.py:163
  101.3 1.4 %slice.15 = f32[1,2048]{1,0:T(1,128)} slice(f32[8,2048]{1,0:T(8,128)} %get-tuple-element.9), slice={[0:1], [0:2048]} | slice | bytes 16384 | tf_op jit(solution)/shard_map/slice | solution.py:639
  102.7 3.2 %all-to-all-start.1 = ((f32[4,1,512]{2,1,0:T(1,128)}), f32[4,1,512]{2,1,0:T(1,128)S(1)}, u32[]{:S(2)}, u32[]{:S(2)}) async-start(f32[4,1,512]{2,1,0:T(1,128)} %bitcast.2), calls=%async_computation.1 | async-start | bytes 16384 | tf_op jit(solution)/shard_map/all_to_all | solution.py:638
  106.0 0.0 copy-done
  106.0 0.1 iota_compare_fusion
  106.1 5.2 %all-to-all-done.1 = f32[4,1,512]{2,1,0:T(1,128)S(1)} async-done(((f32[4,1,512]{2,1,0:T(1,128)}), f32[4,1,512]{2,1,0:T(1,128)S(1)}, u32[]{:S(2)}, u32[]{:S(2)}) %all-to-all-start.1) | async-done | bytes 8224 | tf_op jit(solution)/shard_map/all_to_all | solution.py:638
  111.2 0.6 broadcast_select_fusion
  (8 shorter events, 0.2 us)
Async XLA Ops:
  84.8 21.1 %copy-start = (s32[1,1,1,4]{3,2,1,0:T(1,128)S(1)}, s32[1,1,1,4]{3,2,1,0:T(1,128)}, u32[]{:S(2)}) copy-start(s32[1,1,1,4]{3,2,1,0:T(1,128)} %param.10) | copy-start | bytes 52
  102.7 8.5 %all-to-all-start.1 = ((f32[4,1,512]{2,1,0:T(1,128)}), f32[4,1,512]{2,1,0:T(1,128)S(1)}, u32[]{:S(2)}, u32[]{:S(2)}) async-start(f32[4,1,512]{2,1,0:T(1,128)} %bitcast.2), calls=%async_computation.1 | async-start | bytes 16384 | tf_op jit(solution)/shard_map/all_to_all | solution.py:638

commit v3 on v2

--- a/solution.py
+++ b/solution.py
@@ -26,14 +26,162 @@
     return row, ((row % 2) * LANES + lane).astype(F)
 
 
-def z_hat(pos, cz, fz):
-    return jnp.maximum(1.0 - jnp.abs((pos - cz) - fz), 0.0)
-
-
-def spread_kernel(slots, span_y, q_ref, f_ref, c_ref, out_ref, *scratch):
+def z_hat(pos, z):
+    return jnp.maximum(1.0 - jnp.abs(pos - z), 0.0)
+
+
+def greet(axis, size):
+    barrier, place = pltpu.get_barrier_semaphore(), lax.axis_index(axis)
+    for step in range(1, size):
+        pl.semaphore_signal(
+            barrier, inc=1, device_id={axis: lax.rem(place + step, size)}, device_id_type=MESH
+        )
+    pl.semaphore_wait(barrier, size - 1)
+
+
+def deliver_kernel(
+    size, span_y, q_ref, f_ref, c_ref, count_ref, index_ref, value_ref, q_out, q_in, f_in, c_in, send_sem, recv_sem
+):
+    place = lax.axis_index("gz")
+    capacity = q_out.shape[2]
+    slot = lax.broadcasted_iota(jnp.int32, (1, capacity), 1)
+    for g in range(size):
+        block = pl.ds(g * capacity, capacity)
+        q_out[g] = jnp.where(slot < count_ref[0, 0, 0, g], q_ref[0, 0, :, block], 0.0)
+    greet("gz", size)
+
+    def copies(step, to, source):
+        block = pl.ds(pl.multiple_of(to * capacity, capacity), capacity)
+        parts = (
+            (q_out.at[to], q_in.at[source]),
+            (f_ref.at[:, 0, 0, :, block], f_in.at[source]),
+            (c_ref.at[:, 0, 0, :, block], c_in.at[source]),
+        )
+        return [
+            pltpu.make_async_remote_copy(
+                src_ref=src,
+                dst_ref=dst,
+                send_sem=send_sem.at[step, n],
+                recv_sem=recv_sem.at[step, n],
+                device_id={"gz": to},
+                device_id_type=MESH,
+            )
+            for n, (src, dst) in enumerate(parts)
+        ]
+
+    out = []
+    for step in range(1, size):
+        out.extend(copies(step, lax.rem(place + step, size), place))
+    for copy in out:
+        copy.start()
+
+    def work_out(source, q, f, c):
+        index_ref[source] = (c[0] * span_y + c[1]) * 2
+        value_ref[source, 0] = c[2].astype(F) + f[2]
+        value_ref[source, 1] = f[1]
+        value_ref[source, 2] = f[0]
+        value_ref[source, 3] = q * (1.0 - f[0])
+        value_ref[source, 4] = q * f[0]
+
+    own = pl.ds(pl.multiple_of(place * capacity, capacity), capacity)
+    work_out(
+        place,
+        q_out[place],
+        [f_ref[k, 0, 0, :, own] for k in range(3)],
+        [c_ref[k, 0, 0, :, own] for k in range(3)],
+    )
+    for step in range(1, size):
+        source = lax.rem(place + size - step, size)
+        for copy in copies(step, lax.rem(place + step, size), source):
+            copy.wait_recv()
+        work_out(
+            source,
+            q_in[source],
+            [f_in[source, k] for k in range(3)],
+            [c_in[source, k] for k in range(3)],
+        )
+    for copy in out:
+        copy.wait_send()
+
+
+def deliver(size, span_y, charge, fraction, corner, count):
+    capacity = charge.shape[3] // size
+    vmem = pl.BlockSpec(memory_space=pltpu.VMEM)
+    dma = pltpu.SemaphoreType.DMA
+    return pl.pallas_call(
+        functools.partial(deliver_kernel, size, span_y),
+        out_shape=(
+            jax.ShapeDtypeStruct((size, 1, capacity), jnp.int32),
+            jax.ShapeDtypeStruct((size, 5, 1, capacity), F),
+        ),
+        in_specs=[vmem, vmem, vmem, pl.BlockSpec(memory_space=pltpu.SMEM)],
+        out_specs=(vmem, vmem),
+        scratch_shapes=[
+            pltpu.VMEM((size, 1, capacity), F),
+            pltpu.VMEM((size, 1, capacity), F),
+            pltpu.VMEM((size, 3, 1, capacity), F),
+            pltpu.VMEM((size, 3, 1, capacity), jnp.int32),
+            dma((size, 3)),
+            dma((size, 3)),
+        ],
+        compiler_params=pltpu.CompilerParams(collective_id=1, has_side_effects=True),
+        name="deliver",
+    )(charge, fraction, corner, count)
+
+
+def give_back_kernel(size, sampled_ref, count_ref, out_ref, came, send_sem, recv_sem):
+    place = lax.axis_index("gz")
+    capacity = came.shape[2]
+    slot = lax.broadcasted_iota(jnp.int32, (1, capacity), 1)
+    greet("gz", size)
+
+    def copy_of(step, to, source):
+        block = pl.ds(pl.multiple_of(to * capacity, capacity), capacity)
+        return pltpu.make_async_remote_copy(
+            src_ref=sampled_ref.at[:, block],
+            dst_ref=came.at[source],
+            send_sem=send_sem.at[step],
+            recv_sem=recv_sem.at[step],
+            device_id={"gz": to},
+            device_id_type=MESH,
+        )
+
+    out = [copy_of(step, lax.rem(place + step, size), place) for step in range(1, size)]
+    for copy in out:
+        copy.start()
+
+    def put(source, values):
+        block = pl.ds(pl.multiple_of(source * capacity, capacity), capacity)
+        out_ref[0, 0, :, block] = jnp.where(slot < count_ref[0, 0, 0, source], values, 0.0)
+
+    put(place, sampled_ref[:, pl.ds(pl.multiple_of(place * capacity, capacity), capacity)])
+    for step in range(1, size):
+        source = lax.rem(place + size - step, size)
+        copy_of(step, lax.rem(place + step, size), source).wait_recv()
+        put(source, came[source])
+    for copy in out:
+        copy.wait_send()
+
+
+def give_back(size, sampled, count):
+    slots = sampled.shape[1]
+    vmem = pl.BlockSpec(memory_space=pltpu.VMEM)
+    dma = pltpu.SemaphoreType.DMA
+    return pl.pallas_call(
+        functools.partial(give_back_kernel, size),
+        out_shape=jax.ShapeDtypeStruct((1, 1, 1, slots), F),
+        in_specs=[vmem, pl.BlockSpec(memory_space=pltpu.SMEM)],
+        out_specs=vmem,
+        scratch_shapes=[pltpu.VMEM((size, 1, slots // size), F), dma((size,)), dma((size,))],
+        compiler_params=pltpu.CompilerParams(collective_id=2, has_side_effects=True),
+        name="give_back",
+    )(sampled, count)
+
+
+def spread_kernel(span_y, index_ref, value_ref, out_ref, *scratch):
     tables, sem = scratch[:TABLES], scratch[TABLES]
     rows = out_ref.shape[0]
-    block = 64
+    block = 128
 
     def clear(i, _):
         for table in tables:
@@ -47,26 +195,26 @@
     ya = jnp.where(row < 2, 1.0, 0.0).astype(F)
     yb = jnp.where(row < 2, -1.0, jnp.where(row < 4, 1.0, 0.0)).astype(F)
     plane = 2 * span_y
-
-    def body(i, _):
-        for first in range(0, SLOTS_PER_STEP, TABLES):
-            items = []
-            for which, table in enumerate(tables):
-                s = i * SLOTS_PER_STEP + first + which
-                r = pl.multiple_of((c_ref[s] * span_y + c_ref[slots + s]) * 2, 2)
-                cz = c_ref[2 * slots + s].astype(F)
-                fx, fy, fz = f_ref[s], f_ref[slots + s], f_ref[2 * slots + s]
-                q = q_ref[s]
-                w = (ya + yb * fy) * z_hat(pos, cz, fz)
-                near = table[pl.ds(r, 8), :] + w * (q * (1.0 - fx))
-                far = table[pl.ds(r + plane, 8), :] + w * (q * fx)
-                items.append((table, r, near, far))
-            for table, r, near, far in items:
-                table[pl.ds(r, 8), :] = near
-                table[pl.ds(r + plane, 8), :] = far
-        return 0
-
-    lax.fori_loop(0, slots // SLOTS_PER_STEP, body, 0)
+    groups, _, capacity = index_ref.shape
+
+    for g in range(groups):
+
+        def body(i, _, g=g):
+            for first in range(0, SLOTS_PER_STEP, TABLES):
+                items = []
+                for which, table in enumerate(tables):
+                    s = i * SLOTS_PER_STEP + first + which
+                    r = pl.multiple_of(index_ref[g, 0, s], 2)
+                    w = (ya + yb * value_ref[g, 1, 0, s]) * z_hat(pos, value_ref[g, 0, 0, s])
+                    near = table[pl.ds(r, 8), :] + w * value_ref[g, 3, 0, s]
+                    far = table[pl.ds(r + plane, 8), :] + w * value_ref[g, 4, 0, s]
+                    items.append((table, r, near, far))
+                for table, r, near, far in items:
+                    table[pl.ds(r, 8), :] = near
+                    table[pl.ds(r + plane, 8), :] = far
+            return 0
+
+        lax.fori_loop(0, capacity // SLOTS_PER_STEP, body, 0)
 
     def combine(i, _):
         part = pl.ds(pl.multiple_of(i * block, block), block)
@@ -82,59 +230,61 @@
     copy.wait()
 
 
-def spread(charge, fraction, corner, span):
-    slots = charge.shape[0]
+def spread(index, value, span):
     rows = span[0] * span[1] * 2
     return pl.pallas_call(
-        functools.partial(spread_kernel, slots, span[1]),
+        functools.partial(spread_kernel, span[1]),
         out_shape=jax.ShapeDtypeStruct((rows, LANES), F),
-        in_specs=[pl.BlockSpec(memory_space=pltpu.SMEM)] * 3,
+        in_specs=[pl.BlockSpec(memory_space=pltpu.SMEM)] * 2,
         out_specs=pl.BlockSpec(memory_space=pl.ANY),
         scratch_shapes=[pltpu.VMEM((rows + 8, LANES), F)] * TABLES + [pltpu.SemaphoreType.DMA(())],
         compiler_params=pltpu.CompilerParams(vmem_limit_bytes=56 << 20),
         name="spread",
-    )(charge, fraction, corner)
+    )(index, value)
 
 
 def sample_kernel(
-    slots, span_y, f_ref, c_ref, rows_ref, grid_ref, field_ref, out_ref, table, grid, parts, sums, sems
+    span_y, index_ref, value_ref, rows_ref, grid_ref, field_ref, out_ref, table, grid, parts, sums, sems
 ):
     rows = rows_ref.shape[0]
     load = pltpu.make_async_copy(rows_ref, table.at[pl.ds(8, rows), :], sems.at[1])
     load.start()
-    hold = pltpu.make_async_copy(grid_ref, grid, sems.at[0])
-    hold.start()
     table[pl.ds(0, 8), :] = jnp.zeros((8, LANES), F)
     table[pl.ds(rows + 8, 8), :] = jnp.zeros((8, LANES), F)
     load.wait()
-    hold.wait()
-    keep = pltpu.make_async_copy(grid, field_ref, sems.at[2])
-    keep.start()
+    hold = pltpu.make_async_copy(grid_ref, grid, sems.at[0])
+    hold.start()
     row, pos = patterns()
     first_row, second_row = row % 4 < 2, row < 4
     yb = jnp.where(first_row, -1.0, 1.0).astype(F)
     ya = jnp.where(first_row, 1.0, 0.0).astype(F)
     masks = [jnp.where(second_row, 1.0, 0.0).astype(F), jnp.where(second_row, 0.0, 1.0).astype(F)]
+    weights = [(ya * mask, yb * mask) for mask in masks]
     plane = 2 * span_y
-
-    def body(i, _):
-        for pair in range(SLOTS_PER_STEP // 2):
-            total = None
-            for which in (0, 1):
-                s = i * SLOTS_PER_STEP + 2 * pair + which
-                r = pl.multiple_of((c_ref[s] * span_y + c_ref[slots + s]) * 2, 2)
-                r = r + (8 - 4 * which)
-                cz = c_ref[2 * slots + s].astype(F)
-                fx, fy, fz = f_ref[s], f_ref[slots + s], f_ref[2 * slots + s]
-                w = (ya * masks[which] + (yb * masks[which]) * fy) * z_hat(pos, cz, fz)
-                near, far = table[pl.ds(r, 8), :], table[pl.ds(r + plane, 8), :]
-                term = w * (near * (1.0 - fx) + far * fx)
-                total = term if total is None else total + term
-            start = pl.multiple_of((i * (SLOTS_PER_STEP // 2) + pair) * 8, 8)
-            parts[pl.ds(start, 8), :] = total
-        return 0
-
-    lax.fori_loop(0, slots // SLOTS_PER_STEP, body, 0)
+    groups, _, capacity = index_ref.shape
+    keep = pltpu.make_async_copy(grid, field_ref, sems.at[2])
+
+    for g in range(groups):
+
+        def body(i, _, g=g):
+            for pair in range(SLOTS_PER_STEP // 2):
+                total = None
+                for which in (0, 1):
+                    s = i * SLOTS_PER_STEP + 2 * pair + which
+                    r = pl.multiple_of(index_ref[g, 0, s], 2) + (8 - 4 * which)
+                    wa, wb = weights[which]
+                    w = (wa + wb * value_ref[g, 1, 0, s]) * z_hat(pos, value_ref[g, 0, 0, s])
+                    near, far = table[pl.ds(r, 8), :], table[pl.ds(r + plane, 8), :]
+                    term = w * (near + value_ref[g, 2, 0, s] * (far - near))
+                    total = term if total is None else total + term
+                start = i * (SLOTS_PER_STEP // 2) + (g * (capacity // 2) + pair)
+                parts[pl.ds(pl.multiple_of(start * 8, 8), 8), :] = total
+            return 0
+
+        lax.fori_loop(0, capacity // SLOTS_PER_STEP, body, 0)
+        if g == 0:
+            hold.wait()
+            keep.start()
 
     def fold(i, _):
         start = pl.multiple_of(i * 256, 256)
@@ -144,27 +294,26 @@
         sums[pl.ds(pl.multiple_of(i * 64, 64), 64), :] = total
         return 0
 
-    lax.fori_loop(0, slots // 64, fold, 0)
+    lax.fori_loop(0, groups * capacity // 64, fold, 0)
     out_ref[...] = lax.dot_general(
         jnp.ones((8, LANES), F),
         sums[...],
         (((1,), (1,)), ((), ())),
         precision=lax.Precision.HIGHEST,
         preferred_element_type=F,
-    )
+    )[0:1]
     keep.wait()
 
 
-def sample(fraction, corner, rows_field, grid_field):
-    slots = fraction.shape[0] // 3
-    span_x, span_y, span_z = grid_field.shape
-    rows = rows_field.shape[0]
+def sample(index, value, rows_field, grid_field):
+    span_y, rows = grid_field.shape[1], rows_field.shape[0]
+    slots = index.shape[0] * index.shape[2]
     smem, anywhere = pl.BlockSpec(memory_space=pltpu.SMEM), pl.BlockSpec(memory_space=pl.ANY)
     return pl.pallas_call(
-        functools.partial(sample_kernel, slots, span_y),
+        functools.partial(sample_kernel, span_y),
         out_shape=(
             jax.ShapeDtypeStruct(grid_field.shape, F),
-            jax.ShapeDtypeStruct((8, slots), F),
+            jax.ShapeDtypeStruct((1, slots), F),
         ),
         in_specs=[smem, smem, anywhere, anywhere],
         out_specs=(anywhere, pl.BlockSpec(memory_space=pltpu.VMEM)),
@@ -177,7 +326,7 @@
         ],
         compiler_params=pltpu.CompilerParams(vmem_limit_bytes=56 << 20),
         name="sample",
-    )(fraction, corner, rows_field, grid_field)
+    )(index, value, rows_field, grid_field)
 
 
 def inverse_of(value):
@@ -621,25 +770,13 @@
     atom_charge, atom_fraction, atom_corner, block_count, permittivity, base_potential, ion_access
 ):
     sizes = tuple(lax.axis_size(axis) for axis in AXES)
-    groups = sizes[2]
-    capacity = atom_charge.shape[3] // groups
-    live = jnp.arange(capacity, dtype=jnp.int32)[None, :] < block_count.reshape(groups, 1)
-    charge = jnp.where(live, atom_charge.reshape(groups, capacity), 0.0)
-    fraction = atom_fraction.reshape(3, groups, capacity)
-    corner = atom_corner.reshape(3, groups, capacity)
-    record = jnp.concatenate([charge[None], fraction, corner.astype(F)], axis=0)
-    arrived = lax.all_to_all(record, "gz", split_axis=1, concat_axis=1, tiled=True)
-    there_charge = arrived[0].reshape(-1)
-    there_fraction = arrived[1:4].reshape(-1)
-    there_corner = arrived[4:7].astype(jnp.int32).reshape(-1)
-    sources = spread(there_charge, there_fraction, there_corner, permittivity.shape)
+    index, value = deliver(
+        sizes[2], permittivity.shape[1], atom_charge, atom_fraction, atom_corner, block_count
+    )
+    sources = spread(index, value, permittivity.shape)
     grid_field, rows_field = krylov(sizes, sources, permittivity, base_potential, ion_access)
-    solution_field, sampled = sample(there_fraction, there_corner, rows_field, grid_field)
-    returned = lax.all_to_all(
-        sampled[0].reshape(groups, capacity), "gz", split_axis=0, concat_axis=0, tiled=True
-    )
-    atom_sensitivity = jnp.where(live, returned, 0.0).reshape(1, 1, 1, groups * capacity)
-    return (solution_field, atom_sensitivity)
+    solution_field, sampled = sample(index, value, rows_field, grid_field)
+    return solution_field, give_back(sizes[2], sampled, block_count)
 
 
 def solution(mesh):

time: 113 us -> 103 us (0.912)
  Pallas kernels: 84.6 us -> 100 us
  blocking collectives: 9.8 us -> 0 us
  waiting for transfers between devices: 5.18 us -> 0 us
  other arithmetic: 4.43 us -> 0 us
  starting transfers between devices: 3.25 us -> 0 us
  local copies, waits for them, and re-layouts: 3.91 us -> 1.3 us
    pallas_call x2 -> x4, Pallas kernels: 32.5 us -> 47.9 us  [the longest x1 17.1 us: spread(): pl.pallas_call(functools.partial(spread_kernel, span[1]), out_shape=jax.S...]
    all_to_all x1 -> x0, blocking collectives: 9.8 us -> none  [per_device(): lax.all_to_all(record, 'gz', split_axis=1, concat_axis=1, tiled=True)]
    all_to_all x1 -> x0, waiting for transfers between devices: 5.18 us -> none  [per_device(): lax.all_to_all(sampled[0].reshape(groups, capacity), 'gz', split_axis=0,...]
    all_to_all x1 -> x0, starting transfers between devices: 3.25 us -> none  [per_device(): lax.all_to_all(sampled[0].reshape(groups, capacity), 'gz', split_axis=0,...]
    unnamed x3 -> x0, other arithmetic: 2.19 us -> none
    slice x3 -> x0, local copies, waits for them, and re-layouts: 2.06 us -> none  [the longest x1 1.44 us: per_device(): sampled[0].reshape(groups, capacity)]
    select_n x2 -> x0, other arithmetic: 1.34 us -> none  [the longest x1 0.73 us: per_device(): charge = jnp.where(live, atom_charge.reshape(groups, capacity), 0.0)]
  transfers between devices with their start and end apart: 1 -> 0, of which waited for: 1 -> 0; matrix products, arithmetic and copies ran while one was open for 0% -> 0% of each run, Pallas kernels for 0% -> 0%
where the time goes in v3:
time: 103 us; the launch traced here: 102 us
  Pallas kernels  100 us (97%)
  local copies, waits for them, and re-layouts  1.3 us (1%)
    pallas_call x1, Pallas kernels, krylov(): pl.pallas_call(functools.partial(krylov_kernel, sizes), out_shape=(jax.Sh...  52.6 us
    pallas_call x1, Pallas kernels, spread(): pl.pallas_call(functools.partial(spread_kernel, span[1]), out_shape=jax.S...  17.1 us
    pallas_call x1, Pallas kernels, sample(): pl.pallas_call(functools.partial(sample_kernel, span_y), out_shape=(jax.S...  16.2 us
    pallas_call x1, Pallas kernels, deliver(): pl.pallas_call(functools.partial(deliver_kernel, size, span_y), out_shape...  7.93 us
    pallas_call x1, Pallas kernels, give_back(): pl.pallas_call(functools.partial(give_back_kernel, size), out_shape=jax.S...  6.69 us

profile of v3, /device:TPU:0, one launch (start us, length us, event | category | flops | bytes accessed | tf_op | source)
XLA Modules:
  0.0 102.4 jit_solution(10576867960616983525)
XLA Ops:
  0.6 7.9 %deliver.1 = (s32[4,1,512]{2,1,0:T(1,128)}, f32[4,5,1,512]{3,2,1,0:T(1,128)}) custom-call(f32[1,1,1,2048]{3,2,1,0:T(1,128)} %q_ref.1, f32[3,1,1,1,2048]{4,3,2,1,0:T(1,128)} %f_ref.1, s32[3,1,1,1,2048]{4,3,2,1,0:T(1,128)} %c_ref.1, s32[1,1,1,4]{3,2,1,0:T(1,128)} %count_ref.3), custom_call_target="tpu_custom_call" | custom-call | tf_op jit(solution)/shard_map/deliver/pallas_call | solution.py:111
  8.6 17.1 %spread.1.b_ref = f32[8192,128]{1,0:T(8,128)} custom-call(s32[4,1,512]{2,1,0:T(1,128)} %get-tuple-element.8.index_ref, f32[4,5,1,512]{3,2,1,0:T(1,128)} %get-tuple-element.9.value_ref), custom_call_target="tpu_custom_call" | custom-call | tf_op jit(solution)/shard_map/spread/pallas_call | solution.py:235
  25.7 52.6 %krylov.1 = (f32[64,64,256]{2,1,0:T(8,128)}, f32[8192,128]{1,0:T(8,128)}) custom-call(f32[8192,128]{1,0:T(8,128)} %spread.1.b_ref, f32[64,64,256]{2,1,0:T(8,128)} %eps_ref.1, f32[64,64,256]{2,1,0:T(8,128)} %pot_ref.1, f32[64,64,256]{2,1,0:T(8,128)} %ion_ref.1), custom_call_target="tpu_custom_call" | custom-call | tf_op jit(solution)/shard_map/krylov/pallas_call | solution.py:731
  78.2 16.2 %sample.1 = (f32[64,64,256]{2,1,0:T(8,128)}, f32[1,2048]{1,0:T(1,128)}) custom-call(s32[4,1,512]{2,1,0:T(1,128)} %get-tuple-element.8.index_ref, f32[4,5,1,512]{3,2,1,0:T(1,128)} %get-tuple-element.9.value_ref, f32[8192,128]{1,0:T(8,128)} %get-tuple-element.10.rows_ref, f32[64,64,256]{2,1,0:T(8,128)} %get-tuple-element.11.grid_ref), custom_call_target="tpu_custom_call" | custom-call | tf_op jit(solution)/shard_map/sample/pallas_call | solution.py:312
  94.4 6.7 %give_back.1 = f32[1,1,1,2048]{3,2,1,0:T(1,128)} custom-call(f32[1,2048]{1,0:T(1,128)} %get-tuple-element.13.sampled_ref, s32[1,1,1,4]{3,2,1,0:T(1,128)} %count_ref.3), custom_call_target="tpu_custom_call" | custom-call | tf_op jit(solution)/shard_map/give_back/pallas_call | solution.py:170
  101.1 1.3 %copy.10 = f32[1,1,1,2048]{3,2,1,0:T(1,128)} copy(f32[1,1,1,2048]{3,2,1,0:T(1,128)} %give_back.1) | data formatting | bytes 16384

commit v4 on v3

--- a/solution.py
+++ b/solution.py
@@ -9,11 +9,12 @@
 
 F = jnp.float32
 AXES = ("gx", "gy", "gz")
+STAGES = (("gy",), ("gx", "gz"))
 MESH = pl.DeviceIdType.MESH
 LANES = 128
 PAD = 8
 CHUNK = 16
-SLOTS_PER_STEP = 16
+SLOTS_PER_STEP = 32
 TABLES = 2
 START = 8
 UNROLL_FACES = 4
@@ -76,12 +77,13 @@
         copy.start()
 
     def work_out(source, q, f, c):
-        index_ref[source] = (c[0] * span_y + c[1]) * 2
-        value_ref[source, 0] = c[2].astype(F) + f[2]
-        value_ref[source, 1] = f[1]
-        value_ref[source, 2] = f[0]
-        value_ref[source, 3] = q * (1.0 - f[0])
-        value_ref[source, 4] = q * f[0]
+        block = pl.ds(pl.multiple_of(source * capacity, capacity), capacity)
+        index_ref[:, block] = (c[0] * span_y + c[1]) * 2
+        value_ref[0, :, block] = c[2].astype(F) + f[2]
+        value_ref[1, :, block] = f[1]
+        value_ref[2, :, block] = f[0]
+        value_ref[3, :, block] = q * (1.0 - f[0])
+        value_ref[4, :, block] = q * f[0]
 
     own = pl.ds(pl.multiple_of(place * capacity, capacity), capacity)
     work_out(
@@ -111,8 +113,8 @@
     return pl.pallas_call(
         functools.partial(deliver_kernel, size, span_y),
         out_shape=(
-            jax.ShapeDtypeStruct((size, 1, capacity), jnp.int32),
-            jax.ShapeDtypeStruct((size, 5, 1, capacity), F),
+            jax.ShapeDtypeStruct((1, size * capacity), jnp.int32),
+            jax.ShapeDtypeStruct((5, 1, size * capacity), F),
         ),
         in_specs=[vmem, vmem, vmem, pl.BlockSpec(memory_space=pltpu.SMEM)],
         out_specs=(vmem, vmem),
@@ -195,26 +197,25 @@
     ya = jnp.where(row < 2, 1.0, 0.0).astype(F)
     yb = jnp.where(row < 2, -1.0, jnp.where(row < 4, 1.0, 0.0)).astype(F)
     plane = 2 * span_y
-    groups, _, capacity = index_ref.shape
-
-    for g in range(groups):
-
-        def body(i, _, g=g):
-            for first in range(0, SLOTS_PER_STEP, TABLES):
-                items = []
-                for which, table in enumerate(tables):
-                    s = i * SLOTS_PER_STEP + first + which
-                    r = pl.multiple_of(index_ref[g, 0, s], 2)
-                    w = (ya + yb * value_ref[g, 1, 0, s]) * z_hat(pos, value_ref[g, 0, 0, s])
-                    near = table[pl.ds(r, 8), :] + w * value_ref[g, 3, 0, s]
-                    far = table[pl.ds(r + plane, 8), :] + w * value_ref[g, 4, 0, s]
-                    items.append((table, r, near, far))
-                for table, r, near, far in items:
-                    table[pl.ds(r, 8), :] = near
-                    table[pl.ds(r + plane, 8), :] = far
-            return 0
-
-        lax.fori_loop(0, capacity // SLOTS_PER_STEP, body, 0)
+
+    steps = index_ref.shape[1] // SLOTS_PER_STEP
+
+    def body(i, _):
+        for first in range(0, SLOTS_PER_STEP, TABLES):
+            items = []
+            for which, table in enumerate(tables):
+                s = i * SLOTS_PER_STEP + (first + which)
+                r = pl.multiple_of(index_ref[0, s], 2)
+                w = (ya + yb * value_ref[1, 0, s]) * z_hat(pos, value_ref[0, 0, s])
+                near = table[pl.ds(r, 8), :] + w * value_ref[3, 0, s]
+                far = table[pl.ds(r + plane, 8), :] + w * value_ref[4, 0, s]
+                items.append((table, r, near, far))
+            for table, r, near, far in items:
+                table[pl.ds(r, 8), :] = near
+                table[pl.ds(r + plane, 8), :] = far
+        return 0
+
+    lax.fori_loop(0, steps, body, 0)
 
     def combine(i, _):
         part = pl.ds(pl.multiple_of(i * block, block), block)
@@ -261,30 +262,32 @@
     masks = [jnp.where(second_row, 1.0, 0.0).astype(F), jnp.where(second_row, 0.0, 1.0).astype(F)]
     weights = [(ya * mask, yb * mask) for mask in masks]
     plane = 2 * span_y
-    groups, _, capacity = index_ref.shape
     keep = pltpu.make_async_copy(grid, field_ref, sems.at[2])
 
-    for g in range(groups):
-
-        def body(i, _, g=g):
-            for pair in range(SLOTS_PER_STEP // 2):
-                total = None
-                for which in (0, 1):
-                    s = i * SLOTS_PER_STEP + 2 * pair + which
-                    r = pl.multiple_of(index_ref[g, 0, s], 2) + (8 - 4 * which)
-                    wa, wb = weights[which]
-                    w = (wa + wb * value_ref[g, 1, 0, s]) * z_hat(pos, value_ref[g, 0, 0, s])
-                    near, far = table[pl.ds(r, 8), :], table[pl.ds(r + plane, 8), :]
-                    term = w * (near + value_ref[g, 2, 0, s] * (far - near))
-                    total = term if total is None else total + term
-                start = i * (SLOTS_PER_STEP // 2) + (g * (capacity // 2) + pair)
-                parts[pl.ds(pl.multiple_of(start * 8, 8), 8), :] = total
-            return 0
-
-        lax.fori_loop(0, capacity // SLOTS_PER_STEP, body, 0)
-        if g == 0:
+    steps = index_ref.shape[1] // SLOTS_PER_STEP
+
+    def body(i, _):
+        for pair in range(SLOTS_PER_STEP // 2):
+            total = None
+            for which in (0, 1):
+                s = i * SLOTS_PER_STEP + (2 * pair + which)
+                r = pl.multiple_of(index_ref[0, s], 2) + (8 - 4 * which)
+                wa, wb = weights[which]
+                w = (wa + wb * value_ref[1, 0, s]) * z_hat(pos, value_ref[0, 0, s])
+                near, far = table[pl.ds(r, 8), :], table[pl.ds(r + plane, 8), :]
+                term = w * (near + value_ref[2, 0, s] * (far - near))
+                total = term if total is None else total + term
+            start = i * (SLOTS_PER_STEP // 2) + pair
+            parts[pl.ds(pl.multiple_of(start * 8, 8), 8), :] = total
+
+        @pl.when(i == steps // 4)
+        def _():
             hold.wait()
             keep.start()
+
+        return 0
+
+    lax.fori_loop(0, steps, body, 0)
 
     def fold(i, _):
         start = pl.multiple_of(i * 256, 256)
@@ -294,7 +297,7 @@
         sums[pl.ds(pl.multiple_of(i * 64, 64), 64), :] = total
         return 0
 
-    lax.fori_loop(0, groups * capacity // 64, fold, 0)
+    lax.fori_loop(0, sums.shape[0] // 64, fold, 0)
     out_ref[...] = lax.dot_general(
         jnp.ones((8, LANES), F),
         sums[...],
@@ -307,7 +310,7 @@
 
 def sample(index, value, rows_field, grid_field):
     span_y, rows = grid_field.shape[1], rows_field.shape[0]
-    slots = index.shape[0] * index.shape[2]
+    slots = index.shape[1]
     smem, anywhere = pl.BlockSpec(memory_space=pltpu.SMEM), pl.BlockSpec(memory_space=pl.ANY)
     return pl.pallas_call(
         functools.partial(sample_kernel, span_y),
@@ -338,11 +341,32 @@
     return (2.0 * former * latter) * inverse_of(former + latter)
 
 
+def stage_of(axes, sizes, places):
+    number, count = 0, 1
+    for axis in axes:
+        number = number * sizes[axis] + places[axis]
+        count *= sizes[axis]
+    others = []
+    for step in range(1, count):
+        target, source, source_number, rest = {}, {}, 0, step
+        moves = {}
+        for axis in reversed(axes):
+            moves[axis], rest = rest % sizes[axis], rest // sizes[axis]
+        for axis in axes:
+            size, move = sizes[axis], moves[axis]
+            if move:
+                target[axis] = lax.rem(places[axis] + move, size)
+                source[axis] = lax.rem(places[axis] + size - move, size)
+            source_number = source_number * size + source.get(axis, places[axis])
+        others.append((target, source, source_number))
+    return number, others
+
+
 def krylov_kernel(
     sizes,
     b_ref, eps_ref, pot_ref, ion_ref,
     out_ref, rows_ref,
-    e, fx, fy, fz, rd, v0, v1, v2, b, pot, ion,
+    e, fx, fy, fz, rd, v0, v1, v2, b, pot, ion, sums,
     y_send, y_recv, z_send, z_recv, z_in, red,
     sem_in, send_sem, recv_sem, red_send, red_recv, sem_out,
 ):
@@ -352,7 +376,7 @@
     at_first, at_last, odd = lane == 0, lane == LANES - 1, lane % 2 == 1
     chunks = range(0, span_y, CHUNK)
     body_rows = pl.ds(PAD, span_y)
-    vs = (v0, v1, v2)
+    fields = (e, v0, v1, v2)
     part = span_x // 2
     fzm = ion
 
@@ -384,15 +408,13 @@
                 y_recv[k, side, which] = jnp.zeros((span_x, LANES), F)
 
     barrier = pltpu.get_barrier_semaphore()
-    for axis, place, size in zip(AXES, places, sizes):
-        for step in range(1, size):
-            pl.semaphore_signal(
-                barrier, inc=1, device_id={axis: lax.rem(place + step, size)}, device_id_type=MESH
-            )
-    pl.semaphore_wait(barrier, sum(size - 1 for size in sizes))
-
-    def halo_copies(k, field, x_faces, parts):
-        pairs = []
+    stages = [stage_of(axes, dict(zip(AXES, sizes)), dict(zip(AXES, places))) for axes in STAGES]
+    for _, others in stages:
+        for target, _, _ in others:
+            pl.semaphore_signal(barrier, inc=1, device_id=target, device_id_type=MESH)
+
+    def halo_copies(k, x_faces, parts):
+        pairs, field = [], fields[k]
         for n, (axis, place, size) in enumerate(zip(AXES, places, sizes)):
             if size == 1:
                 continue
@@ -403,7 +425,7 @@
                     ends.append((0, src, field.at[0 if side == 0 else span_x + 1, :, body_rows, :]))
                 if n == 1:
                     for which in parts:
-                        rows = pl.ds(which * part, part)
+                        rows = pl.ds(pl.multiple_of(which * part, 8), part)
                         src = y_send.at[k, side, :, rows, :]
                         ends.append((1 + which, src, y_recv.at[k, side, :, rows, :]))
                 if n == 2:
@@ -434,15 +456,21 @@
         for has_target, _, copy in halo_copies(*exchange):
             pl.when(has_target)(copy.wait_send)
 
-    def pack(k, field, which):
+    def eight(body, first):
+        for n in range(8):
+            body(first + n, 0)
+        return 0
+
+    def pack(k, which):
+        field = fields[k]
+
         def rows_of(i, _):
             x = plane_of(i)
             for half in (0, 1):
                 y_send[k, 1, half, pl.ds(i, 1), :] = field[x + 1, half, pl.ds(PAD, 1), :]
-                if k < 3:
-                    y_send[k, 0, half, pl.ds(i, 1), :] = field[
-                        x + 1, half, pl.ds(PAD + span_y - 1, 1), :
-                    ]
+                y_send[k, 0, half, pl.ds(i, 1), :] = field[
+                    x + 1, half, pl.ds(PAD + span_y - 1, 1), :
+                ]
             return 0
 
         def columns_of(i, accs):
@@ -459,23 +487,24 @@
             return tuple(out)
 
         first = which * part
-        lax.fori_loop(first, first + part, rows_of, 0, unroll=8)
+        lax.fori_loop(0, part // 8, lambda n, c: eight(rows_of, first + 8 * n), 0)
         empty = tuple(jnp.zeros((CHUNK, LANES), F) for _ in chunks)
-        accs = lax.fori_loop(first, first + part, columns_of, empty, unroll=8)
+        accs = lax.fori_loop(0, part, lambda n, c: columns_of(first + n, c), empty, unroll=8)
         for t, acc in zip(chunks, accs):
             z_send[k, which, pl.ds(t, CHUNK), :] = acc
 
-    def unpack(k, field, which):
+    def unpack(k, which):
+        field = fields[k]
+
         def rows_of(i, _):
             x = plane_of(i)
             for half in (0, 1):
-                if k < 3:
-                    field[x + 1, half, pl.ds(PAD - 1, 1), :] = y_recv[k, 0, half, pl.ds(i, 1), :]
+                field[x + 1, half, pl.ds(PAD - 1, 1), :] = y_recv[k, 0, half, pl.ds(i, 1), :]
                 field[x + 1, half, pl.ds(PAD + span_y, 1), :] = y_recv[k, 1, half, pl.ds(i, 1), :]
             return 0
 
         first = which * part
-        lax.fori_loop(first, first + part, rows_of, 0, unroll=8)
+        lax.fori_loop(0, part // 8, lambda n, c: eight(rows_of, first + 8 * n), 0)
         for t in chunks:
             rows = pl.ds(t, CHUNK)
             low = pltpu.roll(z_recv[k, 0, which, rows, :], 2, 1)
@@ -492,26 +521,29 @@
         return pltpu.roll(z_in[which, pl.ds(t, CHUNK), :], LANES - 1 - 2 * x, 1)
 
     def both_parts(body, carry, before, after, unroll):
-        for which in (0, 1):
+        def one(which, carry):
             before(which)
             carry = lax.fori_loop(
-                which * part,
-                (which + 1) * part,
-                functools.partial(body, which),
-                carry,
-                unroll=unroll,
+                0, part, lambda n, c: body(which, which * part + n, c), carry, unroll=unroll
             )
             after(which)
-        return carry
+            return carry
+
+        return lax.fori_loop(0, 2, one, carry)
 
     loads[0].wait()
     loads[1].wait()
     for load in loads[2:]:
         load.start()
-    send(0, e, True, ())
-    for which in (0, 1):
-        pack(0, e, which)
-        send(0, e, False, (which,))
+    pl.semaphore_wait(barrier, sum(len(others) for _, others in stages))
+    send(0, True, ())
+
+    def pack_and_send(which, _):
+        pack(0, which)
+        send(0, False, (which,))
+        return 0
+
+    lax.fori_loop(0, 2, pack_and_send, 0)
 
     for load in loads[2:6]:
         load.wait()
@@ -565,31 +597,39 @@
                 total = total + source * value
         return total
 
-    def ready(k, field):
+    def ready(k):
         def before(which):
-            receive(k, field, which == 1, (which,))
-            unpack(k, field, which)
-            if k == 0:
-                x_face(START if which == 0 else 0)
+            @pl.when(which == 1)
+            def _():
+                receive(k, True, ())
+
+            receive(k, False, (which,))
+            unpack(k, which)
 
         return before
 
-    def done(k, field):
+    def ready_faces(which):
+        ready(0)(which)
+        x_face(START * (1 - which))
+
+    def done(k):
         def after(which):
-            if which == 1:
-                send(k, field, True, ())
-            pack(k, field, which)
-            send(k, field, False, (which,))
+            @pl.when(which == 1)
+            def _():
+                send(k, True, ())
+
+            pack(k, which)
+            send(k, False, (which,))
 
         return after
 
     nothing = jnp.zeros((CHUNK, LANES), F)
-    moments = [both_parts(faces, nothing, ready(0, e), done(1, v0), UNROLL_FACES)]
-
-    for k in (0, 1):
-        v, result = vs[k], vs[k + 1]
-
-        def apply(which, i, carry, v=v, result=result):
+    sums[0] = both_parts(faces, nothing, ready_faces, done(1), UNROLL_FACES)
+
+    def stencil(k):
+        v, result = fields[k], fields[k + 1]
+
+        def apply(which, i, carry):
             first, second = carry
             x = plane_of(i)
             for t in chunks:
@@ -612,11 +652,12 @@
                     second = second + image * value
             return first, second
 
-        moments.extend(
-            both_parts(
-                apply, (nothing, nothing), ready(k + 1, v), done(k + 2, result), UNROLL_APPLY
-            )
-        )
+        first, second = both_parts(apply, (nothing, nothing), ready(k), done(k + 1), UNROLL_APPLY)
+        sums[2 * k - 1] = first
+        sums[2 * k] = second
+
+    stencil(1)
+    stencil(2)
 
     def product(which, i, total):
         x = plane_of(i)
@@ -637,43 +678,35 @@
                 total = total + center[half] * image
         return total
 
-    total = both_parts(product, nothing, ready(3, v2), lambda which: None, UNROLL_APPLY)
-    moments.append(2.0 * total)
+    sums[5] = 2.0 * both_parts(product, nothing, ready(3), lambda which: None, UNROLL_APPLY)
 
     row = lax.broadcasted_iota(jnp.int32, (8, LANES), 0)
     mine = jnp.zeros((8, LANES), F)
-    for n, moment in enumerate(moments):
-        folded = jnp.sum(moment, axis=0, keepdims=True)
+    for n in range(6):
+        folded = jnp.sum(sums[n], axis=0, keepdims=True)
         mine = mine + jnp.where(row == n, folded, 0.0)
-    for n, (axis, place, size) in enumerate(zip(AXES, places, sizes)):
-        red[n, place] = mine
-        copies = []
-        for step in range(1, size):
-            target = lax.rem(place + step, size)
-            copy = pltpu.make_async_remote_copy(
-                src_ref=red.at[n, place],
-                dst_ref=red.at[n, place],
+    for n, (number, others) in enumerate(stages):
+        red[n, number] = mine
+
+        def copy_of(step, device, slot, n=n, number=number):
+            return pltpu.make_async_remote_copy(
+                src_ref=red.at[n, number],
+                dst_ref=red.at[n, slot],
                 send_sem=red_send.at[n, step],
                 recv_sem=red_recv.at[n, step],
-                device_id={axis: target},
+                device_id=device,
                 device_id_type=MESH,
             )
+
+        copies = [copy_of(step, target, number) for step, (target, _, _) in enumerate(others)]
+        for copy in copies:
             copy.start()
-            copies.append(copy)
-        for step in range(1, size):
-            source = lax.rem(place + size - step, size)
-            pltpu.make_async_remote_copy(
-                src_ref=red.at[n, place],
-                dst_ref=red.at[n, source],
-                send_sem=red_send.at[n, step],
-                recv_sem=red_recv.at[n, step],
-                device_id={axis: source},
-                device_id_type=MESH,
-            ).wait_recv()
+        for step, (_, source, slot) in enumerate(others):
+            copy_of(step, source, slot).wait_recv()
         for copy in copies:
             copy.wait_send()
         mine = red[n, 0]
-        for other in range(1, size):
+        for other in range(1, len(others) + 1):
             mine = mine + red[n, other]
     totals = jnp.sum(mine, axis=1, keepdims=True)
     m = [totals[n:n + 1] for n in range(6)]
@@ -714,8 +747,8 @@
     stores.append(pltpu.make_async_copy(b, rows_ref, sem_out.at[2]))
     for store in stores:
         store.start()
-    for k, field in enumerate((e, v0, v1, v2)):
-        sent(k, field, True, (0, 1))
+    for k in range(4):
+        sent(k, True, (0, 1))
     for store in stores:
         store.wait()
 
@@ -727,7 +760,7 @@
     plain = pltpu.VMEM((span_x, 2, span_y, LANES), F)
     dma = pltpu.SemaphoreType.DMA
     anywhere = pl.BlockSpec(memory_space=pl.ANY)
-    most = max(sizes)
+    most = max(sizes[1], sizes[0] * sizes[2])
     return pl.pallas_call(
         functools.partial(krylov_kernel, sizes),
         out_shape=(
@@ -746,17 +779,18 @@
             pltpu.VMEM(b.shape, F),
             plain,
             plain,
+            pltpu.VMEM((6, CHUNK, LANES), F),
             pltpu.VMEM((4, 2, 2, span_x, LANES), F),
             pltpu.VMEM((4, 2, 2, span_x, LANES), F),
             pltpu.VMEM((4, 2, span_y, LANES), F),
             pltpu.VMEM((4, 2, 2, span_y, LANES), F),
             pltpu.VMEM((2, span_y, LANES), F),
-            pltpu.VMEM((3, most, 8, LANES), F),
+            pltpu.VMEM((2, most, 8, LANES), F),
             dma((7,)),
             dma((4, 10)),
             dma((4, 10)),
-            dma((3, most)),
-            dma((3, most)),
+            dma((2, most)),
+            dma((2, most)),
             dma((3,)),
         ],
         compiler_params=pltpu.CompilerParams(

time: 103 us -> 95.7 us (0.929)
  Pallas kernels: 100 us -> 93.2 us
    pallas_call x1, Pallas kernels: 17.1 us -> 14 us  [spread(): pl.pallas_call(functools.partial(spread_kernel, span[1]), out_shape=jax.S...]
    pallas_call x1, Pallas kernels: 16.2 us -> 13.6 us  [sample(): pl.pallas_call(functools.partial(sample_kernel, span_y), out_shape=(jax.S...]
    pallas_call x1, Pallas kernels: 52.6 us -> 50.9 us  [krylov(): pl.pallas_call(functools.partial(krylov_kernel, sizes), out_shape=(jax.Sh...]
where the time goes in v4:
time: 95.7 us; the launch traced here: 95.1 us
  Pallas kernels  93.2 us (97%)
  local copies, waits for them, and re-layouts  1.3 us (1%)
    pallas_call x1, Pallas kernels, krylov(): pl.pallas_call(functools.partial(krylov_kernel, sizes), out_shape=(jax.Sh...  50.9 us
    pallas_call x1, Pallas kernels, spread(): pl.pallas_call(functools.partial(spread_kernel, span[1]), out_shape=jax.S...  14 us
    pallas_call x1, Pallas kernels, sample(): pl.pallas_call(functools.partial(sample_kernel, span_y), out_shape=(jax.S...  13.6 us
    pallas_call x1, Pallas kernels, deliver(): pl.pallas_call(functools.partial(deliver_kernel, size, span_y), out_shape...  7.93 us
    pallas_call x1, Pallas kernels, give_back(): pl.pallas_call(functools.partial(give_back_kernel, size), out_shape=jax.S...  6.69 us

profile of v4, /device:TPU:0, one launch (start us, length us, event | category | flops | bytes accessed | tf_op | source)
XLA Modules:
  0.0 95.1 jit_solution(3370121467355237805)
XLA Ops:
  0.6 7.9 %deliver.1 = (s32[1,2048]{1,0:T(1,128)}, f32[5,1,2048]{2,1,0:T(1,128)}) custom-call(f32[1,1,1,2048]{3,2,1,0:T(1,128)} %q_ref.1, f32[3,1,1,1,2048]{4,3,2,1,0:T(1,128)} %f_ref.1, s32[3,1,1,1,2048]{4,3,2,1,0:T(1,128)} %c_ref.1, s32[1,1,1,4]{3,2,1,0:T(1,128)} %count_ref.3), custom_call_target="tpu_custom_call" | custom-call | tf_op jit(solution)/shard_map/deliver/pallas_call | solution.py:113
  8.6 14.0 %spread.1.b_ref = f32[8192,128]{1,0:T(8,128)} custom-call(s32[1,2048]{1,0:T(1,128)} %get-tuple-element.8.index_ref, f32[5,1,2048]{2,1,0:T(1,128)} %get-tuple-element.9.value_ref), custom_call_target="tpu_custom_call" | custom-call | tf_op jit(solution)/shard_map/spread/pallas_call | solution.py:236
  22.6 50.9 %krylov.1 = (f32[64,64,256]{2,1,0:T(8,128)}, f32[8192,128]{1,0:T(8,128)}) custom-call(f32[8192,128]{1,0:T(8,128)} %spread.1.b_ref, f32[64,64,256]{2,1,0:T(8,128)} %eps_ref.1, f32[64,64,256]{2,1,0:T(8,128)} %pot_ref.1, f32[64,64,256]{2,1,0:T(8,128)} %ion_ref.1), custom_call_target="tpu_custom_call" | custom-call | tf_op jit(solution)/shard_map/krylov/pallas_call | solution.py:764
  73.5 13.6 %sample.1 = (f32[64,64,256]{2,1,0:T(8,128)}, f32[1,2048]{1,0:T(1,128)}) custom-call(s32[1,2048]{1,0:T(1,128)} %get-tuple-element.8.index_ref, f32[5,1,2048]{2,1,0:T(1,128)} %get-tuple-element.9.value_ref, f32[8192,128]{1,0:T(8,128)} %get-tuple-element.10.rows_ref, f32[64,64,256]{2,1,0:T(8,128)} %get-tuple-element.11.grid_ref), custom_call_target="tpu_custom_call" | custom-call | tf_op jit(solution)/shard_map/sample/pallas_call | solution.py:315
  87.1 6.7 %give_back.1 = f32[1,1,1,2048]{3,2,1,0:T(1,128)} custom-call(f32[1,2048]{1,0:T(1,128)} %get-tuple-element.13.sampled_ref, s32[1,1,1,4]{3,2,1,0:T(1,128)} %count_ref.3), custom_call_target="tpu_custom_call" | custom-call | tf_op jit(solution)/shard_map/give_back/pallas_call | solution.py:172
  93.8 1.3 %copy.10 = f32[1,1,1,2048]{3,2,1,0:T(1,128)} copy(f32[1,1,1,2048]{3,2,1,0:T(1,128)} %give_back.1) | data formatting | bytes 16384

commit v5 on v4

--- a/solution.py
+++ b/solution.py
@@ -40,16 +40,74 @@
     pl.semaphore_wait(barrier, size - 1)
 
 
+def inverse_of(value):
+    guess = pl.reciprocal(value, approx=True)
+    return guess * (2.0 - value * guess)
+
+
+def plane_of(i, span_x):
+    return lax.rem(i + START, span_x)
+
+
+def pack_columns(first, count, read, lane, chunks, span_x):
+    def columns_of(n, accs):
+        x = plane_of(first + n, span_x)
+        out = []
+        for t, acc in zip(chunks, accs):
+            low, high = read(x, t)
+            ends = jnp.where(lane == 0, low, jnp.where(lane == LANES - 1, high, 0.0))
+            out.append(acc + pltpu.roll(ends, 2 * x, 1))
+        return tuple(out)
+
+    empty = tuple(jnp.zeros((CHUNK, LANES), F) for _ in chunks)
+    return lax.fori_loop(0, count, columns_of, empty, unroll=8)
+
+
 def deliver_kernel(
-    size, span_y, q_ref, f_ref, c_ref, count_ref, index_ref, value_ref, q_out, q_in, f_in, c_in, send_sem, recv_sem
+    sizes,
+    q_ref, f_ref, c_ref, count_ref, eps_ref, pot_ref, ion_ref,
+    index_ref, value_ref, screen_ref, xh_ref, yh_ref, zh_ref,
+    q_out, q_in, f_in, c_in, e, pot, ion, y_send, z_send, zeros,
+    sem_in, sem_out, sem_zero, send_sem, recv_sem, halo_send, halo_recv,
 ):
-    place = lax.axis_index("gz")
+    span_x, span_y, _ = eps_ref.shape
+    size = sizes[2]
+    places = [lax.axis_index(axis) for axis in AXES]
+    place = places[2]
     capacity = q_out.shape[2]
+    lane = lax.broadcasted_iota(jnp.int32, (CHUNK, LANES), 1)
+    chunks = range(0, span_y, CHUNK)
+
+    loads, pieces = [], [pl.ds(n * (span_x // 4), span_x // 4) for n in range(4)]
+    for half in (0, 1):
+        lanes = pl.ds(half * LANES, LANES)
+        loads.append(pltpu.make_async_copy(eps_ref.at[:, :, lanes], e.at[:, half], sem_in.at[half]))
+    for n, piece in enumerate(pieces):
+        for m, (src, dst) in enumerate(((pot_ref, pot), (ion_ref, ion))):
+            for half in (0, 1):
+                lanes = pl.ds(half * LANES, LANES)
+                sem = sem_in.at[2 + 4 * n + 2 * m + half]
+                loads.append(pltpu.make_async_copy(src.at[piece, :, lanes], dst.at[piece, half], sem))
+    for load in loads:
+        load.start()
+
+    barrier = pltpu.get_barrier_semaphore()
+    greeted = 0
+    for axis, own, count in zip(AXES, places, sizes):
+        steps = range(1, count) if axis == "gz" else ((1, count - 1) if count > 1 else ())
+        for step in steps:
+            pl.semaphore_signal(
+                barrier, inc=1, device_id={axis: lax.rem(own + step, count)}, device_id_type=MESH
+            )
+            greeted += 1
+
     slot = lax.broadcasted_iota(jnp.int32, (1, capacity), 1)
     for g in range(size):
         block = pl.ds(g * capacity, capacity)
         q_out[g] = jnp.where(slot < count_ref[0, 0, 0, g], q_ref[0, 0, :, block], 0.0)
-    greet("gz", size)
+    for half in (0, 1):
+        zeros[half] = jnp.zeros((span_y, LANES), F)
+    pl.semaphore_wait(barrier, greeted)
 
     def copies(step, to, source):
         block = pl.ds(pl.multiple_of(to * capacity, capacity), capacity)
@@ -76,6 +134,70 @@
     for copy in out:
         copy.start()
 
+    loads[0].wait()
+    loads[1].wait()
+    halos = []
+    for n, (axis, own, count) in enumerate(zip(AXES, places, sizes)):
+        for side in (0, 1):
+            src = (e.at[span_x - 1 if side == 0 else 0], y_send.at[side], z_send)[n]
+            dst = (xh_ref, yh_ref, zh_ref)[n].at[side]
+            copy = fill = None
+            if count > 1:
+                copy = pltpu.make_async_remote_copy(
+                    src_ref=src,
+                    dst_ref=dst,
+                    send_sem=halo_send.at[n, side],
+                    recv_sem=halo_recv.at[n, side],
+                    device_id={axis: own + 1 if side == 0 else own - 1},
+                    device_id_type=MESH,
+                )
+            above, below = own < count - 1, own > 0
+            fill = pltpu.make_async_copy(zeros.at[0] if n == 2 else zeros, dst, sem_zero.at[n, side])
+            halos.append((n, above if side == 0 else below, below if side == 0 else above, copy, fill))
+
+    def send(axis):
+        for n, has_target, has_source, copy, fill in halos:
+            if n == axis:
+                if copy is not None:
+                    pl.when(has_target)(copy.start)
+                pl.when(jnp.logical_not(has_source))(fill.start)
+
+    send(0)
+
+    def rows_of(n, _):
+        for m in range(8):
+            i = 8 * n + m
+            x = plane_of(i, span_x)
+            for half in (0, 1):
+                y_send[1, half, pl.ds(i, 1), :] = e[x, half, pl.ds(0, 1), :]
+                y_send[0, half, pl.ds(i, 1), :] = e[x, half, pl.ds(span_y - 1, 1), :]
+        return 0
+
+    lax.fori_loop(0, span_x // 8, rows_of, 0)
+    send(1)
+    accs = pack_columns(
+        0, span_x, lambda x, t: [e[x, half, pl.ds(t, CHUNK), :] for half in (0, 1)], lane, chunks, span_x
+    )
+    for t, acc in zip(chunks, accs):
+        z_send[pl.ds(t, CHUNK), :] = acc
+    send(2)
+
+    def screen(x, _):
+        for half in (0, 1):
+            for t in chunks:
+                rows = pl.ds(t, CHUNK)
+                up = jnp.exp(pot[x, half, rows, :])
+                pot[x, half, rows, :] = ion[x, half, rows, :] * (0.5 * (up + inverse_of(up)))
+        return 0
+
+    stores = []
+    for n, piece in enumerate(pieces):
+        for load in loads[2 + 4 * n:6 + 4 * n]:
+            load.wait()
+        lax.fori_loop(n * (span_x // 4), (n + 1) * (span_x // 4), screen, 0, unroll=4)
+        stores.append(pltpu.make_async_copy(pot.at[piece], screen_ref.at[piece], sem_out.at[n]))
+        stores[-1].start()
+
     def work_out(source, q, f, c):
         block = pl.ds(pl.multiple_of(source * capacity, capacity), capacity)
         index_ref[:, block] = (c[0] * span_y + c[1]) * 2
@@ -85,12 +207,12 @@
         value_ref[3, :, block] = q * (1.0 - f[0])
         value_ref[4, :, block] = q * f[0]
 
-    own = pl.ds(pl.multiple_of(place * capacity, capacity), capacity)
+    own_block = pl.ds(pl.multiple_of(place * capacity, capacity), capacity)
     work_out(
         place,
         q_out[place],
-        [f_ref[k, 0, 0, :, own] for k in range(3)],
-        [c_ref[k, 0, 0, :, own] for k in range(3)],
+        [f_ref[k, 0, 0, :, own_block] for k in range(3)],
+        [c_ref[k, 0, 0, :, own_block] for k in range(3)],
     )
     for step in range(1, size):
         source = lax.rem(place + size - step, size)
@@ -102,39 +224,65 @@
             [f_in[source, k] for k in range(3)],
             [c_in[source, k] for k in range(3)],
         )
+    for _, has_target, has_source, copy, fill in halos:
+        if copy is not None:
+            pl.when(has_source)(copy.wait_recv)
+            pl.when(has_target)(copy.wait_send)
+        pl.when(jnp.logical_not(has_source))(fill.wait)
     for copy in out:
         copy.wait_send()
-
-
-def deliver(size, span_y, charge, fraction, corner, count):
+    for store in stores:
+        store.wait()
+
+
+def deliver(sizes, charge, fraction, corner, count, eps, pot, ion):
+    size = sizes[2]
     capacity = charge.shape[3] // size
-    vmem = pl.BlockSpec(memory_space=pltpu.VMEM)
+    span_x, span_y, _ = eps.shape
+    vmem, anywhere = pl.BlockSpec(memory_space=pltpu.VMEM), pl.BlockSpec(memory_space=pl.ANY)
     dma = pltpu.SemaphoreType.DMA
+    plain = (span_x, 2, span_y, LANES)
     return pl.pallas_call(
-        functools.partial(deliver_kernel, size, span_y),
+        functools.partial(deliver_kernel, sizes),
         out_shape=(
             jax.ShapeDtypeStruct((1, size * capacity), jnp.int32),
             jax.ShapeDtypeStruct((5, 1, size * capacity), F),
+            jax.ShapeDtypeStruct(plain, F),
+            jax.ShapeDtypeStruct((2, 2, span_y, LANES), F),
+            jax.ShapeDtypeStruct((2, 2, span_x, LANES), F),
+            jax.ShapeDtypeStruct((2, span_y, LANES), F),
         ),
-        in_specs=[vmem, vmem, vmem, pl.BlockSpec(memory_space=pltpu.SMEM)],
-        out_specs=(vmem, vmem),
+        in_specs=[vmem, vmem, vmem, pl.BlockSpec(memory_space=pltpu.SMEM)] + [anywhere] * 3,
+        out_specs=(vmem, vmem) + (anywhere,) * 4,
         scratch_shapes=[
             pltpu.VMEM((size, 1, capacity), F),
             pltpu.VMEM((size, 1, capacity), F),
             pltpu.VMEM((size, 3, 1, capacity), F),
             pltpu.VMEM((size, 3, 1, capacity), jnp.int32),
+            pltpu.VMEM(plain, F),
+            pltpu.VMEM(plain, F),
+            pltpu.VMEM(plain, F),
+            pltpu.VMEM((2, 2, span_x, LANES), F),
+            pltpu.VMEM((span_y, LANES), F),
+            pltpu.VMEM((2, span_y, LANES), F),
+            dma((18,)),
+            dma((4,)),
+            dma((3, 2)),
             dma((size, 3)),
             dma((size, 3)),
+            dma((3, 2)),
+            dma((3, 2)),
         ],
-        compiler_params=pltpu.CompilerParams(collective_id=1, has_side_effects=True),
+        compiler_params=pltpu.CompilerParams(
+            vmem_limit_bytes=60 << 20, collective_id=1, has_side_effects=True
+        ),
         name="deliver",
-    )(charge, fraction, corner, count)
-
-
-def give_back_kernel(size, sampled_ref, count_ref, out_ref, came, send_sem, recv_sem):
+    )(charge, fraction, corner, count, eps, pot, ion)
+
+
+def give_back_kernel(size, sampled_ref, out_ref, came, send_sem, recv_sem):
     place = lax.axis_index("gz")
     capacity = came.shape[2]
-    slot = lax.broadcasted_iota(jnp.int32, (1, capacity), 1)
     greet("gz", size)
 
     def copy_of(step, to, source):
@@ -154,7 +302,7 @@
 
     def put(source, values):
         block = pl.ds(pl.multiple_of(source * capacity, capacity), capacity)
-        out_ref[0, 0, :, block] = jnp.where(slot < count_ref[0, 0, 0, source], values, 0.0)
+        out_ref[:, block] = values
 
     put(place, sampled_ref[:, pl.ds(pl.multiple_of(place * capacity, capacity), capacity)])
     for step in range(1, size):
@@ -165,19 +313,19 @@
         copy.wait_send()
 
 
-def give_back(size, sampled, count):
+def give_back(size, sampled):
     slots = sampled.shape[1]
     vmem = pl.BlockSpec(memory_space=pltpu.VMEM)
     dma = pltpu.SemaphoreType.DMA
     return pl.pallas_call(
         functools.partial(give_back_kernel, size),
-        out_shape=jax.ShapeDtypeStruct((1, 1, 1, slots), F),
-        in_specs=[vmem, pl.BlockSpec(memory_space=pltpu.SMEM)],
+        out_shape=jax.ShapeDtypeStruct((1, slots), F),
+        in_specs=[vmem],
         out_specs=vmem,
         scratch_shapes=[pltpu.VMEM((size, 1, slots // size), F), dma((size,)), dma((size,))],
         compiler_params=pltpu.CompilerParams(collective_id=2, has_side_effects=True),
         name="give_back",
-    )(sampled, count)
+    )(sampled)
 
 
 def spread_kernel(span_y, index_ref, value_ref, out_ref, *scratch):
@@ -225,10 +373,14 @@
         tables[0][part, :] = total
         return 0
 
-    lax.fori_loop(0, rows // block, combine, 0)
-    copy = pltpu.make_async_copy(tables[0].at[pl.ds(0, rows), :], out_ref, sem)
-    copy.start()
-    copy.wait()
+    pieces, copies = rows // block // 4, []
+    for n in range(4):
+        lax.fori_loop(n * pieces, (n + 1) * pieces, combine, 0, unroll=2)
+        part = pl.ds(n * pieces * block, pieces * block)
+        copies.append(pltpu.make_async_copy(tables[0].at[part, :], out_ref.at[part, :], sem.at[n]))
+        copies[-1].start()
+    for copy in copies:
+        copy.wait()
 
 
 def spread(index, value, span):
@@ -238,14 +390,14 @@
         out_shape=jax.ShapeDtypeStruct((rows, LANES), F),
         in_specs=[pl.BlockSpec(memory_space=pltpu.SMEM)] * 2,
         out_specs=pl.BlockSpec(memory_space=pl.ANY),
-        scratch_shapes=[pltpu.VMEM((rows + 8, LANES), F)] * TABLES + [pltpu.SemaphoreType.DMA(())],
-        compiler_params=pltpu.CompilerParams(vmem_limit_bytes=56 << 20),
+        scratch_shapes=[pltpu.VMEM((rows + 8, LANES), F)] * TABLES + [pltpu.SemaphoreType.DMA((4,))],
+        compiler_params=pltpu.CompilerParams(vmem_limit_bytes=60 << 20),
         name="spread",
     )(index, value)
 
 
 def sample_kernel(
-    span_y, index_ref, value_ref, rows_ref, grid_ref, field_ref, out_ref, table, grid, parts, sums, sems
+    span_y, index_ref, value_ref, rows_ref, field_ref, out_ref, table, grid, parts, sums, sems
 ):
     rows = rows_ref.shape[0]
     load = pltpu.make_async_copy(rows_ref, table.at[pl.ds(8, rows), :], sems.at[1])
@@ -253,8 +405,6 @@
     table[pl.ds(0, 8), :] = jnp.zeros((8, LANES), F)
     table[pl.ds(rows + 8, 8), :] = jnp.zeros((8, LANES), F)
     load.wait()
-    hold = pltpu.make_async_copy(grid_ref, grid, sems.at[0])
-    hold.start()
     row, pos = patterns()
     first_row, second_row = row % 4 < 2, row < 4
     yb = jnp.where(first_row, -1.0, 1.0).astype(F)
@@ -262,7 +412,10 @@
     masks = [jnp.where(second_row, 1.0, 0.0).astype(F), jnp.where(second_row, 0.0, 1.0).astype(F)]
     weights = [(ya * mask, yb * mask) for mask in masks]
     plane = 2 * span_y
-    keep = pltpu.make_async_copy(grid, field_ref, sems.at[2])
+    span_x = grid.shape[0]
+    turn = span_x // (index_ref.shape[1] // SLOTS_PER_STEP)
+    halves = [pl.ds(n * (span_x // 2), span_x // 2) for n in (0, 1)]
+    keeps = [pltpu.make_async_copy(grid.at[h], field_ref.at[h], sems.at[2 * n]) for n, h in enumerate(halves)]
 
     steps = index_ref.shape[1] // SLOTS_PER_STEP
 
@@ -280,14 +433,21 @@
             start = i * (SLOTS_PER_STEP // 2) + pair
             parts[pl.ds(pl.multiple_of(start * 8, 8), 8), :] = total
 
-        @pl.when(i == steps // 4)
+        for n in range(turn):
+            x = i * turn + n
+            for half in (0, 1):
+                for t in range(0, span_y, CHUNK):
+                    place = pl.ds(8 + x * plane + 2 * t + half, CHUNK, stride=2)
+                    grid[x, pl.ds(t, CHUNK), half * LANES:(half + 1) * LANES] = table[place, :]
+
+        @pl.when(i == steps // 2)
         def _():
-            hold.wait()
-            keep.start()
+            keeps[0].start()
 
         return 0
 
     lax.fori_loop(0, steps, body, 0)
+    keeps[1].start()
 
     def fold(i, _):
         start = pl.multiple_of(i * 256, 256)
@@ -305,36 +465,32 @@
         precision=lax.Precision.HIGHEST,
         preferred_element_type=F,
     )[0:1]
-    keep.wait()
-
-
-def sample(index, value, rows_field, grid_field):
-    span_y, rows = grid_field.shape[1], rows_field.shape[0]
+    for keep in keeps:
+        keep.wait()
+
+
+def sample(index, value, rows_field, span):
+    span_y, rows = span[1], rows_field.shape[0]
     slots = index.shape[1]
     smem, anywhere = pl.BlockSpec(memory_space=pltpu.SMEM), pl.BlockSpec(memory_space=pl.ANY)
     return pl.pallas_call(
         functools.partial(sample_kernel, span_y),
         out_shape=(
-            jax.ShapeDtypeStruct(grid_field.shape, F),
+            jax.ShapeDtypeStruct(span, F),
             jax.ShapeDtypeStruct((1, slots), F),
         ),
-        in_specs=[smem, smem, anywhere, anywhere],
+        in_specs=[smem, smem, anywhere],
         out_specs=(anywhere, pl.BlockSpec(memory_space=pltpu.VMEM)),
         scratch_shapes=[
             pltpu.VMEM((rows + 16, LANES), F),
-            pltpu.VMEM(grid_field.shape, F),
+            pltpu.VMEM(span, F),
             pltpu.VMEM((slots * 4, LANES), F),
             pltpu.VMEM((slots, LANES), F),
             pltpu.SemaphoreType.DMA((3,)),
         ],
-        compiler_params=pltpu.CompilerParams(vmem_limit_bytes=56 << 20),
+        compiler_params=pltpu.CompilerParams(vmem_limit_bytes=60 << 20),
         name="sample",
-    )(index, value, rows_field, grid_field)
-
-
-def inverse_of(value):
-    guess = pl.reciprocal(value, approx=True)
-    return guess * (2.0 - value * guess)
+    )(index, value, rows_field)
 
 
 def harmonic(former, latter):
@@ -364,9 +520,9 @@
 
 def krylov_kernel(
     sizes,
-    b_ref, eps_ref, pot_ref, ion_ref,
-    out_ref, rows_ref,
-    e, fx, fy, fz, rd, v0, v1, v2, b, pot, ion, sums,
+    b_ref, eps_ref, screen_ref, xh_ref, yh_ref, zh_ref,
+    rows_ref,
+    e, fx, fy, fz, fzm, rd, v0, v1, v2, b, sums,
     y_send, y_recv, z_send, z_recv, z_in, red,
     sem_in, send_sem, recv_sem, red_send, red_recv, sem_out,
 ):
@@ -378,30 +534,62 @@
     body_rows = pl.ds(PAD, span_y)
     fields = (e, v0, v1, v2)
     part = span_x // 2
-    fzm = ion
-
-    def plane_of(i):
-        return lax.rem(i + START, span_x)
-
+
+    def load_planes(src, dst, number, first, count, shift):
+        out = []
+        for start, many in ((first, min(count, span_x - first)), (0, count - min(count, span_x - first))):
+            if many:
+                out.append((src(start, many), dst(start + shift, many)))
+        return [pltpu.make_async_copy(a, b, sem_in.at[number + n]) for n, (a, b) in enumerate(out)]
+
+    tall = 2 * span_y
     loads = []
-    for n, (src, dst) in enumerate(((eps_ref, e), (pot_ref, pot), (ion_ref, ion))):
+    for which in (0, 1):
+        group = []
         for half in (0, 1):
-            place = dst.at[pl.ds(1, span_x), half, body_rows, :] if n == 0 else dst.at[:, half]
-            loads.append(
-                pltpu.make_async_copy(
-                    src.at[:, :, pl.ds(half * LANES, LANES)], place, sem_in.at[2 * n + half]
+            group += load_planes(
+                lambda a, m: eps_ref.at[pl.ds(a, m), :, pl.ds(half * LANES, LANES)],
+                lambda a, m: e.at[pl.ds(a, m), half, body_rows, :],
+                12 * which + 2 * half,
+                START - 1 if which == 0 else START + part + 1,
+                part + 2 if which == 0 else part - 2,
+                1,
+            )
+        group += load_planes(
+            lambda a, m: screen_ref.at[pl.ds(a, m)],
+            lambda a, m: rd.at[pl.ds(a, m)],
+            12 * which + 4,
+            START + part * which,
+            part,
+            0,
+        )
+        group += load_planes(
+            lambda a, m: b_ref.at[pl.ds(a * tall, m * tall), :],
+            lambda a, m: b.at[pl.ds(a * tall, m * tall), :],
+            12 * which + 6,
+            START + part * which,
+            part,
+            0,
+        )
+        if which == 0:
+            group.append(pltpu.make_async_copy(yh_ref, y_recv.at[0], sem_in.at[8]))
+            group.append(pltpu.make_async_copy(zh_ref, z_recv.at[0, :, 0], sem_in.at[9]))
+            for side in (0, 1):
+                x = span_x + 1 if side else 0
+                group.append(
+                    pltpu.make_async_copy(xh_ref.at[side], e.at[x, :, body_rows, :], sem_in.at[10 + side])
                 )
-            )
-    loads.append(pltpu.make_async_copy(b_ref, b, sem_in.at[6]))
-    loads[0].start()
-    loads[1].start()
+        loads.append(group)
+    for group in loads:
+        for load in group:
+            load.start()
 
     zero = jnp.zeros((span_y, LANES), F)
-    for field in (e, v0, v1, v2):
+    for field in (v0, v1, v2):
         for half in (0, 1):
             for x in (0, span_x + 1):
                 field[x, half, body_rows, :] = zero
-    for k in range(4):
+    for k in range(1, 4):
         for side in (0, 1):
             for which in (0, 1):
                 z_recv[k, side, which] = zero
@@ -465,7 +653,7 @@
         field = fields[k]
 
         def rows_of(i, _):
-            x = plane_of(i)
+            x = plane_of(i, span_x)
             for half in (0, 1):
                 y_send[k, 1, half, pl.ds(i, 1), :] = field[x + 1, half, pl.ds(PAD, 1), :]
                 y_send[k, 0, half, pl.ds(i, 1), :] = field[
@@ -473,23 +661,16 @@
                 ]
             return 0
 
-        def columns_of(i, accs):
-            x = plane_of(i)
-            out = []
-            for t, acc in zip(chunks, accs):
-                rows = pl.ds(PAD + t, CHUNK)
-                ends = jnp.where(
-                    at_first,
-                    field[x + 1, 0, rows, :],
-                    jnp.where(at_last, field[x + 1, 1, rows, :], 0.0),
-                )
-                out.append(acc + pltpu.roll(ends, 2 * x, 1))
-            return tuple(out)
-
         first = which * part
         lax.fori_loop(0, part // 8, lambda n, c: eight(rows_of, first + 8 * n), 0)
-        empty = tuple(jnp.zeros((CHUNK, LANES), F) for _ in chunks)
-        accs = lax.fori_loop(0, part, lambda n, c: columns_of(first + n, c), empty, unroll=8)
+        accs = pack_columns(
+            first,
+            part,
+            lambda x, t: [field[x + 1, half, pl.ds(PAD + t, CHUNK), :] for half in (0, 1)],
+            lane,
+            chunks,
+            span_x,
+        )
         for t, acc in zip(chunks, accs):
             z_send[k, which, pl.ds(t, CHUNK), :] = acc
 
@@ -497,7 +678,7 @@
         field = fields[k]
 
         def rows_of(i, _):
-            x = plane_of(i)
+            x = plane_of(i, span_x)
             for half in (0, 1):
                 field[x + 1, half, pl.ds(PAD - 1, 1), :] = y_recv[k, 0, half, pl.ds(i, 1), :]
                 field[x + 1, half, pl.ds(PAD + span_y, 1), :] = y_recv[k, 1, half, pl.ds(i, 1), :]
@@ -507,8 +688,9 @@
         lax.fori_loop(0, part // 8, lambda n, c: eight(rows_of, first + 8 * n), 0)
         for t in chunks:
             rows = pl.ds(t, CHUNK)
-            low = pltpu.roll(z_recv[k, 0, which, rows, :], 2, 1)
-            z_in[which, rows, :] = jnp.where(odd, low, z_recv[k, 1, which, rows, :])
+            held = which if k > 0 else 0
+            low = pltpu.roll(z_recv[k, 0, held, rows, :], 2, 1)
+            z_in[which, rows, :] = jnp.where(odd, low, z_recv[k, 1, held, rows, :])
 
     def z_neighbours(center, outer):
         after = [pltpu.roll(c, LANES - 1, 1) for c in center]
@@ -531,34 +713,6 @@
 
         return lax.fori_loop(0, 2, one, carry)
 
-    loads[0].wait()
-    loads[1].wait()
-    for load in loads[2:]:
-        load.start()
-    pl.semaphore_wait(barrier, sum(len(others) for _, others in stages))
-    send(0, True, ())
-
-    def pack_and_send(which, _):
-        pack(0, which)
-        send(0, False, (which,))
-        return 0
-
-    lax.fori_loop(0, 2, pack_and_send, 0)
-
-    for load in loads[2:6]:
-        load.wait()
-
-    def screen(x, _):
-        for half in (0, 1):
-            for t in chunks:
-                rows = pl.ds(t, CHUNK)
-                up = jnp.exp(pot[x, half, rows, :])
-                rd[x, half, rows, :] = ion[x, half, rows, :] * (0.5 * (up + inverse_of(up)))
-        return 0
-
-    lax.fori_loop(0, span_x, screen, 0, unroll=2)
-    loads[6].wait()
-
     def x_face(x):
         for half in (0, 1):
             for t in chunks:
@@ -566,7 +720,7 @@
                 fx[x, half, pl.ds(t, CHUNK), :] = harmonic(e[x, half, rows, :], e[x + 1, half, rows, :])
 
     def faces(which, i, total):
-        x = plane_of(i)
+        x = plane_of(i, span_x)
         for half in (0, 1):
             fy[x, half, pl.ds(PAD - 1, 1), :] = harmonic(
                 e[x + 1, half, pl.ds(PAD - 1, 1), :], e[x + 1, half, pl.ds(PAD, 1), :]
@@ -609,11 +763,24 @@
         return before
 
     def ready_faces(which):
-        ready(0)(which)
+        for n in (0, 1):
+
+            @pl.when(which == n)
+            def _():
+                for load in loads[n]:
+                    load.wait()
+
+        unpack(0, which)
         x_face(START * (1 - which))
 
     def done(k):
         def after(which):
+            if k == 1:
+
+                @pl.when(which == 0)
+                def _():
+                    pl.semaphore_wait(barrier, sum(len(others) for _, others in stages))
+
             @pl.when(which == 1)
             def _():
                 send(k, True, ())
@@ -631,7 +798,7 @@
 
         def apply(which, i, carry):
             first, second = carry
-            x = plane_of(i)
+            x = plane_of(i, span_x)
             for t in chunks:
                 rows, wide = pl.ds(t, CHUNK), pl.ds(PAD + t, CHUNK)
                 up, down = pl.ds(PAD + t + 1, CHUNK), pl.ds(PAD + t - 1, CHUNK)
@@ -660,7 +827,7 @@
     stencil(2)
 
     def product(which, i, total):
-        x = plane_of(i)
+        x = plane_of(i, span_x)
         for t in chunks:
             rows, wide = pl.ds(t, CHUNK), pl.ds(PAD + t, CHUNK)
             center = [v2[x + 1, half, wide, :] for half in (0, 1)]
@@ -733,27 +900,22 @@
                 value = weights[0] * v0[x + 1, half, wide, :]
                 value = value + weights[1] * v1[x + 1, half, wide, :]
                 value = value + weights[2] * v2[x + 1, half, wide, :]
-                pot[x, half, pl.ds(t, CHUNK), :] = value
                 b[pl.ds(x * (2 * span_y) + 2 * t + half, CHUNK, stride=2), :] = value
         return 0
 
-    lax.fori_loop(0, span_x, finish, 0, unroll=2)
-    stores = [
-        pltpu.make_async_copy(
-            pot.at[:, half], out_ref.at[:, :, pl.ds(half * LANES, LANES)], sem_out.at[half]
-        )
-        for half in (0, 1)
-    ]
-    stores.append(pltpu.make_async_copy(b, rows_ref, sem_out.at[2]))
-    for store in stores:
-        store.start()
-    for k in range(4):
+    stores, some = [], span_x // 4
+    for n in range(4):
+        lax.fori_loop(n * some, (n + 1) * some, finish, 0, unroll=2)
+        rows = pl.ds(n * some * tall, some * tall)
+        stores.append(pltpu.make_async_copy(b.at[rows, :], rows_ref.at[rows, :], sem_out.at[n]))
+        stores[-1].start()
+    for k in range(1, 4):
         sent(k, True, (0, 1))
     for store in stores:
         store.wait()
 
 
-def krylov(sizes, b, eps, pot, ion):
+def krylov(sizes, b, eps, screen, x_halo, y_halo, z_halo):
     span_x, span_y, span_z = eps.shape
     tall = span_y + 2 * PAD
     padded = pltpu.VMEM((span_x + 2, 2, tall, LANES), F)
@@ -763,22 +925,18 @@
     most = max(sizes[1], sizes[0] * sizes[2])
     return pl.pallas_call(
         functools.partial(krylov_kernel, sizes),
-        out_shape=(
-            jax.ShapeDtypeStruct(eps.shape, F),
-            jax.ShapeDtypeStruct(b.shape, F),
-        ),
-        in_specs=[anywhere] * 4,
-        out_specs=(anywhere, anywhere),
+        out_shape=jax.ShapeDtypeStruct(b.shape, F),
+        in_specs=[anywhere] * 6,
+        out_specs=anywhere,
         scratch_shapes=[
             padded,
             pltpu.VMEM((span_x + 1, 2, span_y, LANES), F),
             pltpu.VMEM((span_x, 2, tall, LANES), F),
             plain,
             plain,
+            plain,
             padded, padded, padded,
             pltpu.VMEM(b.shape, F),
-            plain,
-            plain,
             pltpu.VMEM((6, CHUNK, LANES), F),
             pltpu.VMEM((4, 2, 2, span_x, LANES), F),
             pltpu.VMEM((4, 2, 2, span_x, LANES), F),
@@ -786,31 +944,37 @@
             pltpu.VMEM((4, 2, 2, span_y, LANES), F),
             pltpu.VMEM((2, span_y, LANES), F),
             pltpu.VMEM((2, most, 8, LANES), F),
-            dma((7,)),
+            dma((24,)),
             dma((4, 10)),
             dma((4, 10)),
             dma((2, most)),
             dma((2, most)),
-            dma((3,)),
+            dma((4,)),
         ],
         compiler_params=pltpu.CompilerParams(
             vmem_limit_bytes=60 << 20, collective_id=0, has_side_effects=True
         ),
         name="krylov",
-    )(b, eps, pot, ion)
+    )(b, eps, screen, x_halo, y_halo, z_halo)
 
 
 def per_device(
     atom_charge, atom_fraction, atom_corner, block_count, permittivity, base_potential, ion_access
 ):
     sizes = tuple(lax.axis_size(axis) for axis in AXES)
-    index, value = deliver(
-        sizes[2], permittivity.shape[1], atom_charge, atom_fraction, atom_corner, block_count
+    slots = atom_charge.shape[3]
+    index, value, screen, *halos = deliver(
+        sizes,
+        atom_charge, atom_fraction, atom_corner, block_count,
+        permittivity, base_potential, ion_access,
     )
     sources = spread(index, value, permittivity.shape)
-    grid_field, rows_field = krylov(sizes, sources, permittivity, base_potential, ion_access)
-    solution_field, sampled = sample(index, value, rows_field, grid_field)
-    return solution_field, give_back(sizes[2], sampled, block_count)
+    rows_field = krylov(sizes, sources, permittivity, screen, *halos)
+    solution_field, sampled = sample(index, value, rows_field, permittivity.shape)
+    returned = give_back(sizes[2], sampled).reshape(sizes[2], -1)
+    slot = lax.broadcasted_iota(jnp.int32, returned.shape, 1)
+    live = slot < block_count.reshape(sizes[2], 1)
+    return solution_field, jnp.where(live, returned, 0.0).reshape(1, 1, 1, slots)
 
 
 def solution(mesh):

time: 95.7 us -> 90.1 us (0.941)
  Pallas kernels: 93.2 us -> 87.5 us
  other arithmetic: 0 us -> 1.38 us
  local copies, waits for them, and re-layouts: 1.3 us -> 0.02 us
    pallas_call x2, Pallas kernels: 58.9 us -> 53.8 us  [the longest x1 42.5 us: krylov(): pl.pallas_call(functools.partial(krylov_kernel, sizes), out_shape=jax.Sha...]
    select_n x0 -> x1, other arithmetic: none -> 1.31 us  [per_device(): jnp.where(live, returned, 0.0).reshape(1, 1, 1, slots)]
    unnamed x1 -> x2, local copies, waits for them, and re-layouts: 1.3 us -> 0.01 us
where the time goes in v5:
time: 90.1 us; the launch traced here: 89.5 us
  Pallas kernels  87.5 us (97%)
  other arithmetic  1.38 us (2%)
    pallas_call x1, Pallas kernels, krylov(): pl.pallas_call(functools.partial(krylov_kernel, sizes), out_shape=jax.Sha...  42.5 us
    pallas_call x1, Pallas kernels, sample(): pl.pallas_call(functools.partial(sample_kernel, span_y), out_shape=(jax.S...  13.6 us
    pallas_call x1, Pallas kernels, spread(): pl.pallas_call(functools.partial(spread_kernel, span[1]), out_shape=jax.S...  13.5 us
    pallas_call x1, Pallas kernels, deliver(): pl.pallas_call(functools.partial(deliver_kernel, sizes), out_shape=(jax.S...  11.3 us
    pallas_call x1, Pallas kernels, give_back(): pl.pallas_call(functools.partial(give_back_kernel, size), out_shape=jax.S...  6.55 us

profile of v5, /device:TPU:0, one launch (start us, length us, event | category | flops | bytes accessed | tf_op | source)
XLA Modules:
  0.0 89.5 jit_solution(7338266887733940856)
XLA Ops:
  0.6 11.3 %deliver.1 = (s32[1,2048]{1,0:T(1,128)}, f32[5,1,2048]{2,1,0:T(1,128)}, f32[64,2,64,128]{3,2,1,0:T(8,128)}, f32[2,2,64,128]{3,2,1,0:T(8,128)}, f32[2,2,64,128]{3,2,1,0:T(8,128)}, /*index=5*/f32[2,64,128]{2,1,0:T(8,128)}) custom-call(f32[1,1,1,2048]{3,2,1,0:T(1,128)} %q_ref.1, f32[3,1,1,1,2048]{4,3,2,1,0:T(1,128)} %f_ref.1, s32[3,1,1,1,2048]{4,3,2,1,0:T(1,128)} %c_ref.1, ...), custom_call_target="tpu_custom_call" | custom-call | tf_op jit(solution)/shard_map/deliver/pallas_call | solution.py:245
  12.0 13.5 %spread.1.b_ref = f32[8192,128]{1,0:T(8,128)} custom-call(s32[1,2048]{1,0:T(1,128)} %get-tuple-element.10.index_ref, f32[5,1,2048]{2,1,0:T(1,128)} %get-tuple-element.11.value_ref), custom_call_target="tpu_custom_call" | custom-call | tf_op jit(solution)/shard_map/spread/pallas_call | solution.py:388
  25.4 42.5 %krylov.1.rows_ref = f32[8192,128]{1,0:T(8,128)} custom-call(f32[8192,128]{1,0:T(8,128)} %spread.1.b_ref, f32[64,64,256]{2,1,0:T(8,128)} %eps_ref.3, f32[64,2,64,128]{3,2,1,0:T(8,128)} %get-tuple-element.12.screen_ref, f32[2,2,64,128]{3,2,1,0:T(8,128)} %get-tuple-element.13.xh_ref, f32[2,2,64,128]{3,2,1,0:T(8,128)} %get-tuple-element.14.yh_ref, ...), custom_call_target="tpu_custom_call" | custom-call | tf_op jit(solution)/shard_map/krylov/pallas_call | solution.py:926
  67.9 0.0 copy-start
  67.9 13.6 %sample.1 = (f32[64,64,256]{2,1,0:T(8,128)}, f32[1,2048]{1,0:T(1,128)}) custom-call(s32[1,2048]{1,0:T(1,128)} %get-tuple-element.10.index_ref, f32[5,1,2048]{2,1,0:T(1,128)} %get-tuple-element.11.value_ref, f32[8192,128]{1,0:T(8,128)} %krylov.1.rows_ref), custom_call_target="tpu_custom_call" | custom-call | tf_op jit(solution)/shard_map/sample/pallas_call | solution.py:476
  81.6 6.6 %give_back.1 = f32[1,2048]{1,0:T(1,128)} custom-call(f32[1,2048]{1,0:T(1,128)} %get-tuple-element.17.sampled_ref), custom_call_target="tpu_custom_call" | custom-call | tf_op jit(solution)/shard_map/give_back/pallas_call | solution.py:320
  88.1 0.0 copy-done
  88.1 0.1 iota_compare_fusion
  88.2 1.3 %bitcast_select_fusion = f32[1,1,1,2048]{3,2,1,0:T(1,128)} fusion(pred[1,1,1,2048]{3,2,1,0:T(4,128)(4,1)S(1)} %lt.23, f32[1,2048]{1,0:T(1,128)} %give_back.1), kind=kLoop, calls=%fused_computation | loop fusion | flops 2048 | bytes 18432 | tf_op jit(solution)/shard_map/jit(_where)/select_n | solution.py:977
  (1 shorter events, 0.0 us)
Async XLA Ops:
  67.9 20.2 %copy-start = (s32[1,1,1,4]{3,2,1,0:T(1,128)S(1)}, s32[1,1,1,4]{3,2,1,0:T(1,128)}, u32[]{:S(2)}) copy-start(s32[1,1,1,4]{3,2,1,0:T(1,128)} %count_ref.1) | copy-start | bytes 52

commit v6 on v5

--- a/solution.py
+++ b/solution.py
@@ -14,11 +14,12 @@
 LANES = 128
 PAD = 8
 CHUNK = 16
-SLOTS_PER_STEP = 32
+SLOTS_PER_STEP = 64
 TABLES = 2
 START = 8
-UNROLL_FACES = 4
-UNROLL_APPLY = 8
+PARTS = 4
+UNROLL_FACES = 8
+UNROLL_APPLY = 16
 
 
 def patterns():
@@ -66,7 +67,7 @@
 def deliver_kernel(
     sizes,
     q_ref, f_ref, c_ref, count_ref, eps_ref, pot_ref, ion_ref,
-    index_ref, value_ref, screen_ref, xh_ref, yh_ref, zh_ref,
+    index_ref, value_ref, live_ref, screen_ref, xh_ref, yh_ref, zh_ref,
     q_out, q_in, f_in, c_in, e, pot, ion, y_send, z_send, zeros,
     sem_in, sem_out, sem_zero, send_sem, recv_sem, halo_send, halo_recv,
 ):
@@ -104,7 +105,9 @@
     slot = lax.broadcasted_iota(jnp.int32, (1, capacity), 1)
     for g in range(size):
         block = pl.ds(g * capacity, capacity)
-        q_out[g] = jnp.where(slot < count_ref[0, 0, 0, g], q_ref[0, 0, :, block], 0.0)
+        live = slot < count_ref[0, 0, 0, g]
+        live_ref[:, block] = jnp.where(live, 1.0, 0.0)
+        q_out[g] = jnp.where(live, q_ref[0, 0, :, block], 0.0)
     for half in (0, 1):
         zeros[half] = jnp.zeros((span_y, LANES), F)
     pl.semaphore_wait(barrier, greeted)
@@ -247,13 +250,14 @@
         out_shape=(
             jax.ShapeDtypeStruct((1, size * capacity), jnp.int32),
             jax.ShapeDtypeStruct((5, 1, size * capacity), F),
+            jax.ShapeDtypeStruct((1, size * capacity), F),
             jax.ShapeDtypeStruct(plain, F),
             jax.ShapeDtypeStruct((2, 2, span_y, LANES), F),
             jax.ShapeDtypeStruct((2, 2, span_x, LANES), F),
             jax.ShapeDtypeStruct((2, span_y, LANES), F),
         ),
         in_specs=[vmem, vmem, vmem, pl.BlockSpec(memory_space=pltpu.SMEM)] + [anywhere] * 3,
-        out_specs=(vmem, vmem) + (anywhere,) * 4,
+        out_specs=(vmem,) * 3 + (anywhere,) * 4,
         scratch_shapes=[
             pltpu.VMEM((size, 1, capacity), F),
             pltpu.VMEM((size, 1, capacity), F),
@@ -533,7 +537,7 @@
     chunks = range(0, span_y, CHUNK)
     body_rows = pl.ds(PAD, span_y)
     fields = (e, v0, v1, v2)
-    part = span_x // 2
+    part = span_x // PARTS
 
     def load_planes(src, dst, number, first, count, shift):
         out = []
@@ -544,21 +548,22 @@
 
     tall = 2 * span_y
     loads = []
-    for which in (0, 1):
-        group = []
+    for which in range(PARTS):
+        group, base = [], 8 * which
+        last = which == PARTS - 1
         for half in (0, 1):
             group += load_planes(
                 lambda a, m: eps_ref.at[pl.ds(a, m), :, pl.ds(half * LANES, LANES)],
                 lambda a, m: e.at[pl.ds(a, m), half, body_rows, :],
-                12 * which + 2 * half,
-                START - 1 if which == 0 else START + part + 1,
-                part + 2 if which == 0 else part - 2,
+                base + 2 * half,
+                START - 1 if which == 0 else START + part * which + 1,
+                part + (2 if which == 0 else -2 if last else 0),
                 1,
             )
         group += load_planes(
             lambda a, m: screen_ref.at[pl.ds(a, m)],
             lambda a, m: rd.at[pl.ds(a, m)],
-            12 * which + 4,
+            base + 4,
             START + part * which,
             part,
             0,
@@ -566,18 +571,18 @@
         group += load_planes(
             lambda a, m: b_ref.at[pl.ds(a * tall, m * tall), :],
             lambda a, m: b.at[pl.ds(a * tall, m * tall), :],
-            12 * which + 6,
+            base + 6,
             START + part * which,
             part,
             0,
         )
         if which == 0:
-            group.append(pltpu.make_async_copy(yh_ref, y_recv.at[0], sem_in.at[8]))
-            group.append(pltpu.make_async_copy(zh_ref, z_recv.at[0, :, 0], sem_in.at[9]))
+            group.append(pltpu.make_async_copy(yh_ref, y_recv.at[0], sem_in.at[8 * PARTS]))
+            group.append(pltpu.make_async_copy(zh_ref, z_recv.at[0, :, 0], sem_in.at[8 * PARTS + 1]))
             for side in (0, 1):
                 x = span_x + 1 if side else 0
                 group.append(
-                    pltpu.make_async_copy(xh_ref.at[side], e.at[x, :, body_rows, :], sem_in.at[10 + side])
+                    pltpu.make_async_copy(xh_ref.at[side], e.at[x, :, body_rows, :], sem_in.at[8 * PARTS + 2 + side])
                 )
         loads.append(group)
     for group in loads:
@@ -591,9 +596,10 @@
                 field[x, half, body_rows, :] = zero
     for k in range(1, 4):
         for side in (0, 1):
-            for which in (0, 1):
+            for which in range(PARTS):
                 z_recv[k, side, which] = zero
-                y_recv[k, side, which] = jnp.zeros((span_x, LANES), F)
+            for half in (0, 1):
+                y_recv[k, side, half] = jnp.zeros((span_x, LANES), F)
 
     barrier = pltpu.get_barrier_semaphore()
     stages = [stage_of(axes, dict(zip(AXES, sizes)), dict(zip(AXES, places))) for axes in STAGES]
@@ -618,7 +624,7 @@
                         ends.append((1 + which, src, y_recv.at[k, side, :, rows, :]))
                 if n == 2:
                     for which in parts:
-                        ends.append((3 + which, z_send.at[k, which], z_recv.at[k, side, which]))
+                        ends.append((1 + PARTS + which, z_send.at[k, which], z_recv.at[k, side, which]))
                 for kind, src, dst in ends:
                     copy = pltpu.make_async_remote_copy(
                         src_ref=src,
@@ -711,7 +717,7 @@
             after(which)
             return carry
 
-        return lax.fori_loop(0, 2, one, carry)
+        return lax.fori_loop(0, PARTS, one, carry)
 
     def x_face(x):
         for half in (0, 1):
@@ -753,7 +759,7 @@
 
     def ready(k):
         def before(which):
-            @pl.when(which == 1)
+            @pl.when(which == PARTS - 1)
             def _():
                 receive(k, True, ())
 
@@ -763,15 +769,19 @@
         return before
 
     def ready_faces(which):
-        for n in (0, 1):
+        for n in range(PARTS):
 
             @pl.when(which == n)
-            def _():
+            def _(n=n):
                 for load in loads[n]:
                     load.wait()
 
         unpack(0, which)
-        x_face(START * (1 - which))
+        for n, x in ((0, START), (PARTS - 1, 0)):
+
+            @pl.when(which == n)
+            def _(x=x):
+                x_face(x)
 
     def done(k):
         def after(which):
@@ -781,7 +791,7 @@
                 def _():
                     pl.semaphore_wait(barrier, sum(len(others) for _, others in stages))
 
-            @pl.when(which == 1)
+            @pl.when(which == PARTS - 1)
             def _():
                 send(k, True, ())
 
@@ -852,6 +862,7 @@
     for n in range(6):
         folded = jnp.sum(sums[n], axis=0, keepdims=True)
         mine = mine + jnp.where(row == n, folded, 0.0)
+    pending = []
     for n, (number, others) in enumerate(stages):
         red[n, number] = mine
 
@@ -870,8 +881,7 @@
             copy.start()
         for step, (_, source, slot) in enumerate(others):
             copy_of(step, source, slot).wait_recv()
-        for copy in copies:
-            copy.wait_send()
+        pending.extend(copies)
         mine = red[n, 0]
         for other in range(1, len(others) + 1):
             mine = mine + red[n, other]
@@ -910,7 +920,9 @@
         stores.append(pltpu.make_async_copy(b.at[rows, :], rows_ref.at[rows, :], sem_out.at[n]))
         stores[-1].start()
     for k in range(1, 4):
-        sent(k, True, (0, 1))
+        sent(k, True, range(PARTS))
+    for copy in pending:
+        copy.wait_send()
     for store in stores:
         store.wait()
 
@@ -940,13 +952,13 @@
             pltpu.VMEM((6, CHUNK, LANES), F),
             pltpu.VMEM((4, 2, 2, span_x, LANES), F),
             pltpu.VMEM((4, 2, 2, span_x, LANES), F),
-            pltpu.VMEM((4, 2, span_y, LANES), F),
-            pltpu.VMEM((4, 2, 2, span_y, LANES), F),
-            pltpu.VMEM((2, span_y, LANES), F),
+            pltpu.VMEM((4, PARTS, span_y, LANES), F),
+            pltpu.VMEM((4, 2, PARTS, span_y, LANES), F),
+            pltpu.VMEM((PARTS, span_y, LANES), F),
             pltpu.VMEM((2, most, 8, LANES), F),
-            dma((24,)),
-            dma((4, 10)),
-            dma((4, 10)),
+            dma((8 * PARTS + 4,)),
+            dma((4, 2 + 4 * PARTS)),
+            dma((4, 2 + 4 * PARTS)),
             dma((2, most)),
             dma((2, most)),
             dma((4,)),
@@ -963,7 +975,7 @@
 ):
     sizes = tuple(lax.axis_size(axis) for axis in AXES)
     slots = atom_charge.shape[3]
-    index, value, screen, *halos = deliver(
+    index, value, live, screen, *halos = deliver(
         sizes,
         atom_charge, atom_fraction, atom_corner, block_count,
         permittivity, base_potential, ion_access,
@@ -971,10 +983,8 @@
     sources = spread(index, value, permittivity.shape)
     rows_field = krylov(sizes, sources, permittivity, screen, *halos)
     solution_field, sampled = sample(index, value, rows_field, permittivity.shape)
-    returned = give_back(sizes[2], sampled).reshape(sizes[2], -1)
-    slot = lax.broadcasted_iota(jnp.int32, returned.shape, 1)
-    live = slot < block_count.reshape(sizes[2], 1)
-    return solution_field, jnp.where(live, returned, 0.0).reshape(1, 1, 1, slots)
+    returned = give_back(sizes[2], sampled)
+    return solution_field, jnp.where(live > 0.0, returned, 0.0).reshape(1, 1, 1, slots)
 
 
 def solution(mesh):

time: 90.1 us -> 87.5 us (0.971)
  Pallas kernels: 87.5 us -> 85 us
    pallas_call x1, Pallas kernels: 42.5 us -> 40.6 us  [krylov(): pl.pallas_call(functools.partial(krylov_kernel, sizes), out_shape=jax.Sha...]
    reshape x0 -> x1, other arithmetic: none -> 1.31 us  [per_device(): jnp.where(live > 0.0, returned, 0.0).reshape(1, 1, 1, slots)]
    select_n x1 -> x0, other arithmetic: 1.31 us -> none  [per_device(): jnp.where(live, returned, 0.0).reshape(1, 1, 1, slots)]
where the time goes in v6:
time: 87.5 us; the launch traced here: 87 us
  Pallas kernels  85 us (97%)
  other arithmetic  1.31 us (1%)
    pallas_call x1, Pallas kernels, krylov(): pl.pallas_call(functools.partial(krylov_kernel, sizes), out_shape=jax.Sha...  40.6 us
    pallas_call x1, Pallas kernels, sample(): pl.pallas_call(functools.partial(sample_kernel, span_y), out_shape=(jax.S...  13.3 us
    pallas_call x1, Pallas kernels, spread(): pl.pallas_call(functools.partial(spread_kernel, span[1]), out_shape=jax.S...  13.2 us
    pallas_call x1, Pallas kernels, deliver(): pl.pallas_call(functools.partial(deliver_kernel, sizes), out_shape=(jax.S...  11.3 us
    pallas_call x1, Pallas kernels, give_back(): pl.pallas_call(functools.partial(give_back_kernel, size), out_shape=jax.S...  6.55 us

profile of v6, /device:TPU:0, one launch (start us, length us, event | category | flops | bytes accessed | tf_op | source)
XLA Modules:
  0.0 87.0 jit_solution(16661888387890511350)
XLA Ops:
  0.6 11.3 %deliver.1 = (s32[1,2048]{1,0:T(1,128)}, f32[5,1,2048]{2,1,0:T(1,128)}, f32[1,2048]{1,0:T(1,128)}, f32[64,2,64,128]{3,2,1,0:T(8,128)}, f32[2,2,64,128]{3,2,1,0:T...) custom-call(f32[1,1,1,2048]{3,2,1,0:T(1,128)} %q_ref.1, f32[3,1,1,1,2048]{4,3,2,1,0:T(1,128)} %f_ref.1, ...), custom_call_target="tpu_custom_call" | custom-call | tf_op jit(solution)/shard_map/deliver/pallas_call | solution.py:248
  12.0 13.2 %spread.1.b_ref = f32[8192,128]{1,0:T(8,128)} custom-call(s32[1,2048]{1,0:T(1,128)} %get-tuple-element.11.index_ref, f32[5,1,2048]{2,1,0:T(1,128)} %get-tuple-element.12.value_ref), custom_call_target="tpu_custom_call" | custom-call | tf_op jit(solution)/shard_map/spread/pallas_call | solution.py:392
  25.2 40.6 %krylov.1.rows_ref = f32[8192,128]{1,0:T(8,128)} custom-call(f32[8192,128]{1,0:T(8,128)} %spread.1.b_ref, f32[64,64,256]{2,1,0:T(8,128)} %eps_ref.3, f32[64,2,64,128]{3,2,1,0:T(8,128)} %get-tuple-element.13.screen_ref, f32[2,2,64,128]{3,2,1,0:T(8,128)} %get-tuple-element.14.xh_ref, f32[2,2,64,128]{3,2,1,0:T(8,128)} %get-tuple-element.15.yh_ref, ...), custom_call_target="tpu_custom_call" | custom-call | tf_op jit(solution)/shard_map/krylov/pallas_call | solution.py:938
  65.8 0.0 copy-start
  65.8 13.3 %sample.1 = (f32[64,64,256]{2,1,0:T(8,128)}, f32[1,2048]{1,0:T(1,128)}) custom-call(s32[1,2048]{1,0:T(1,128)} %get-tuple-element.11.index_ref, f32[5,1,2048]{2,1,0:T(1,128)} %get-tuple-element.12.value_ref, f32[8192,128]{1,0:T(8,128)} %krylov.1.rows_ref), custom_call_target="tpu_custom_call" | custom-call | tf_op jit(solution)/shard_map/sample/pallas_call | solution.py:480
  79.1 6.6 %give_back.1 = f32[1,2048]{1,0:T(1,128)} custom-call(f32[1,2048]{1,0:T(1,128)} %get-tuple-element.19.sampled_ref), custom_call_target="tpu_custom_call" | custom-call | tf_op jit(solution)/shard_map/give_back/pallas_call | solution.py:324
  85.7 0.0 copy-done
  85.7 1.3 %fusion = f32[1,1,1,2048]{3,2,1,0:T(1,128)} fusion(f32[1,2048]{1,0:T(1,128)} %give_back.1, f32[1,2048]{1,0:T(1,128)S(1)} %copy-done), kind=kLoop, calls=%fused_computation.1 | loop fusion | flops 4096 | bytes 24576 | tf_op jit(solution)/shard_map/reshape | solution.py:987
Async XLA Ops:
  65.8 19.9 %copy-start = (f32[1,2048]{1,0:T(1,128)S(1)}, f32[1,2048]{1,0:T(1,128)}, u32[]{:S(2)}) copy-start(f32[1,2048]{1,0:T(1,128)} %get-tuple-element.18) | copy-start | bytes 24580

commit v7 on v6

--- a/solution.py
+++ b/solution.py
@@ -14,7 +14,7 @@
 LANES = 128
 PAD = 8
 CHUNK = 16
-SLOTS_PER_STEP = 64
+SLOTS_PER_STEP = 128
 TABLES = 2
 START = 8
 PARTS = 4
@@ -61,7 +61,7 @@
         return tuple(out)
 
     empty = tuple(jnp.zeros((CHUNK, LANES), F) for _ in chunks)
-    return lax.fori_loop(0, count, columns_of, empty, unroll=8)
+    return lax.fori_loop(0, count, columns_of, empty, unroll=16)
 
 
 def deliver_kernel(

time: 87.5 us -> 86.1 us (0.984)
  Pallas kernels: 85 us -> 83.6 us
    pallas_call x1, Pallas kernels: 40.6 us -> 39.3 us  [krylov(): pl.pallas_call(functools.partial(krylov_kernel, sizes), out_shape=jax.Sha...]
where the time goes in v7:
time: 86.1 us; the launch traced here: 85.6 us
  Pallas kernels  83.6 us (97%)
  other arithmetic  1.31 us (2%)
    pallas_call x1, Pallas kernels, krylov(): pl.pallas_call(functools.partial(krylov_kernel, sizes), out_shape=jax.Sha...  39.3 us
    pallas_call x1, Pallas kernels, sample(): pl.pallas_call(functools.partial(sample_kernel, span_y), out_shape=(jax.S...  13.2 us
    pallas_call x1, Pallas kernels, spread(): pl.pallas_call(functools.partial(spread_kernel, span[1]), out_shape=jax.S...  13.1 us
    pallas_call x1, Pallas kernels, deliver(): pl.pallas_call(functools.partial(deliver_kernel, sizes), out_shape=(jax.S...  11.5 us
    pallas_call x1, Pallas kernels, give_back(): pl.pallas_call(functools.partial(give_back_kernel, size), out_shape=jax.S...  6.55 us

profile of v7, /device:TPU:0, one launch (start us, length us, event | category | flops | bytes accessed | tf_op | source)
XLA Modules:
  0.0 85.6 jit_solution(15903593180419242693)
XLA Ops:
  0.6 11.5 %deliver.1 = (s32[1,2048]{1,0:T(1,128)}, f32[5,1,2048]{2,1,0:T(1,128)}, f32[1,2048]{1,0:T(1,128)}, f32[64,2,64,128]{3,2,1,0:T(8,128)}, f32[2,2,64,128]{3,2,1,0:T...) custom-call(f32[1,1,1,2048]{3,2,1,0:T(1,128)} %q_ref.1, f32[3,1,1,1,2048]{4,3,2,1,0:T(1,128)} %f_ref.1, ...), custom_call_target="tpu_custom_call" | custom-call | tf_op jit(solution)/shard_map/deliver/pallas_call | solution.py:248
  12.1 13.1 %spread.1.b_ref = f32[8192,128]{1,0:T(8,128)} custom-call(s32[1,2048]{1,0:T(1,128)} %get-tuple-element.11.index_ref, f32[5,1,2048]{2,1,0:T(1,128)} %get-tuple-element.12.value_ref), custom_call_target="tpu_custom_call" | custom-call | tf_op jit(solution)/shard_map/spread/pallas_call | solution.py:392
  25.2 39.3 %krylov.1.rows_ref = f32[8192,128]{1,0:T(8,128)} custom-call(f32[8192,128]{1,0:T(8,128)} %spread.1.b_ref, f32[64,64,256]{2,1,0:T(8,128)} %eps_ref.3, f32[64,2,64,128]{3,2,1,0:T(8,128)} %get-tuple-element.13.screen_ref, f32[2,2,64,128]{3,2,1,0:T(8,128)} %get-tuple-element.14.xh_ref, f32[2,2,64,128]{3,2,1,0:T(8,128)} %get-tuple-element.15.yh_ref, ...), custom_call_target="tpu_custom_call" | custom-call | tf_op jit(solution)/shard_map/krylov/pallas_call | solution.py:938
  64.5 0.0 copy-start
  64.5 13.2 %sample.1 = (f32[64,64,256]{2,1,0:T(8,128)}, f32[1,2048]{1,0:T(1,128)}) custom-call(s32[1,2048]{1,0:T(1,128)} %get-tuple-element.11.index_ref, f32[5,1,2048]{2,1,0:T(1,128)} %get-tuple-element.12.value_ref, f32[8192,128]{1,0:T(8,128)} %krylov.1.rows_ref), custom_call_target="tpu_custom_call" | custom-call | tf_op jit(solution)/shard_map/sample/pallas_call | solution.py:480
  77.7 6.6 %give_back.1 = f32[1,2048]{1,0:T(1,128)} custom-call(f32[1,2048]{1,0:T(1,128)} %get-tuple-element.19.sampled_ref), custom_call_target="tpu_custom_call" | custom-call | tf_op jit(solution)/shard_map/give_back/pallas_call | solution.py:324
  84.3 0.0 copy-done
  84.3 1.3 %fusion = f32[1,1,1,2048]{3,2,1,0:T(1,128)} fusion(f32[1,2048]{1,0:T(1,128)} %give_back.1, f32[1,2048]{1,0:T(1,128)S(1)} %copy-done), kind=kLoop, calls=%fused_computation.1 | loop fusion | flops 4096 | bytes 24576 | tf_op jit(solution)/shard_map/reshape | solution.py:987
Async XLA Ops:
  64.5 19.7 %copy-start = (f32[1,2048]{1,0:T(1,128)S(1)}, f32[1,2048]{1,0:T(1,128)}, u32[]{:S(2)}) copy-start(f32[1,2048]{1,0:T(1,128)} %get-tuple-element.18) | copy-start | bytes 24580

commit v8 on v7

--- a/solution.py
+++ b/solution.py
@@ -507,7 +507,15 @@
         number = number * sizes[axis] + places[axis]
         count *= sizes[axis]
     others = []
-    for step in range(1, count):
+
+    def hops(step):
+        total = 0
+        for axis in reversed(axes):
+            move, step = step % sizes[axis], step // sizes[axis]
+            total += min(move, sizes[axis] - move)
+        return total
+
+    for step in sorted(range(1, count), key=hops, reverse=True):
         target, source, source_number, rest = {}, {}, 0, step
         moves = {}
         for axis in reversed(axes):

time: 86.1 us -> 85.8 us (level)
  no operation moved by 1% of the time
where the time goes in v8:
time: 85.8 us; the launch traced here: 85.3 us
  Pallas kernels  83.3 us (97%)
  other arithmetic  1.31 us (2%)
    pallas_call x1, Pallas kernels, krylov(): pl.pallas_call(functools.partial(krylov_kernel, sizes), out_shape=jax.Sha...  39.1 us
    pallas_call x1, Pallas kernels, sample(): pl.pallas_call(functools.partial(sample_kernel, span_y), out_shape=(jax.S...  13.2 us
    pallas_call x1, Pallas kernels, spread(): pl.pallas_call(functools.partial(spread_kernel, span[1]), out_shape=jax.S...  13.1 us
    pallas_call x1, Pallas kernels, deliver(): pl.pallas_call(functools.partial(deliver_kernel, sizes), out_shape=(jax.S...  11.5 us
    pallas_call x1, Pallas kernels, give_back(): pl.pallas_call(functools.partial(give_back_kernel, size), out_shape=jax.S...  6.55 us

profile of v8, /device:TPU:0, one launch (start us, length us, event | category | flops | bytes accessed | tf_op | source)
XLA Modules:
  0.0 85.3 jit_solution(758555563445314266)
XLA Ops:
  0.6 11.5 %deliver.1 = (s32[1,2048]{1,0:T(1,128)}, f32[5,1,2048]{2,1,0:T(1,128)}, f32[1,2048]{1,0:T(1,128)}, f32[64,2,64,128]{3,2,1,0:T(8,128)}, f32[2,2,64,128]{3,2,1,0:T...) custom-call(f32[1,1,1,2048]{3,2,1,0:T(1,128)} %q_ref.1, f32[3,1,1,1,2048]{4,3,2,1,0:T(1,128)} %f_ref.1, ...), custom_call_target="tpu_custom_call" | custom-call | tf_op jit(solution)/shard_map/deliver/pallas_call | solution.py:248
  12.1 13.1 %spread.1.b_ref = f32[8192,128]{1,0:T(8,128)} custom-call(s32[1,2048]{1,0:T(1,128)} %get-tuple-element.11.index_ref, f32[5,1,2048]{2,1,0:T(1,128)} %get-tuple-element.12.value_ref), custom_call_target="tpu_custom_call" | custom-call | tf_op jit(solution)/shard_map/spread/pallas_call | solution.py:392
  25.2 39.1 %krylov.1.rows_ref = f32[8192,128]{1,0:T(8,128)} custom-call(f32[8192,128]{1,0:T(8,128)} %spread.1.b_ref, f32[64,64,256]{2,1,0:T(8,128)} %eps_ref.3, f32[64,2,64,128]{3,2,1,0:T(8,128)} %get-tuple-element.13.screen_ref, f32[2,2,64,128]{3,2,1,0:T(8,128)} %get-tuple-element.14.xh_ref, f32[2,2,64,128]{3,2,1,0:T(8,128)} %get-tuple-element.15.yh_ref, ...), custom_call_target="tpu_custom_call" | custom-call | tf_op jit(solution)/shard_map/krylov/pallas_call | solution.py:946
  64.2 0.0 copy-start
  64.2 13.2 %sample.1 = (f32[64,64,256]{2,1,0:T(8,128)}, f32[1,2048]{1,0:T(1,128)}) custom-call(s32[1,2048]{1,0:T(1,128)} %get-tuple-element.11.index_ref, f32[5,1,2048]{2,1,0:T(1,128)} %get-tuple-element.12.value_ref, f32[8192,128]{1,0:T(8,128)} %krylov.1.rows_ref), custom_call_target="tpu_custom_call" | custom-call | tf_op jit(solution)/shard_map/sample/pallas_call | solution.py:480
  77.4 6.6 %give_back.1 = f32[1,2048]{1,0:T(1,128)} custom-call(f32[1,2048]{1,0:T(1,128)} %get-tuple-element.19.sampled_ref), custom_call_target="tpu_custom_call" | custom-call | tf_op jit(solution)/shard_map/give_back/pallas_call | solution.py:324
  84.0 0.0 copy-done
  84.0 1.3 %fusion = f32[1,1,1,2048]{3,2,1,0:T(1,128)} fusion(f32[1,2048]{1,0:T(1,128)} %give_back.1, f32[1,2048]{1,0:T(1,128)S(1)} %copy-done), kind=kLoop, calls=%fused_computation.1 | loop fusion | flops 4096 | bytes 24576 | tf_op jit(solution)/shard_map/reshape | solution.py:995
Async XLA Ops:
  64.2 19.7 %copy-start = (f32[1,2048]{1,0:T(1,128)S(1)}, f32[1,2048]{1,0:T(1,128)}, u32[]{:S(2)}) copy-start(f32[1,2048]{1,0:T(1,128)} %get-tuple-element.18) | copy-start | bytes 24580
